TPU v7x, 512 devices: a whole 4x4x16 slice. The times are simulated.
512 devices in a mesh: view: 4 (over x), dev: 128 (over z, y, core).
Axes of the slice: x: 4, y: 4, z: 16, core: 2. Of those that a mesh axis runs over, the one named last changes fastest.
Arguments:
- attributes: float32 [59, 65536], P(None, 'dev'), may hold values from -6 to 8, as said below
- camera: float32 [4, 6], P('view'), may hold values from -0.2 to 0.2
- list_owner: int32 [4, 512, 256, 1], P('view', 'dev'), may hold values from 0 to 127; in each aligned block of 1024 rows (0 to 1023, 1024 to 2047, ..., all dimensions but the last counted through in order) at most 16 rows name the same one
- list_local: int32 [4, 512, 256], P('view', 'dev'), may hold values from 0 to 511
- term_depth: int32 [4, 512, 256], P('view', 'dev'), may hold values from 1 to 256
- image_cot: float32 [4, 3, 512, 256], P('view', None, 'dev'), may hold values from -6 to 6
Outputs:
- image: float32 [4, 3, 512, 256], P('view', None, 'dev')
- attr_grad: float32 [59, 65536], P(None, 'dev')
Inputs may be any that keep to these rules, and one draw needn't show every extreme that they name: `attributes`: the quaternion's real part lies in 0.5 to 1.5, the third position coordinate in 4 to 8. `list_owner`: among the slots of one device's tiles of one view no owner is named more than 16 times.
All inputs are finite; a program needn't handle non-finite values.
Results may differ from a plain program's by a relative error of at most 0.0003.
Values sent between devices are 32-bit elements; how exact they have to be, the bound alone decides.
No kernel may reach another device: no remote copies, remote signals or barrier semaphores. Data moves between devices by JAX's collectives and lax.ppermute only.
A program may use at most 64 MiB of HBM per device.

v0:
```python
import jax
import jax.numpy as jnp
from jax import lax
from jax.sharding import PartitionSpec as P

TILE_COLS = 16


SH_C0 = 0.28209479177387814
SH_C1 = 0.4886025119029199
SH_C2 = (
    1.0925484305920792,
    -1.0925484305920792,
    0.31539156525252005,
    -1.0925484305920792,
    0.5462742152960396,
)
SH_C3 = (
    -0.5900435899266435,
    2.890611442640554,
    -0.4570457994644658,
    0.3731763325901154,
    -0.4570457994644658,
    1.445305721320277,
    -0.5900435899266435,
)
BLUR = 1e-05


def rotation(angles):
    one = jnp.ones((), jnp.float32)
    zero = jnp.zeros((), jnp.float32)
    cosx, sinx = (jnp.cos(angles[0]), jnp.sin(angles[0]))
    cosy, siny = (jnp.cos(angles[1]), jnp.sin(angles[1]))
    cosz, sinz = (jnp.cos(angles[2]), jnp.sin(angles[2]))
    rot_x = jnp.stack(
        [
            jnp.stack([one, zero, zero]),
            jnp.stack([zero, cosx, -sinx]),
            jnp.stack([zero, sinx, cosx]),
        ]
    )
    rot_y = jnp.stack(
        [
            jnp.stack([cosy, zero, siny]),
            jnp.stack([zero, one, zero]),
            jnp.stack([-siny, zero, cosy]),
        ]
    )
    rot_z = jnp.stack(
        [
            jnp.stack([cosz, -sinz, zero]),
            jnp.stack([sinz, cosz, zero]),
            jnp.stack([zero, zero, one]),
        ]
    )
    high = lax.Precision.HIGHEST
    return jnp.dot(rot_z, jnp.dot(rot_y, rot_x, precision=high), precision=high)


def harmonics(dirx, diry, dirz):
    xx, yy, zz = (dirx * dirx, diry * diry, dirz * dirz)
    return [
        SH_C0 + 0.0 * dirx,
        -SH_C1 * diry,
        SH_C1 * dirz,
        -SH_C1 * dirx,
        SH_C2[0] * dirx * diry,
        SH_C2[1] * diry * dirz,
        SH_C2[2] * (2.0 * zz - xx - yy),
        SH_C2[3] * dirx * dirz,
        SH_C2[4] * (xx - yy),
        SH_C3[0] * diry * (3.0 * xx - yy),
        SH_C3[1] * dirx * diry * dirz,
        SH_C3[2] * diry * (4.0 * zz - xx - yy),
        SH_C3[3] * dirz * (2.0 * zz - 3.0 * xx - 3.0 * yy),
        SH_C3[4] * dirx * (4.0 * zz - xx - yy),
        SH_C3[5] * dirz * (xx - yy),
        SH_C3[6] * dirx * (xx - 3.0 * yy),
    ]


def project(attrs, cam):
    rot = rotation(cam[0:3])
    shift = cam[3:6]
    pos = attrs[0:3]
    campos = jnp.dot(rot, pos, precision=lax.Precision.HIGHEST) + shift[:, None]
    posx, posy, posz = (campos[0], campos[1], campos[2])
    inverse = 1.0 / posz
    jac = [
        [inverse, 0.0 * inverse, -posx * inverse * inverse],
        [0.0 * inverse, inverse, -posy * inverse * inverse],
    ]
    tmat = [[sum((jac[r][i] * rot[i, j] for i in range(3))) for j in range(3)] for r in range(2)]
    scale = jnp.exp(attrs[3:6])
    quat = attrs[6:10]
    quat = quat * lax.rsqrt(jnp.sum(quat * quat, axis=0))
    qw, qa, qb, qc = (quat[0], quat[1], quat[2], quat[3])
    rgau = [
        [1 - 2 * (qb * qb + qc * qc), 2 * (qa * qb - qw * qc), 2 * (qa * qc + qw * qb)],
        [2 * (qa * qb + qw * qc), 1 - 2 * (qa * qa + qc * qc), 2 * (qb * qc - qw * qa)],
        [2 * (qa * qc - qw * qb), 2 * (qb * qc + qw * qa), 1 - 2 * (qa * qa + qb * qb)],
    ]
    mscaled = [[rgau[i][k] * scale[k] for k in range(3)] for i in range(3)]
    cov = [
        [sum((mscaled[i][k] * mscaled[j][k] for k in range(3))) for j in range(3)] for i in range(3)
    ]
    sig = [
        [
            sum((tmat[r][i] * cov[i][j] * tmat[s][j] for i in range(3) for j in range(3)))
            for s in range(2)
        ]
        for r in range(2)
    ]
    sig_a = sig[0][0] + BLUR
    sig_b = sig[0][1]
    sig_c = sig[1][1] + BLUR
    det = sig_a * sig_c - sig_b * sig_b
    centre = [
        -(rot[0, j] * shift[0] + rot[1, j] * shift[1] + rot[2, j] * shift[2]) for j in range(3)
    ]
    dirs = [pos[j] - centre[j] for j in range(3)]
    norm_inv = lax.rsqrt(dirs[0] * dirs[0] + dirs[1] * dirs[1] + dirs[2] * dirs[2])
    basis = harmonics(dirs[0] * norm_inv, dirs[1] * norm_inv, dirs[2] * norm_inv)
    colors = [0.5 + sum((basis[k] * attrs[11 + 3 * k + ch] for k in range(16))) for ch in range(3)]
    opacity = jax.nn.sigmoid(attrs[10])
    return jnp.stack(
        [posx * inverse, posy * inverse, sig_c / det, -sig_b / det, sig_a / det, opacity] + colors
    )


def pixel_coords(tile, ntiles):
    pixel = jnp.arange(256, dtype=jnp.int32)
    col = tile % TILE_COLS
    row = tile // TILE_COLS
    xs = ((col * 16 + pixel % 16).astype(jnp.float32) + 0.5) / (16.0 * TILE_COLS) - 0.5
    ys = ((row * 16 + pixel // 16).astype(jnp.float32) + 0.5) / (16.0 * (ntiles // TILE_COLS)) - 0.5
    return (xs, ys)


def tile_color(rows, xs, ys, depth):
    slot_entries = rows.shape[1]
    delta_x = xs[:, None] - rows[0][None, :]
    delta_y = ys[:, None] - rows[1][None, :]
    power = (
        0.5 * (rows[2][None, :] * delta_x * delta_x + rows[4][None, :] * delta_y * delta_y)
        + rows[3][None, :] * delta_x * delta_y
    )
    live = (jnp.arange(slot_entries, dtype=jnp.int32)[None, :] < depth[:, None]).astype(jnp.float32)
    alpha = rows[5][None, :] * jnp.exp(-power) * live
    keep = jnp.cumprod(1.0 - alpha, axis=1)
    trans = jnp.concatenate([jnp.ones((xs.shape[0], 1), jnp.float32), keep[:, :-1]], axis=1)
    weight = trans * alpha
    return jnp.einsum("ps,cs->cp", weight, rows[6:9], precision=lax.Precision.HIGHEST)


def composite(rows_slot, first_tile, ntiles, depth, cotangent):
    tile_entries = depth.shape[0]
    rows_tiles = jnp.transpose(rows_slot.reshape(rows_slot.shape[0], tile_entries, -1), (1, 0, 2))

    def tile_work(packed):
        rows, tile, pixel_depth, pixel_cot = packed
        xs, ys = pixel_coords(tile, ntiles)
        color, pull = jax.vjp(lambda r: tile_color(r, xs, ys, pixel_depth), rows)
        return (color, pull(pixel_cot)[0])

    tile_ids = first_tile + jnp.arange(tile_entries, dtype=jnp.int32)
    color, grads = lax.map(tile_work, (rows_tiles, tile_ids, depth, cotangent))
    return (color, jnp.transpose(grads, (1, 0, 2)).reshape(rows_slot.shape[0], -1))


def per_device(attributes, camera, list_owner, list_local, term_depth, image_cot):
    device_total = lax.axis_size("dev")
    g_dev = attributes.shape[1]
    tile_entries = list_local.shape[1]
    slot_entries = list_local.shape[2]
    slot_total = tile_entries * slot_entries
    slot_capacity = 2 * slot_total // device_total
    ntiles = tile_entries * device_total
    owner = list_owner[0, :, :, 0].reshape(-1)
    local_ids = list_local[0].reshape(-1)
    onehot = (owner[:, None] == jnp.arange(device_total, dtype=jnp.int32)[None, :]).astype(
        jnp.int32
    )
    counts = jnp.sum(onehot, axis=0)
    starts = jnp.cumsum(counts) - counts
    initial_slot = jnp.sum(onehot * starts[None, :], axis=1)
    sorted_order = jnp.argsort(owner, stable=True)
    rank = (
        jnp.zeros((slot_total,), jnp.int32)
        .at[sorted_order]
        .set(jnp.arange(slot_total, dtype=jnp.int32) - initial_slot[sorted_order])
    )
    position = owner * slot_capacity + rank
    request = jnp.zeros((device_total * slot_capacity,), jnp.int32).at[position].set(local_ids)
    asked = lax.all_to_all(
        request.reshape(device_total, slot_capacity), "dev", split_axis=0, concat_axis=0, tiled=True
    ).reshape(-1)
    cam = camera[0]
    first_tile = lax.axis_index("dev") * tile_entries
    depth = term_depth[0]
    cotangent = jnp.transpose(image_cot[0], (1, 0, 2))
    total = None
    rows_owner, pull_owner = jax.vjp(lambda a: project(a, cam), attributes)
    sent = rows_owner[:, asked]
    arrived = lax.all_to_all(
        sent.reshape(9, device_total, slot_capacity), "dev", split_axis=1, concat_axis=1, tiled=True
    ).reshape(9, -1)
    rows_slot = arrived[:, position]
    color, grad_slot = composite(rows_slot, first_tile, ntiles, depth, cotangent)
    grad_buffer = (
        jnp.zeros((9, device_total * slot_capacity), jnp.float32).at[:, position].set(grad_slot)
    )
    returned = lax.all_to_all(
        grad_buffer.reshape(9, device_total, slot_capacity),
        "dev",
        split_axis=1,
        concat_axis=1,
        tiled=True,
    ).reshape(9, -1)
    grad_rows = jnp.zeros((9, g_dev), jnp.float32).at[:, asked].add(returned)
    attr_grad = pull_owner(grad_rows)[0]
    total = lax.psum(attr_grad, "view")
    image = jnp.transpose(color, (1, 0, 2))[None]
    return (image, total)


def solution(mesh):
    in_specs = (
        P(None, "dev"),
        P("view", None),
        P("view", "dev", None, None),
        P("view", "dev", None),
        P("view", "dev", None),
        P("view", None, "dev", None),
    )
    out_specs = (P("view", None, "dev", None), P(None, "dev"))
    return jax.shard_map(
        per_device, mesh=mesh, in_specs=in_specs, out_specs=out_specs, check_vma=False
    )
```

profile of v0, /device:TPU:1, one launch (start us, length us, event | category | flops | bytes accessed | tf_op | source)
XLA Modules:
  0.0 315.2 jit_solution(12072224999658758813)
XLA Ops:
  7.2 0.9 convert_reduce_fusion
  8.8 4.4 %sort.17 = (s32[1024]{0:T(1024)}, s32[1024]{0:T(1024)S(1)}) sort(s32[1024]{0:T(1024)S(1)} %bitcast.195, s32[1024]{0:T(1024)S(1)} %iota.41), dimensions={0}, to_apply=%region_1.0 | sort | flops 10240 | bytes 16384 | tf_op jit(solution)/shard_map/jit(argsort)/sort | solution.py:188
  13.9 4.5 %gather_fusion = s32[1024]{0:T(1024)S(1)} fusion(s32[1024]{0:T(1024)S(1)} %select_reduce_fusion, s32[1024]{0:T(1024)S(1)} %get-tuple-element.358), kind=kCustom, calls=%fused_computation | custom fusion | bytes 12288 | tf_op jit(solution)/shard_map/gather | solution.py:192
  18.5 4.3 %scatter_custom_fusion = s32[1024]{0:T(1024)S(1)} fusion(s32[1024]{0:T(1024)S(1)} %get-tuple-element.359, s32[1024]{0:T(1024)S(1)} %iota_subtract_fusion, s32[]{:T(128)} %constant.192.clone.1), kind=kCustom, calls=%fused_computation.292 | custom fusion | bytes 4100 | tf_op jit(solution)/shard_map/scatter | solution.py:192
  22.8 4.3 %scatter_custom_fusion.1 = s32[2048]{0:T(1024)S(1)} fusion(s32[1024]{0:T(1024)S(1)} %get-tuple-element.215, s32[1024]{0:T(1024)S(1)} %bitcast.202, s32[]{:T(128)} %constant.192.clone.1), kind=kCustom, calls=%fused_computation.165 | custom fusion | bytes 8196 | tf_op jit(solution)/shard_map/scatter | solution.py:195
  27.2 0.7 all_to_all.12
  27.9 20.6 %all-to-all-start = ((s32[128,1,16]{2,1,0:T(1,128)}), s32[128,1,16]{2,1,0:T(1,128)S(1)}, u32[]{:S(2)}, u32[]{:S(2)}) async-start(s32[128,1,16]{2,1,0:T(1,128)} %bitcast.48), calls=%async_computation | async-start | bytes 131072 | tf_op jit(solution)/shard_map/all_to_all | solution.py:196
  55.9 0.7 fusion.152
  75.6 2.1 fusion.143
  78.5 0.8 reduce.4
  79.4 5.5 %gather_fusion.1 = f32[2048,9]{1,0:T(8,128)S(1)} fusion(f32[9,512]{0,1:T(8,128)S(1)} %copy.57, s32[2048]{0:T(1024)S(1)} %broadcast_clamp_fusion), kind=kCustom, calls=%fused_computation.1 | custom fusion | bytes 155648 | tf_op jit(solution)/shard_map/gather | solution.py:205
  84.9 1.4 reshape.321
  86.3 16.2 %all-to-all-start.1 = ((f32[128,1,144]{2,1,0:T(1,128)}), f32[128,1,144]{2,1,0:T(1,128)S(1)}, u32[]{:S(2)}, u32[]{:S(2)}) async-start(f32[128,1,144]{2,1,0:T(1,128)} %reshape.321), calls=%async_computation.1 | async-start | bytes 262144 | tf_op jit(solution)/shard_map/all_to_all | solution.py:206
  102.9 15.8 %all-to-all-done.1 = f32[128,1,144]{2,1,0:T(1,128)S(1)} async-done(((f32[128,1,144]{2,1,0:T(1,128)}), f32[128,1,144]{2,1,0:T(1,128)S(1)}, u32[]{:S(2)}, u32[]{:S(2)}) %all-to-all-start.1) | async-done | bytes 73760 | tf_op jit(solution)/shard_map/all_to_all | solution.py:206
  119.2 0.9 reduce.5
  120.8 2.8 gather_fusion.2
  124.4 82.5 %while.15 = (s32[]{:T(128)}, f32[4,3,256]{2,0,1:T(4,128)S(1)}, f32[4,9,256]{2,1,0:T(8,128)S(1)}, f32[4,9,256]{2,1,0:T(8,128)S(1)}, s32[4,256]{1,0:T(4,128)}, /*i...) while((s32[]{:T(128)}, f32[4,3,256]{2,0,1:T(4,128)S(1)}, ...), condition=%wide.region_14.15_spmd, body=%wide.region_7.14_spmd.sunk | while | flops 15078685 | bytes 22935272 | solution.py:168
  127.6 0.7 constant_dynamic-slice_fusion.10
  134.4 0.7 slice-done.9
  148.3 0.7 constant_dynamic-slice_fusion.10
  168.9 0.7 constant_dynamic-slice_fusion.10
  189.5 0.7 constant_dynamic-slice_fusion.10
  207.8 3.3 %scatter_custom_fusion.2 = f32[9,2048]{0,1:T(8,128)S(1)} fusion(s32[1024]{0:T(1024)S(1)} %get-tuple-element.215, f32[1024,9]{1,0:T(8,128)S(1)} %copy.62, f32[]{:T(128)} %constant.193.clone.1), kind=kCustom, calls=%fused_computation.138 | custom fusion | bytes 73732 | tf_op jit(solution)/shard_map/scatter | solution.py:212
  211.1 0.8 reshape.323
  211.9 23.4 %all_to_all.19 = f32[128,1,144]{2,1,0:T(1,128)S(1)} all-to-all(f32[128,1,144]{2,1,0:T(1,128)S(1)} %reshape.323), channel_id=1, replica_groups=mesh['view'=4,'dev'=128] {'dev'}, dimensions={0} | all-to-all | bytes 147456 | tf_op jit(solution)/shard_map/all_to_all | solution.py:214
  235.3 0.9 reduce.6
  236.8 12.1 %scatter_custom_fusion.3 = f32[9,512]{0,1:T(8,128)S(1)} fusion(s32[2048]{0:T(1024)S(1)} %bitcast.199, f32[2048,9]{1,0:T(8,128)S(1)} %bitcast.148, f32[]{:T(128)} %constant.193.clone.1), kind=kCustom, calls=%fused_computation.144 | custom fusion | flops 18432 | bytes 18436 | tf_op jit(solution)/shard_map/scatter-add | solution.py:221
  251.5 5.8 %fusion.98 = (f32[1,512]{1,0:T(1,128)S(1)}, f32[1,512]{1,0:T(1,128)S(1)}, f32[1,512]{1,0:T(1,128)S(1)}, f32[1,512]{1,0:T(1,128)S(1)}, f32[1,512]{1,0:T(1,128)S(1...) fusion(f32[1,512]{1,0:T(1,128)S(1)} %copy.82, f32[1,512]{1,0:T(1,128)S(1)} %copy.81, ...), kind=kLoop, calls=%fused_computation.325 | loop fusion | flops 81920 | bytes 100388 | tf_op jit(solution)/shard_map/transpose(jvp())/neg | solution.py:89
  257.3 2.0 negate_add_fusion.1
  259.6 0.9 pad_add_fusion.9
  260.6 46.2 %all-reduce.135.cloned.1.call-done = f32[59,512]{1,0:T(8,128)} async-done(((f32[59,512]{1,0:T(8,128)}), f32[59,512]{1,0:T(8,128)}) %all-reduce.135.cloned.1.call-update) | async-done | bytes 120848 | tf_op jit(solution)/shard_map/psum | solution.py:223
  306.7 1.6 copy.180
  (873 shorter events, 77.2 us)
Async XLA Ops:
  7.2 0.9 copy-start.16
  8.1 0.7 copy-start.12
  18.5 30.0 %copy-start.11 = (f32[59,512]{1,0:T(8,128)S(1)}, f32[59,512]{1,0:T(8,128)}, u32[]{:S(2)}) copy-start(f32[59,512]{1,0:T(8,128)} %param.8) | copy-start | bytes 362500
  27.9 50.1 %all-to-all-start = ((s32[128,1,16]{2,1,0:T(1,128)}), s32[128,1,16]{2,1,0:T(1,128)S(1)}, u32[]{:S(2)}, u32[]{:S(2)}) async-start(s32[128,1,16]{2,1,0:T(1,128)} %bitcast.48), calls=%async_computation | async-start | bytes 131072 | tf_op jit(solution)/shard_map/all_to_all | solution.py:196
  86.3 16.5 %copy-start.15 = (f32[1,3,4,256]{3,2,1,0:T(4,128)S(1)}, f32[1,3,4,256]{3,2,1,0:T(4,128)}, u32[]{:S(2)}) copy-start(f32[1,3,4,256]{3,2,1,0:T(4,128)} %param.13) | copy-start | bytes 36868
  86.3 32.3 %all-to-all-start.1 = ((f32[128,1,144]{2,1,0:T(1,128)}), f32[128,1,144]{2,1,0:T(1,128)S(1)}, u32[]{:S(2)}, u32[]{:S(2)}) async-start(f32[128,1,144]{2,1,0:T(1,128)} %reshape.321), calls=%async_computation.1 | async-start | bytes 262144 | tf_op jit(solution)/shard_map/all_to_all | solution.py:206
  102.6 204.2 %all-reduce.135.cloned.1.call-start = ((), (), s32[]{:S(2)}) async-start(), calls=%async_computation.3 | async-start | bytes 262144 | tf_op jit(solution)/shard_map/psum | solution.py:223
  129.3 11.2 %copy-start = (f32[256,128]{0,1:T(8,128)}, f32[256,128]{0,1:T(8,128)S(1)}, u32[]{:S(2)}) copy-start(f32[256,128]{0,1:T(8,128)S(1)} %slice.1658) | copy-start | bytes 393220 | tf_op jit(solution)/shard_map/while
  133.4 5.5 %copy-start.2 = (f32[256,64]{0,1:T(8,128)}, f32[256,64]{0,1:T(8,128)S(1)}, u32[]{:S(2)}) copy-start(f32[256,64]{0,1:T(8,128)S(1)} %slice.1665) | copy-start | bytes 196612 | tf_op jit(solution)/shard_map/while
  133.5 4.0 %copy-start.4 = (f32[256,32]{0,1:T(8,128)}, f32[256,32]{0,1:T(8,128)S(1)}, u32[]{:S(2)}) copy-start(f32[256,32]{0,1:T(8,128)S(1)} %slice.1666) | copy-start | bytes 98308 | tf_op jit(solution)/shard_map/while
  133.6 2.4 copy-start.6
  133.7 1.6 copy-start.8
  134.4 0.7 slice-start.9
  139.0 0.7 slice-start.1
  149.9 11.2 %copy-start = (f32[256,128]{0,1:T(8,128)}, f32[256,128]{0,1:T(8,128)S(1)}, u32[]{:S(2)}) copy-start(f32[256,128]{0,1:T(8,128)S(1)} %slice.1658) | copy-start | bytes 393220 | tf_op jit(solution)/shard_map/while
  154.0 5.5 %copy-start.2 = (f32[256,64]{0,1:T(8,128)}, f32[256,64]{0,1:T(8,128)S(1)}, u32[]{:S(2)}) copy-start(f32[256,64]{0,1:T(8,128)S(1)} %slice.1665) | copy-start | bytes 196612 | tf_op jit(solution)/shard_map/while
  154.1 4.0 %copy-start.4 = (f32[256,32]{0,1:T(8,128)}, f32[256,32]{0,1:T(8,128)S(1)}, u32[]{:S(2)}) copy-start(f32[256,32]{0,1:T(8,128)S(1)} %slice.1666) | copy-start | bytes 98308 | tf_op jit(solution)/shard_map/while
  154.2 2.4 copy-start.6
  154.3 1.6 copy-start.8
  155.0 0.7 slice-start.9
  159.6 0.7 slice-start.1
  170.5 11.2 %copy-start = (f32[256,128]{0,1:T(8,128)}, f32[256,128]{0,1:T(8,128)S(1)}, u32[]{:S(2)}) copy-start(f32[256,128]{0,1:T(8,128)S(1)} %slice.1658) | copy-start | bytes 393220 | tf_op jit(solution)/shard_map/while
  174.7 5.5 %copy-start.2 = (f32[256,64]{0,1:T(8,128)}, f32[256,64]{0,1:T(8,128)S(1)}, u32[]{:S(2)}) copy-start(f32[256,64]{0,1:T(8,128)S(1)} %slice.1665) | copy-start | bytes 196612 | tf_op jit(solution)/shard_map/while
  174.8 4.0 %copy-start.4 = (f32[256,32]{0,1:T(8,128)}, f32[256,32]{0,1:T(8,128)S(1)}, u32[]{:S(2)}) copy-start(f32[256,32]{0,1:T(8,128)S(1)} %slice.1666) | copy-start | bytes 98308 | tf_op jit(solution)/shard_map/while
  174.9 2.4 copy-start.6
  174.9 1.6 copy-start.8
  175.6 0.7 slice-start.9
  191.1 11.2 %copy-start = (f32[256,128]{0,1:T(8,128)}, f32[256,128]{0,1:T(8,128)S(1)}, u32[]{:S(2)}) copy-start(f32[256,128]{0,1:T(8,128)S(1)} %slice.1658) | copy-start | bytes 393220 | tf_op jit(solution)/shard_map/while
  195.3 5.5 %copy-start.2 = (f32[256,64]{0,1:T(8,128)}, f32[256,64]{0,1:T(8,128)S(1)}, u32[]{:S(2)}) copy-start(f32[256,64]{0,1:T(8,128)S(1)} %slice.1665) | copy-start | bytes 196612 | tf_op jit(solution)/shard_map/while
  195.4 4.0 %copy-start.4 = (f32[256,32]{0,1:T(8,128)}, f32[256,32]{0,1:T(8,128)S(1)}, u32[]{:S(2)}) copy-start(f32[256,32]{0,1:T(8,128)S(1)} %slice.1666) | copy-start | bytes 98308 | tf_op jit(solution)/shard_map/while
  195.5 2.4 copy-start.6
  195.6 1.6 copy-start.8
  (69 other events, 44.8 us)
Sparse Core Ops, SparseCore 0:
  260.7 45.9 all-reduce.134
where the time goes:
time: 318 us; the launch traced here: 315 us
  local copies, waits for them, and re-layouts  94.4 us (30%)
  waiting for transfers between devices  62 us (19%)
  other arithmetic  40.8 us (13%)
  between operations  37.4 us (12%)
  starting transfers between devices  37 us (12%)
  blocking collectives  23.4 us (7%)
  loops' own time  14 us (4%)
  matrix products  6.13 us (2%)
    psum x1, waiting for transfers between devices, per_device(): total = lax.psum(attr_grad, 'view')  46.2 us
    all_to_all x1, blocking collectives, per_device(): lax.all_to_all(grad_buffer.reshape(9, device_total, slot_capacity), 'dev'...  23.4 us
    all_to_all x1, starting transfers between devices, per_device(): lax.all_to_all(request.reshape(device_total, slot_capacity), 'dev', split...  20.6 us
    slice x180, local copies, waits for them, and re-layouts, tile_color(): keep = jnp.cumprod(1.0 - alpha, axis=1)  18.3 us
    all_to_all x1, starting transfers between devices, per_device(): lax.all_to_all(sent.reshape(9, device_total, slot_capacity), 'dev', split...  16.2 us
    all_to_all x1, waiting for transfers between devices, per_device(): lax.all_to_all(sent.reshape(9, device_total, slot_capacity), 'dev', split...  15.8 us
    split x48, local copies, waits for them, and re-layouts, tile_color(): keep = jnp.cumprod(1.0 - alpha, axis=1)  15.2 us
    another operation x1, loops' own time, composite(): color, grads = lax.map(tile_work, (rows_tiles, tile_ids, depth, cotangent))  14 us
  transfers between devices with their start and end apart: 3, of which 2 were waited for; matrix products, arithmetic and copies ran while one was open for 1% of the time, Pallas kernels for 0%

commit v1 on v0

v1 whole, which is shorter than its diff:
```python
import jax
import jax.numpy as jnp
from jax import lax
from jax.experimental import pallas as pl
from jax.experimental.pallas import tpu as pltpu
from jax.sharding import PartitionSpec as P

TILE_COLS = 16
TILES = 4
SLOTS = 256
CAP = 16
OWNERS = 128
G_DEV = 512
ATTR = 59
VIEWS = 4
LOG2E = 1.4426950408889634

SH_C0 = 0.28209479177387814
SH_C1 = 0.4886025119029199
SH_C2 = (
    1.0925484305920792,
    -1.0925484305920792,
    0.31539156525252005,
    -1.0925484305920792,
    0.5462742152960396,
)
SH_C3 = (
    -0.5900435899266435,
    2.890611442640554,
    -0.4570457994644658,
    0.3731763325901154,
    -0.4570457994644658,
    1.445305721320277,
    -0.5900435899266435,
)
BLUR = 1e-05

F32 = jnp.float32
BF16 = jnp.bfloat16
I32 = jnp.int32


def camera_terms(angles, shift):
    cosx, sinx = jnp.cos(angles[0]), jnp.sin(angles[0])
    cosy, siny = jnp.cos(angles[1]), jnp.sin(angles[1])
    cosz, sinz = jnp.cos(angles[2]), jnp.sin(angles[2])
    yx = [
        [cosy, siny * sinx, siny * cosx],
        [None, cosx, -sinx],
        [-siny, cosy * sinx, cosy * cosx],
    ]
    rot = [
        [cosz * yx[0][0]] + [cosz * yx[0][j] - sinz * yx[1][j] for j in (1, 2)],
        [sinz * yx[0][0]] + [sinz * yx[0][j] + cosz * yx[1][j] for j in (1, 2)],
        yx[2],
    ]
    centre = [-(rot[0][j] * shift[0] + rot[1][j] * shift[1] + rot[2][j] * shift[2]) for j in range(3)]
    return rot, shift, centre


def harmonics(dirx, diry, dirz):
    xx, yy, zz = (dirx * dirx, diry * diry, dirz * dirz)
    return [
        -SH_C1 * diry,
        SH_C1 * dirz,
        -SH_C1 * dirx,
        SH_C2[0] * dirx * diry,
        SH_C2[1] * diry * dirz,
        SH_C2[2] * (2.0 * zz - xx - yy),
        SH_C2[3] * dirx * dirz,
        SH_C2[4] * (xx - yy),
        SH_C3[0] * diry * (3.0 * xx - yy),
        SH_C3[1] * dirx * diry * dirz,
        SH_C3[2] * diry * (4.0 * zz - xx - yy),
        SH_C3[3] * dirz * (2.0 * zz - 3.0 * xx - 3.0 * yy),
        SH_C3[4] * dirx * (4.0 * zz - xx - yy),
        SH_C3[5] * dirz * (xx - yy),
        SH_C3[6] * dirx * (xx - 3.0 * yy),
    ]


def project(pos, logscale, quat, sh, cam):
    rot, shift, centre = cam
    cpos = [rot[i][0] * pos[0] + rot[i][1] * pos[1] + rot[i][2] * pos[2] + shift[i] for i in range(3)]
    inverse = 1.0 / cpos[2]
    u, w = cpos[0] * inverse, cpos[1] * inverse
    tmat = [
        [inverse * (rot[0][j] - u * rot[2][j]) for j in range(3)],
        [inverse * (rot[1][j] - w * rot[2][j]) for j in range(3)],
    ]
    scale = [jnp.exp(s) for s in logscale]
    norm = lax.rsqrt(quat[0] * quat[0] + quat[1] * quat[1] + quat[2] * quat[2] + quat[3] * quat[3])
    qw, qa, qb, qc = [q * norm for q in quat]
    rgau = [
        [1 - 2 * (qb * qb + qc * qc), 2 * (qa * qb - qw * qc), 2 * (qa * qc + qw * qb)],
        [2 * (qa * qb + qw * qc), 1 - 2 * (qa * qa + qc * qc), 2 * (qb * qc - qw * qa)],
        [2 * (qa * qc - qw * qb), 2 * (qb * qc + qw * qa), 1 - 2 * (qa * qa + qb * qb)],
    ]
    trs = [
        [(tmat[r][0] * rgau[0][k] + tmat[r][1] * rgau[1][k] + tmat[r][2] * rgau[2][k]) * scale[k] for k in range(3)]
        for r in range(2)
    ]
    sig_a = trs[0][0] * trs[0][0] + trs[0][1] * trs[0][1] + trs[0][2] * trs[0][2] + BLUR
    sig_b = trs[0][0] * trs[1][0] + trs[0][1] * trs[1][1] + trs[0][2] * trs[1][2]
    sig_c = trs[1][0] * trs[1][0] + trs[1][1] * trs[1][1] + trs[1][2] * trs[1][2] + BLUR
    det_inv = 1.0 / (sig_a * sig_c - sig_b * sig_b)
    dirs = [pos[j] - centre[j] for j in range(3)]
    norm_inv = lax.rsqrt(dirs[0] * dirs[0] + dirs[1] * dirs[1] + dirs[2] * dirs[2])
    basis = harmonics(dirs[0] * norm_inv, dirs[1] * norm_inv, dirs[2] * norm_inv)
    colors = []
    for ch in range(3):
        color = 0.5 + SH_C0 * sh[ch]
        for k in range(1, 16):
            color = color + basis[k - 1] * sh[3 * k + ch]
        colors.append(color)
    return [u, w, sig_c * det_inv, -sig_b * det_inv, sig_a * det_inv] + colors


def spread_attributes(attr_ref, wide_ref):
    for j in range(4):
        part = attr_ref[:, 128 * j : 128 * (j + 1)]
        wide_ref[pl.ds(j, ATTR, stride=8), :] = part
        wide_ref[pl.ds(j + 4, ATTR, stride=8), :] = part


def split_attributes(wide_ref):
    attrs = [wide_ref[8 * a : 8 * (a + 1), :] for a in range(ATTR)]
    return attrs[0:3], attrs[3:6], attrs[6:10], attrs[10], attrs[11:]


def dot(a, b, ca, cb):
    return lax.dot_general(a, b, (((ca,), (cb,)), ((), ())), preferred_element_type=F32)


def lane_gather(x, idx):
    return jnp.take_along_axis(x, idx, axis=1, mode="promise_in_bounds")


def split2(x):
    hi = x.astype(BF16)
    return hi, (x - hi.astype(F32)).astype(BF16)


def split3(x):
    hi = x.astype(BF16)
    rest = x - hi.astype(F32)
    mid = rest.astype(BF16)
    return hi, mid, (rest - mid.astype(F32)).astype(BF16)


def route_kernel(owner_ref, local_ref, attr_ref, cam_ref, asked_ref, rank_ref, inv_ref, rows_ref, wide_ref, tmp_ref):
    before = (
        lax.broadcasted_iota(I32, (SLOTS, SLOTS), 0) < lax.broadcasted_iota(I32, (SLOTS, SLOTS), 1)
    ).astype(F32).astype(BF16)
    every = jnp.ones((SLOTS, SLOTS), BF16)
    oid = lax.broadcasted_iota(I32, (OWNERS, SLOTS), 0)
    kid = lax.broadcasted_iota(I32, (CAP, SLOTS), 0)
    lane = lax.broadcasted_iota(I32, (1, SLOTS), 1)
    base = jnp.zeros((OWNERS, SLOTS), F32)
    table = jnp.zeros((4 * CAP, OWNERS), F32)
    for t in range(TILES):
        owner = owner_ref[:, SLOTS * t : SLOTS * (t + 1)]
        hot = (oid == owner).astype(F32)
        hot16 = hot.astype(BF16)
        count = dot(hot16, before, 1, 0) + base
        base = base + dot(hot16, every, 1, 0)
        rank = jnp.sum(hot * count, axis=0, keepdims=True).astype(I32)
        rank_ref[:, SLOTS * t : SLOTS * (t + 1)] = rank
        place = (kid == rank).astype(F32)
        local = local_ref[t : t + 1, :]
        slot = lane + (SLOTS * t + 1)
        parts = [local & 255, local >> 8, slot & 255, slot >> 8]
        vals = jnp.concatenate([place * p.astype(F32) for p in parts], axis=0).astype(BF16)
        table = table + dot(vals, hot16, 1, 1)
    asked = table[0:CAP] + 256.0 * table[CAP : 2 * CAP]
    inv_ref[...] = (table[2 * CAP : 3 * CAP] + 256.0 * table[3 * CAP :]).astype(I32)
    asked = jnp.concatenate([asked, jnp.zeros((128 - CAP, OWNERS), F32)], axis=0)
    asked_ref[...] = jnp.transpose(asked)
    spread_attributes(attr_ref, wide_ref)
    pos, logscale, quat, logit, sh = split_attributes(wide_ref)
    cam = [jnp.broadcast_to(cam_ref[:, j : j + 1], (8, 128)) for j in range(6)]
    rows = project(pos, logscale, quat, sh, camera_terms(cam[:3], cam[3:]))
    log_opacity = -LOG2E * jnp.log(1.0 + jnp.exp(-logit))
    for c, row in enumerate(rows[:5] + [log_opacity] + rows[5:]):
        tmp_ref[8 * c : 8 * (c + 1), :] = row
    for j in range(4):
        rows_ref[:, 128 * j : 128 * (j + 1)] = tmp_ref[pl.ds(j, 16, stride=8), :]


def serve_kernel(asked_ref, rows_ref, out_ref, ids_ref):
    ids = jnp.transpose(asked_ref[...])[0:CAP].astype(I32)
    ids_ref[...] = ids
    rows = [rows_ref[0:8, 128 * j : 128 * (j + 1)] for j in range(4)]
    last = [jnp.broadcast_to(rows_ref[8:9, 128 * j : 128 * (j + 1)], (8, 128)) for j in range(4)]

    def pick(tables, idx):
        low, high = idx & 127, idx >> 7
        got = lane_gather(tables[0], low)
        for j in range(1, 4):
            got = jnp.where(high == j, lane_gather(tables[j], low), got)
        return got

    main = [pick(rows, jnp.broadcast_to(ids[k : k + 1], (8, 128))) for k in range(CAP)]
    out_ref[pl.ds(0, OWNERS, stride=2), :] = jnp.transpose(jnp.concatenate(main, axis=0))
    more = [pick(last, ids[0:8]), pick(last, ids[8:16]), jnp.zeros((128 - CAP, 128), F32)]
    out_ref[pl.ds(1, OWNERS, stride=2), :] = jnp.transpose(jnp.concatenate(more, axis=0))


def composite_kernel(
    tile_ref, got_ref, owner_ref, rank_ref, inv_ref, depth_ref, cot_ref, image_ref, out_ref,
    par_ref, alpha_ref, pull_ref, weight_ref, grad_ref, stack_ref,
):
    table = jnp.transpose(got_ref[pl.ds(0, OWNERS, stride=2), :])
    table_last = jnp.transpose(got_ref[pl.ds(1, OWNERS, stride=2), :])[0:CAP]
    sub = lax.broadcasted_iota(I32, (8, 128), 0)
    for b in range(8):
        owner = jnp.broadcast_to(owner_ref[:, 128 * b : 128 * (b + 1)], (8, 128))
        rank = jnp.broadcast_to(rank_ref[:, 128 * b : 128 * (b + 1)], (8, 128))
        got = lane_gather(table[0:8], owner)
        for k in range(1, CAP):
            got = jnp.where(rank == k, lane_gather(table[8 * k : 8 * (k + 1)], owner), got)
        par_ref[0:8, 128 * b : 128 * (b + 1)] = got
        low = jnp.where(rank == sub, lane_gather(table_last[0:8], owner), 0.0)
        high = jnp.where(rank == sub + 8, lane_gather(table_last[8:16], owner), 0.0)
        par_ref[8:9, 128 * b : 128 * (b + 1)] = jnp.sum(low + high, axis=0, keepdims=True)

    q = lax.broadcasted_iota(I32, (16, 128), 1)
    row16 = lax.broadcasted_iota(I32, (16, 128), 0)
    X = (q & 15).astype(F32) - 7.5
    Y = (q >> 4).astype(F32) - 3.5
    mono = jnp.where(row16 == 0, 1.0, 0.0)
    for n, m in enumerate([X, Y, X * X, X * Y, Y * Y]):
        mono = jnp.where(row16 == n + 1, m, mono)
    mono8 = mono[0:8]
    mono16 = mono.astype(BF16)
    mono_twice = jnp.concatenate([mono16, mono16], axis=1)
    ex, ey = 1.0 / (16.0 * TILE_COLS), 1.0 / (16.0 * (TILES * OWNERS // TILE_COLS))

    zero = jnp.zeros((1, SLOTS), F32)
    zero5 = jnp.zeros((5, SLOTS), F32)
    blank = jnp.zeros((8, 128), F32)
    cots = []
    geometry = []
    for t in range(TILES):
        par = [par_ref[c : c + 1, SLOTS * t : SLOTS * (t + 1)] for c in range(9)]
        u, w, ca, cb, cc, log_op = par[:6]
        tile = tile_ref[0] + t
        cx = ((tile % TILE_COLS) * 16 + 8).astype(F32) * ex - 0.5
        dx0 = cx - u
        A, B, C = -0.5 * LOG2E * ca, -LOG2E * cb, -0.5 * LOG2E * cc
        colors = jnp.concatenate([par[6], par[7], par[8], zero5], axis=0)
        chi, cmid, clo = [c.astype(F32) for c in split3(colors)]
        dy0s = []
        for h in range(2):
            th = 4 * h + t
            cy = ((tile // TILE_COLS) * 16 + 8 * h + 4).astype(F32) * ey - 0.5
            dy0 = cy - w
            dy0s.append(dy0)
            coef = jnp.concatenate(
                [
                    (A * dx0 + B * dy0) * dx0 + C * dy0 * dy0 + log_op,
                    (2.0 * A * dx0 + B * dy0) * ex,
                    (B * dx0 + 2.0 * C * dy0) * ey,
                    A * (ex * ex),
                    B * (ex * ey),
                    C * (ey * ey),
                    zero,
                    zero,
                ],
                axis=0,
            )
            khi, kmid, klo = [k.astype(F32) for k in split3(coef)]
            left = jnp.concatenate([khi, kmid, klo, chi, chi, chi, cmid, cmid, clo], axis=0)
            left = jnp.concatenate([left, jnp.zeros((128 - 72, SLOTS), F32)], axis=0)
            g = jnp.concatenate([cot_ref[c, t : t + 1, 128 * h : 128 * (h + 1)] for c in range(3)] + [blank[0:5]], axis=0)
            ghi, gmid, glo = [x.astype(F32) for x in split3(g)]
            cots.append((th, ghi, gmid))
            right = jnp.concatenate(
                [
                    jnp.concatenate([mono8, mono8, mono8, blank, blank, blank, blank, blank, blank], axis=0),
                    jnp.concatenate([blank, blank, blank, ghi, gmid, glo, ghi, gmid, ghi], axis=0),
                ],
                axis=1,
            )
            right = jnp.concatenate([right, jnp.zeros((128 - 72, 256), F32)], axis=0)
            both = dot(jnp.transpose(left).astype(BF16), right.astype(BF16), 1, 0)
            alpha_ref[pl.ds(th, SLOTS, stride=8), :] = both[:, :128]
            pull_ref[pl.ds(th, SLOTS, stride=8), :] = both[:, 128:]
        geometry.append((ca, cb, cc, dx0, dy0s, chi, cmid))

    depth = jnp.concatenate([depth_ref[:, 0:128], depth_ref[:, 128:256]], axis=0)
    unroll = 8

    def forward(j, trans):
        for i in range(unroll):
            s = j * unroll + i
            at = pl.ds(pl.multiple_of(s * 8, 8), 8)
            alpha = jnp.where(s < depth, jnp.exp2(alpha_ref[at, :]), 0.0)
            weight = trans * alpha
            alpha_ref[at, :] = alpha
            weight_ref[at, :] = weight
            trans = trans - weight
        return trans

    lax.fori_loop(0, SLOTS // unroll, forward, jnp.ones((8, 128), F32))

    def backward(j, rest):
        for i in range(unroll):
            s = SLOTS - 1 - (j * unroll + i)
            at = pl.ds(pl.multiple_of(s * 8, 8), 8)
            more = pull_ref[at, :] - rest
            rest = rest + alpha_ref[at, :] * more
            pull_ref[at, :] = weight_ref[at, :] * more
        return rest

    lax.fori_loop(0, SLOTS // unroll, backward, jnp.zeros((8, 128), F32))

    cots = {th: (ghi, gmid) for th, ghi, gmid in cots}
    for t in range(TILES):
        ca, cb, cc, dx0, dy0s, chi, cmid = geometry[t]
        color_rows = jnp.concatenate([chi, cmid], axis=0).astype(BF16)
        total = [jnp.zeros((1, SLOTS), F32) for _ in range(6)]
        dcolor = jnp.zeros((3, SLOTS), F32)
        for h in range(2):
            th = 4 * h + t
            dy0 = dy0s[h]
            whi, wlo = split2(weight_ref[pl.ds(th, SLOTS, stride=8), :])
            weights = jnp.concatenate([whi, wlo], axis=1)
            ghi, glo = split2(pull_ref[pl.ds(th, SLOTS, stride=8), :])
            grads = jnp.concatenate([ghi, glo], axis=1)
            seen = dot(color_rows, weights, 1, 0)
            seen = seen[:, :128] + seen[:, 128:]
            seen = seen[0:8] + seen[8:16]
            for c in range(3):
                image_ref[c, t : t + 1, 128 * h : 128 * (h + 1)] = seen[c : c + 1]
            cot = jnp.concatenate(cots[th], axis=0).astype(BF16)
            dcol = dot(jnp.concatenate([cot, cot], axis=1), weights, 1, 1)
            dcolor = dcolor + dcol[0:3] + dcol[8:11]
            mom = dot(mono_twice, grads, 1, 1)
            m0 = mom[0:1]
            mx, my = ex * mom[1:2], ey * mom[2:3]
            total[0] = total[0] + m0
            total[1] = total[1] + dx0 * m0 + mx
            total[2] = total[2] + dy0 * m0 + my
            total[3] = total[3] + dx0 * (dx0 * m0 + 2.0 * mx) + (ex * ex) * mom[3:4]
            total[4] = total[4] + dx0 * (dy0 * m0 + my) + dy0 * mx + (ex * ey) * mom[4:5]
            total[5] = total[5] + dy0 * (dy0 * m0 + 2.0 * my) + (ey * ey) * mom[5:6]
        s0, sx, sy, sxx, sxy, syy = total
        made = [ca * sx + cb * sy, cb * sx + cc * sy, -0.5 * sxx, -sxy, -0.5 * syy, s0, dcolor]
        grad_ref[0:9, SLOTS * t : SLOTS * (t + 1)] = jnp.concatenate(made, axis=0)

    inv = inv_ref[...]

    def pick(tables, idx):
        at = jnp.maximum(idx - 1, 0)
        low, high = at & 127, at >> 7
        got = lane_gather(tables[0], low)
        for j in range(1, 8):
            got = jnp.where(high == j, lane_gather(tables[j], low), got)
        return jnp.where(idx > 0, got, 0.0)

    tables = [grad_ref[0:8, 128 * j : 128 * (j + 1)] for j in range(8)]
    last = [jnp.broadcast_to(grad_ref[8:9, 128 * j : 128 * (j + 1)], (8, 128)) for j in range(8)]
    main = [pick(tables, jnp.broadcast_to(inv[k : k + 1], (8, 128))) for k in range(CAP)]
    out_ref[pl.ds(0, OWNERS, stride=2), :] = jnp.transpose(jnp.concatenate(main, axis=0))
    more = [pick(last, inv[0:8]), pick(last, inv[8:16]), jnp.zeros((128 - CAP, 128), F32)]
    out_ref[pl.ds(1, OWNERS, stride=2), :] = jnp.transpose(jnp.concatenate(more, axis=0))


def collect_kernel(back_ref, ids_ref, cam_ref, out_ref):
    table = jnp.transpose(back_ref[pl.ds(0, OWNERS, stride=2), :])
    table_last = jnp.transpose(back_ref[pl.ds(1, OWNERS, stride=2), :])[0:CAP]
    lid = lax.broadcasted_iota(I32, (G_DEV, 128), 0)
    acc = jnp.zeros((48, G_DEV), F32)
    pad = jnp.zeros((7, 128), F32)
    for k in range(0, CAP, 2):
        lefts, hots = [], []
        for kk in (k, k + 1):
            both = jnp.concatenate([table[8 * kk : 8 * (kk + 1)], table_last[kk : kk + 1], pad], axis=0)
            lefts.append(jnp.concatenate(split3(both), axis=0))
            hots.append((lid == ids_ref[kk : kk + 1, :]).astype(F32).astype(BF16))
        acc = acc + dot(jnp.concatenate(lefts, axis=1), jnp.concatenate(hots, axis=1), 1, 1)
    rows = acc[0:16] + acc[16:32] + acc[32:48]
    blank = jnp.zeros((8, 128), F32)
    for v in range(VIEWS):
        for j in range(4):
            out_ref[pl.ds(40 * v + j, 9, stride=4), :] = rows[0:9, 128 * j : 128 * (j + 1)]
        out_ref[40 * v + 36 : 40 * v + 40, :] = blank[0:4]
        out_ref[40 * v + 36 : 40 * v + 37, 0:6] = cam_ref[...]


def pull_kernel(all_ref, attr_ref, out_ref, wide_ref, res_ref):
    spread_attributes(attr_ref, wide_ref)
    pos, logscale, quat, logit, sh = split_attributes(wide_ref)
    total = None
    opacity_grad = None
    for pair in range(VIEWS // 2):
        starts = (80 * pair, 80 * pair + 40)
        cot = [
            jnp.concatenate([all_ref[s + 4 * c : s + 4 * c + 4, :] for s in starts], axis=0) for c in range(9)
        ]
        cam = [
            jnp.concatenate(
                [jnp.broadcast_to(all_ref[s + 36 : s + 37, j : j + 1], (4, 128)) for s in starts], axis=0
            )
            for j in range(6)
        ]
        terms = camera_terms(cam[:3], cam[3:])
        _, pull = jax.vjp(lambda a, b, c, d: project(a, b, c, d, terms), pos, logscale, quat, sh)
        grads = jax.tree.leaves(pull(cot[:5] + cot[6:]))
        total = grads if total is None else [a + b for a, b in zip(total, grads)]
        opacity_grad = cot[5] if opacity_grad is None else opacity_grad + cot[5]
    grads = total[:10] + [opacity_grad / (1.0 + jnp.exp(logit))] + total[10:]
    for a in range(ATTR):
        res_ref[4 * a : 4 * a + 4, :] = grads[a][0:4] + grads[a][4:8]
    for j in range(4):
        out_ref[:, 128 * j : 128 * (j + 1)] = res_ref[pl.ds(j, ATTR, stride=4), :]


VMEM = pl.BlockSpec(memory_space=pltpu.VMEM)
SMEM = pl.BlockSpec(memory_space=pltpu.SMEM)
PARAMS = pltpu.CompilerParams(vmem_limit_bytes=24 * 1024 * 1024)


def call(kernel, outs, args, scratch=(), in_specs=None):
    return pl.pallas_call(
        kernel,
        out_shape=[jax.ShapeDtypeStruct(s, d) for s, d in outs],
        in_specs=in_specs or [VMEM] * len(args),
        out_specs=[VMEM] * len(outs),
        scratch_shapes=[pltpu.VMEM(s, F32) for s in scratch],
        compiler_params=PARAMS,
    )(*args)


def route(owner, local, attributes, camera):
    return call(
        route_kernel,
        [((OWNERS, 128), F32), ((1, TILES * SLOTS), I32), ((CAP, OWNERS), I32), ((16, G_DEV), F32)],
        (owner, local, attributes, camera),
        [(ATTR * 8, 128), (128, 128)],
    )


def serve(asked, rows):
    return call(serve_kernel, [((2 * OWNERS, 128), F32), ((CAP, OWNERS), I32)], (asked, rows))


def composite(first_tile, got, owner, rank, inv, depth, cot):
    big = (SLOTS * 8, 128)
    return call(
        composite_kernel,
        [((3, TILES, 256), F32), ((2 * OWNERS, 128), F32)],
        (first_tile, got, owner, rank, inv, depth, cot),
        [(16, TILES * SLOTS), big, big, big, (16, TILES * SLOTS), (8, 128)],
        [SMEM] + [VMEM] * 6,
    )


def collect(back, ids, camera):
    return call(collect_kernel, [((40 * VIEWS, 128), F32)], (back, ids, camera))[0]


def pull_back(everything, attributes):
    return call(
        pull_kernel, [((ATTR, G_DEV), F32)], (everything, attributes), [(ATTR * 8, 128), (ATTR * 4, 128)]
    )[0]


def exchange(x, axis="dev"):
    return lax.all_to_all(x, axis, split_axis=0, concat_axis=0, tiled=True)


def per_device(attributes, camera, list_owner, list_local, term_depth, image_cot):
    owner = list_owner.reshape(1, -1)
    asked, rank, inv, rows = route(owner, list_local[0], attributes, camera)
    asked = exchange(asked.reshape(OWNERS, 1, 128)).reshape(OWNERS, 128)
    sent, ids = serve(asked, rows)
    got = exchange(sent.reshape(OWNERS, 2, 128)).reshape(2 * OWNERS, 128)
    first_tile = (lax.axis_index("dev") * TILES).astype(I32).reshape(1)
    image, grads = composite(first_tile, got, owner, rank, inv, term_depth[0], image_cot[0])
    back = exchange(grads.reshape(OWNERS, 2, 128)).reshape(2 * OWNERS, 128)
    mine = collect(back, ids, camera)
    everything = exchange(mine.reshape(VIEWS, 40, 128), "view").reshape(VIEWS * 40, 128)
    return image[None], pull_back(everything, attributes)


def solution(mesh):
    in_specs = (
        P(None, "dev"),
        P("view", None),
        P("view", "dev", None, None),
        P("view", "dev", None),
        P("view", "dev", None),
        P("view", None, "dev", None),
    )
    out_specs = (P("view", None, "dev", None), P(None, "dev"))
    return jax.shard_map(
        per_device, mesh=mesh, in_specs=in_specs, out_specs=out_specs, check_vma=False
    )
```

time: 318 us -> 102 us (0.32)
  local copies, waits for them, and re-layouts: 94.4 us -> 3.65 us
  waiting for transfers between devices: 62 us -> 16.1 us
  blocking collectives: 23.4 us -> 67.2 us
  other arithmetic: 40.8 us -> 0 us
  between operations: 37.4 us -> 0.68 us
  starting transfers between devices: 37 us -> 5.8 us
  loops' own time: 14 us -> 0 us
  Pallas kernels: 0 us -> 7.8 us
  matrix products: 6.13 us -> 0 us
    psum x1 -> x0, waiting for transfers between devices: 46.2 us -> none  [per_device(): total = lax.psum(attr_grad, 'view')]
    all_to_all x1 -> x3, blocking collectives: 23.4 us -> 67.2 us  [exchange(): return lax.all_to_all(x, axis, split_axis=0, concat_axis=0, tiled=True)]
    all_to_all x2 -> x1, starting transfers between devices: 36.8 us -> 5.8 us  [exchange(): return lax.all_to_all(x, axis, split_axis=0, concat_axis=0, tiled=True)]
    slice x190 -> x0, local copies, waits for them, and re-layouts: 19.9 us -> none  [the longest x180 18.3 us: tile_color(): keep = jnp.cumprod(1.0 - alpha, axis=1)]
    split x48 -> x0, local copies, waits for them, and re-layouts: 15.2 us -> none  [tile_color(): keep = jnp.cumprod(1.0 - alpha, axis=1)]
    another operation x1 -> x0, loops' own time: 14 us -> none  [composite(): color, grads = lax.map(tile_work, (rows_tiles, tile_ids, depth, cotangent))]
    while x92 -> x0, local copies, waits for them, and re-layouts: 13.6 us -> none
    gather x3 -> x0, local copies, waits for them, and re-layouts: 12.8 us -> none  [the longest x1 5.46 us: per_device(): sent = rows_owner[:, asked]]
  transfers between devices with their start and end apart: 3 -> 1, of which waited for: 2 -> 1; matrix products, arithmetic and copies ran while one was open for 1% -> 0% of each run, Pallas kernels for 0% -> 0%
where the time goes in v1:
time: 102 us; the launch traced here: 101 us
  blocking collectives  67.2 us (66%)
  waiting for transfers between devices  16.1 us (16%)
  Pallas kernels  7.8 us (8%)
  starting transfers between devices  5.8 us (6%)
  local copies, waits for them, and re-layouts  3.65 us (4%)
    all_to_all x3, blocking collectives, exchange(): return lax.all_to_all(x, axis, split_axis=0, concat_axis=0, tiled=True)  67.2 us
    all_to_all x1, waiting for transfers between devices, exchange(): return lax.all_to_all(x, axis, split_axis=0, concat_axis=0, tiled=True)  16.1 us
    pallas_call x5, Pallas kernels, call(): pl.pallas_call(kernel, out_shape=[jax.ShapeDtypeStruct(s, d) for s, d in...  7.8 us
    all_to_all x1, starting transfers between devices, exchange(): return lax.all_to_all(x, axis, split_axis=0, concat_axis=0, tiled=True)  5.8 us
    unnamed x16, local copies, waits for them, and re-layouts  3.65 us
  transfers between devices with their start and end apart: 1, of which 1 were waited for; matrix products, arithmetic and copies ran while one was open for 0% of the time, Pallas kernels for 0%

profile of v1, /device:TPU:1, one launch (start us, length us, event | category | flops | bytes accessed | tf_op | source)
XLA Modules:
  0.0 101.2 jit_solution(4498223102026314074)
XLA Ops:
  0.6 0.0 copy-start.7
  0.6 0.6 copy-done.7
  1.3 0.0 copy-start
  1.3 0.9 copy-done
  2.2 0.0 copy-start.2
  2.2 0.7 copy-done.2
  2.9 0.0 copy-start.5
  2.9 0.7 copy-done.5
  3.6 0.6 shard_map.77
  4.2 35.3 %all_to_all.20 = f32[128,1,128]{2,1,0:T(1,128)S(1)} all-to-all(f32[128,1,128]{2,1,0:T(1,128)S(1)} %bitcast.22), channel_id=1, replica_groups=mesh['view'=4,'dev'=128] {'dev'}, dimensions={0} | all-to-all | bytes 131072 | tf_op jit(solution)/shard_map/all_to_all | solution.py:471
  39.4 1.1 %shard_map.78 = (f32[256,128]{1,0:T(8,128)}, s32[16,128]{1,0:T(8,128)S(1)}) custom-call(f32[128,128]{1,0:T(8,128)S(1)} %bitcast.20, f32[16,512]{1,0:T(8,128)S(1)} %get-tuple-element.11.rows_ref), custom_call_target="tpu_custom_call" | custom-call | tf_op jit(solution)/shard_map/pallas_call | solution.py:426
  40.5 0.0 copy-start.6
  40.5 5.8 %all-to-all-start.1 = ((f32[128,2,128]{2,1,0:T(2,128)}), f32[128,2,128]{2,1,0:T(2,128)S(1)}, u32[]{:S(2)}, u32[]{:S(2)}) async-start(f32[128,2,128]{2,1,0:T(2,128)} %bitcast.6), calls=%async_computation.1 | async-start | bytes 262144 | tf_op jit(solution)/shard_map/all_to_all | solution.py:471
  46.3 0.0 copy-start.4
  46.3 16.1 %all-to-all-done.1 = f32[128,2,128]{2,1,0:T(2,128)S(1)} async-done(((f32[128,2,128]{2,1,0:T(2,128)}), f32[128,2,128]{2,1,0:T(2,128)S(1)}, u32[]{:S(2)}, u32[]{:S(2)}) %all-to-all-start.1) | async-done | bytes 131104 | tf_op jit(solution)/shard_map/all_to_all | solution.py:471
  62.4 0.0 copy-start.3
  62.4 0.0 copy-done.6
  62.4 0.0 copy-done.4
  62.4 0.7 copy-done.3
  63.1 4.3 %shard_map.79 = (f32[3,4,256]{2,1,0:T(4,128)}, f32[256,128]{1,0:T(8,128)S(1)}) custom-call(s32[1]{0:T(128)} %bitcast.tile_ref, f32[256,128]{1,0:T(8,128)S(1)} %bitcast.16, s32[1,1024]{1,0:T(1,128)S(1)} %bitcast.24, s32[1,1024]{1,0:T(1,128)S(1)} %get-tuple-element.13.rank_ref, s32[16,128]{1,0:T(8,128)S(1)} %get-tuple-element.14.inv_ref, ...), custom_call_target="tpu_custom_call" | custom-call | tf_op jit(solution)/shard_map/pallas_call | solution.py:426
  67.4 23.4 %all_to_all.21 = f32[128,2,128]{2,1,0:T(2,128)S(1)} all-to-all(f32[128,2,128]{2,1,0:T(2,128)S(1)} %bitcast.21), channel_id=1, replica_groups=mesh['view'=4,'dev'=128] {'dev'}, dimensions={0} | all-to-all | bytes 262144 | tf_op jit(solution)/shard_map/all_to_all | solution.py:471
  90.8 0.7 shard_map.80
  91.5 0.0 copy-start.1
  91.6 8.5 %all_to_all.22 = f32[4,40,128]{2,1,0:T(8,128)S(1)} all-to-all(f32[4,40,128]{2,1,0:T(8,128)S(1)} %bitcast.18), channel_id=1, replica_groups=mesh['view'=4,'dev'=128] {'view'}, dimensions={0} | all-to-all | bytes 163840 | tf_op jit(solution)/shard_map/all_to_all | solution.py:471
  100.1 0.0 copy-done.1
  100.1 1.1 %shard_map.81 = f32[59,512]{1,0:T(8,128)} custom-call(f32[160,128]{1,0:T(8,128)S(1)} %bitcast.19, f32[59,512]{1,0:T(8,128)S(1)} %copy-done.1), custom_call_target="tpu_custom_call" | custom-call | tf_op jit(solution)/shard_map/pallas_call | solution.py:426
Async XLA Ops:
  0.6 0.7 copy-start.7
  1.3 0.9 copy-start
  2.2 0.7 copy-start.2
  2.9 0.7 copy-start.5
  40.5 21.9 %copy-start.6 = (s32[1,4,256]{2,1,0:T(4,128)S(1)}, s32[1,4,256]{2,1,0:T(4,128)}, u32[]{:S(2)}) copy-start(s32[1,4,256]{2,1,0:T(4,128)} %param.10) | copy-start | bytes 12292
  40.5 21.9 %all-to-all-start.1 = ((f32[128,2,128]{2,1,0:T(2,128)}), f32[128,2,128]{2,1,0:T(2,128)S(1)}, u32[]{:S(2)}, u32[]{:S(2)}) async-start(f32[128,2,128]{2,1,0:T(2,128)} %bitcast.6), calls=%async_computation.1 | async-start | bytes 262144 | tf_op jit(solution)/shard_map/all_to_all | solution.py:471
  46.3 16.1 %copy-start.4 = (f32[1,3,4,256]{3,2,1,0:T(4,128)S(1)}, f32[1,3,4,256]{3,2,1,0:T(4,128)}, u32[]{:S(2)}) copy-start(f32[1,3,4,256]{3,2,1,0:T(4,128)} %param.11) | copy-start | bytes 36868
  62.4 0.7 copy-start.3
  91.5 8.5 %copy-start.1 = (f32[59,512]{1,0:T(8,128)S(1)}, f32[59,512]{1,0:T(8,128)}, u32[]{:S(2)}) copy-start(f32[59,512]{1,0:T(8,128)} %attr_ref.3) | copy-start | bytes 362500

commit v2 on v1

--- a/solution.py
+++ b/solution.py
@@ -10,6 +10,7 @@
 SLOTS = 256
 CAP = 16
 OWNERS = 128
+PLANES = 16
 G_DEV = 512
 ATTR = 59
 VIEWS = 4
@@ -148,16 +149,25 @@
     return hi, mid, (rest - mid.astype(F32)).astype(BF16)
 
 
-def route_kernel(owner_ref, local_ref, attr_ref, cam_ref, asked_ref, rank_ref, inv_ref, rows_ref, wide_ref, tmp_ref):
+def route_kernel(
+    owner_hbm, local_hbm, attr_hbm, cam_hbm, asked_ref, inv_ref, place_ref, rows_ref,
+    owner_ref, local_ref, attr_ref, cam_ref, wide_ref, sem,
+):
+    pairs = [(owner_hbm, owner_ref), (local_hbm, local_ref), (attr_hbm, attr_ref), (cam_hbm, cam_ref)]
+    copies = [pltpu.make_async_copy(src, dst, sem.at[n]) for n, (src, dst) in enumerate(pairs)]
+    for copy in copies:
+        copy.start()
     before = (
         lax.broadcasted_iota(I32, (SLOTS, SLOTS), 0) < lax.broadcasted_iota(I32, (SLOTS, SLOTS), 1)
     ).astype(F32).astype(BF16)
     every = jnp.ones((SLOTS, SLOTS), BF16)
     oid = lax.broadcasted_iota(I32, (OWNERS, SLOTS), 0)
-    kid = lax.broadcasted_iota(I32, (CAP, SLOTS), 0)
+    zid = lax.broadcasted_iota(I32, (PLANES, SLOTS), 0)
     lane = lax.broadcasted_iota(I32, (1, SLOTS), 1)
     base = jnp.zeros((OWNERS, SLOTS), F32)
-    table = jnp.zeros((4 * CAP, OWNERS), F32)
+    table = jnp.zeros((4 * PLANES, 128), F32)
+    copies[0].wait()
+    copies[1].wait()
     for t in range(TILES):
         owner = owner_ref[:, SLOTS * t : SLOTS * (t + 1)]
         hot = (oid == owner).astype(F32)
@@ -165,63 +175,75 @@
         count = dot(hot16, before, 1, 0) + base
         base = base + dot(hot16, every, 1, 0)
         rank = jnp.sum(hot * count, axis=0, keepdims=True).astype(I32)
-        rank_ref[:, SLOTS * t : SLOTS * (t + 1)] = rank
-        place = (kid == rank).astype(F32)
+        plane = owner >> 3
+        lanes = (owner & 7) * CAP + rank
+        place_ref[0:1, SLOTS * t : SLOTS * (t + 1)] = plane
+        place_ref[1:2, SLOTS * t : SLOTS * (t + 1)] = lanes
+        hot_plane = (zid == plane).astype(F32)
+        hot_lane = (oid == lanes).astype(F32).astype(BF16)
         local = local_ref[t : t + 1, :]
         slot = lane + (SLOTS * t + 1)
         parts = [local & 255, local >> 8, slot & 255, slot >> 8]
-        vals = jnp.concatenate([place * p.astype(F32) for p in parts], axis=0).astype(BF16)
-        table = table + dot(vals, hot16, 1, 1)
-    asked = table[0:CAP] + 256.0 * table[CAP : 2 * CAP]
-    inv_ref[...] = (table[2 * CAP : 3 * CAP] + 256.0 * table[3 * CAP :]).astype(I32)
-    asked = jnp.concatenate([asked, jnp.zeros((128 - CAP, OWNERS), F32)], axis=0)
-    asked_ref[...] = jnp.transpose(asked)
+        vals = jnp.concatenate([hot_plane * p.astype(F32) for p in parts], axis=0).astype(BF16)
+        table = table + dot(vals, hot_lane, 1, 1)
+    n = PLANES
+    asked_ref[...] = table[0:n] + 256.0 * table[n : 2 * n]
+    inv_ref[...] = (table[2 * n : 3 * n] + 256.0 * table[3 * n :]).astype(I32)
+    copies[2].wait()
+    copies[3].wait()
     spread_attributes(attr_ref, wide_ref)
     pos, logscale, quat, logit, sh = split_attributes(wide_ref)
     cam = [jnp.broadcast_to(cam_ref[:, j : j + 1], (8, 128)) for j in range(6)]
     rows = project(pos, logscale, quat, sh, camera_terms(cam[:3], cam[3:]))
     log_opacity = -LOG2E * jnp.log(1.0 + jnp.exp(-logit))
-    for c, row in enumerate(rows[:5] + [log_opacity] + rows[5:]):
-        tmp_ref[8 * c : 8 * (c + 1), :] = row
+    rows = rows[:5] + [log_opacity] + rows[5:]
+    for c in range(8):
+        rows_ref[pl.ds(c, 4, stride=8), :] = rows[c][0:4]
+    rows_ref[32:36, :] = rows[8][0:4]
+    rows_ref[36:40, :] = jnp.zeros((4, 128), F32)
+
+
+def serve_kernel(asked_ref, rows_ref, out_ref):
+    table = []
     for j in range(4):
-        rows_ref[:, 128 * j : 128 * (j + 1)] = tmp_ref[pl.ds(j, 16, stride=8), :]
-
-
-def serve_kernel(asked_ref, rows_ref, out_ref, ids_ref):
-    ids = jnp.transpose(asked_ref[...])[0:CAP].astype(I32)
-    ids_ref[...] = ids
-    rows = [rows_ref[0:8, 128 * j : 128 * (j + 1)] for j in range(4)]
-    last = [jnp.broadcast_to(rows_ref[8:9, 128 * j : 128 * (j + 1)], (8, 128)) for j in range(4)]
-
-    def pick(tables, idx):
-        low, high = idx & 127, idx >> 7
-        got = lane_gather(tables[0], low)
-        for j in range(1, 4):
-            got = jnp.where(high == j, lane_gather(tables[j], low), got)
-        return got
-
-    main = [pick(rows, jnp.broadcast_to(ids[k : k + 1], (8, 128))) for k in range(CAP)]
-    out_ref[pl.ds(0, OWNERS, stride=2), :] = jnp.transpose(jnp.concatenate(main, axis=0))
-    more = [pick(last, ids[0:8]), pick(last, ids[8:16]), jnp.zeros((128 - CAP, 128), F32)]
-    out_ref[pl.ds(1, OWNERS, stride=2), :] = jnp.transpose(jnp.concatenate(more, axis=0))
+        part = [rows_ref[40 * r + 8 * j : 40 * r + 8 * j + 8, :] for r in range(8)]
+        part.append(rows_ref[pl.ds(32 + j, 8, stride=40), :])
+        table.append(jnp.concatenate(part, axis=0))
+    table = [x.astype(F32) for x in split3(jnp.concatenate(table, axis=1))]
+    table = jnp.concatenate(table + [jnp.zeros((8, G_DEV), F32)], axis=0).astype(BF16)
+    lid = lax.broadcasted_iota(I32, (G_DEV, 256), 0)
+    sub = lax.broadcasted_iota(I32, (8, 128), 0)
+    near = lax.broadcasted_iota(I32, (8, 128), 1) >> 4
+    for z in range(0, PLANES, 2):
+        ids = jnp.concatenate([asked_ref[z : z + 1, :], asked_ref[z + 1 : z + 2, :]], axis=1).astype(I32)
+        hot = (lid == ids).astype(F32).astype(BF16)
+        got = dot(table, hot, 1, 0)
+        got = got[0:72] + got[72:144] + got[144:216]
+        for i in range(2):
+            half = got[:, 128 * i : 128 * (i + 1)]
+            main = half[0:8]
+            for r in range(1, 8):
+                main = jnp.where(near == r, half[8 * r : 8 * (r + 1)], main)
+            out_ref[9 * (z + i) : 9 * (z + i) + 8, :] = main
+            last = jnp.sum(jnp.where(near == sub, half[64:72], 0.0), axis=0, keepdims=True)
+            out_ref[9 * (z + i) + 8 : 9 * (z + i) + 9, :] = last
 
 
 def composite_kernel(
-    tile_ref, got_ref, owner_ref, rank_ref, inv_ref, depth_ref, cot_ref, image_ref, out_ref,
-    par_ref, alpha_ref, pull_ref, weight_ref, grad_ref, stack_ref,
+    tile_ref, got_ref, place_ref, inv_ref, depth_ref, cot_ref, image_ref, out_ref,
+    par_ref, alpha_ref, pull_ref, weight_ref, grad_ref,
 ):
-    table = jnp.transpose(got_ref[pl.ds(0, OWNERS, stride=2), :])
-    table_last = jnp.transpose(got_ref[pl.ds(1, OWNERS, stride=2), :])[0:CAP]
+    last = got_ref[pl.ds(8, PLANES, stride=9), :]
     sub = lax.broadcasted_iota(I32, (8, 128), 0)
     for b in range(8):
-        owner = jnp.broadcast_to(owner_ref[:, 128 * b : 128 * (b + 1)], (8, 128))
-        rank = jnp.broadcast_to(rank_ref[:, 128 * b : 128 * (b + 1)], (8, 128))
-        got = lane_gather(table[0:8], owner)
-        for k in range(1, CAP):
-            got = jnp.where(rank == k, lane_gather(table[8 * k : 8 * (k + 1)], owner), got)
+        plane = jnp.broadcast_to(place_ref[0:1, 128 * b : 128 * (b + 1)], (8, 128))
+        lanes = jnp.broadcast_to(place_ref[1:2, 128 * b : 128 * (b + 1)], (8, 128))
+        got = lane_gather(got_ref[0:8, :], lanes)
+        for z in range(1, PLANES):
+            got = jnp.where(plane == z, lane_gather(got_ref[9 * z : 9 * z + 8, :], lanes), got)
         par_ref[0:8, 128 * b : 128 * (b + 1)] = got
-        low = jnp.where(rank == sub, lane_gather(table_last[0:8], owner), 0.0)
-        high = jnp.where(rank == sub + 8, lane_gather(table_last[8:16], owner), 0.0)
+        low = jnp.where(plane == sub, lane_gather(last[0:8], lanes), 0.0)
+        high = jnp.where(plane == sub + 8, lane_gather(last[8:16], lanes), 0.0)
         par_ref[8:9, 128 * b : 128 * (b + 1)] = jnp.sum(low + high, axis=0, keepdims=True)
 
     q = lax.broadcasted_iota(I32, (16, 128), 1)
@@ -361,35 +383,49 @@
 
     tables = [grad_ref[0:8, 128 * j : 128 * (j + 1)] for j in range(8)]
     last = [jnp.broadcast_to(grad_ref[8:9, 128 * j : 128 * (j + 1)], (8, 128)) for j in range(8)]
-    main = [pick(tables, jnp.broadcast_to(inv[k : k + 1], (8, 128))) for k in range(CAP)]
-    out_ref[pl.ds(0, OWNERS, stride=2), :] = jnp.transpose(jnp.concatenate(main, axis=0))
-    more = [pick(last, inv[0:8]), pick(last, inv[8:16]), jnp.zeros((128 - CAP, 128), F32)]
-    out_ref[pl.ds(1, OWNERS, stride=2), :] = jnp.transpose(jnp.concatenate(more, axis=0))
-
-
-def collect_kernel(back_ref, ids_ref, cam_ref, out_ref):
-    table = jnp.transpose(back_ref[pl.ds(0, OWNERS, stride=2), :])
-    table_last = jnp.transpose(back_ref[pl.ds(1, OWNERS, stride=2), :])[0:CAP]
-    lid = lax.broadcasted_iota(I32, (G_DEV, 128), 0)
-    acc = jnp.zeros((48, G_DEV), F32)
-    pad = jnp.zeros((7, 128), F32)
-    for k in range(0, CAP, 2):
-        lefts, hots = [], []
-        for kk in (k, k + 1):
-            both = jnp.concatenate([table[8 * kk : 8 * (kk + 1)], table_last[kk : kk + 1], pad], axis=0)
-            lefts.append(jnp.concatenate(split3(both), axis=0))
-            hots.append((lid == ids_ref[kk : kk + 1, :]).astype(F32).astype(BF16))
-        acc = acc + dot(jnp.concatenate(lefts, axis=1), jnp.concatenate(hots, axis=1), 1, 1)
-    rows = acc[0:16] + acc[16:32] + acc[32:48]
-    blank = jnp.zeros((8, 128), F32)
+    for z in range(PLANES):
+        out_ref[9 * z : 9 * z + 8, :] = pick(tables, jnp.broadcast_to(inv[z : z + 1], (8, 128)))
+    more = jnp.concatenate([pick(last, inv[0:8]), pick(last, inv[8:16])], axis=0)
+    out_ref[pl.ds(8, PLANES, stride=9), :] = more
+
+
+def collect_kernel(back_ref, asked_ref, cam_ref, out_ref):
+    lid = lax.broadcasted_iota(I32, (G_DEV, 256), 0)
+    sub = lax.broadcasted_iota(I32, (8, 128), 0)
+    near = lax.broadcasted_iota(I32, (8, 128), 1) >> 4
+    acc = jnp.zeros((144, G_DEV), F32)
+    for z in range(0, PLANES, 2):
+        ids = jnp.concatenate([asked_ref[z : z + 1, :], asked_ref[z + 1 : z + 2, :]], axis=1).astype(I32)
+        hot = (lid == ids).astype(F32).astype(BF16)
+        left = []
+        for i in range(2):
+            at = 9 * (z + i)
+            main = [x.astype(F32) for x in split2(back_ref[at : at + 8, :])]
+            last = [x.astype(F32) for x in split2(jnp.broadcast_to(back_ref[at + 8 : at + 9, :], (8, 128)))]
+            rows = []
+            for m, l in zip(main, last):
+                rows += [jnp.where(near == r, m, 0.0) for r in range(8)] + [jnp.where(near == sub, l, 0.0)]
+            left.append(jnp.concatenate(rows, axis=0).astype(BF16))
+        acc = acc + dot(jnp.concatenate(left, axis=1), hot, 1, 1)
+    rows = acc[0:72] + acc[72:144]
+    cam = jnp.concatenate([cam_ref[...], jnp.zeros((1, 122), F32)], axis=1)
+    tail = jnp.concatenate([cam, jnp.zeros((3, 128), F32)], axis=0)
+    for r in range(8):
+        part = [rows[8 * r : 8 * r + 8, 128 * j : 128 * (j + 1)] for j in range(4)]
+        part += [rows[64 + r : 65 + r, 128 * j : 128 * (j + 1)] for j in range(4)] + [tail]
+        part = jnp.concatenate(part, axis=0)
+        for v in range(VIEWS):
+            out_ref[40 * (8 * v + r) : 40 * (8 * v + r + 1), :] = part
+
+
+def pull_kernel(parts_ref, attr_ref, out_ref, wide_ref, res_ref, all_ref):
     for v in range(VIEWS):
-        for j in range(4):
-            out_ref[pl.ds(40 * v + j, 9, stride=4), :] = rows[0:9, 128 * j : 128 * (j + 1)]
-        out_ref[40 * v + 36 : 40 * v + 40, :] = blank[0:4]
-        out_ref[40 * v + 36 : 40 * v + 37, 0:6] = cam_ref[...]
-
-
-def pull_kernel(all_ref, attr_ref, out_ref, wide_ref, res_ref):
+        start = 320 * v
+        total = parts_ref[start : start + 36, :]
+        for r in range(1, 8):
+            total = total + parts_ref[start + 40 * r : start + 40 * r + 36, :]
+        all_ref[40 * v : 40 * v + 36, :] = total
+        all_ref[40 * v + 36 : 40 * v + 40, :] = parts_ref[start + 36 : start + 40, :]
     spread_attributes(attr_ref, wide_ref)
     pos, logscale, quat, logit, sh = split_attributes(wide_ref)
     total = None
@@ -397,8 +433,9 @@
     for pair in range(VIEWS // 2):
         starts = (80 * pair, 80 * pair + 40)
         cot = [
-            jnp.concatenate([all_ref[s + 4 * c : s + 4 * c + 4, :] for s in starts], axis=0) for c in range(9)
+            jnp.concatenate([all_ref[pl.ds(s + c, 4, stride=8), :] for s in starts], axis=0) for c in range(8)
         ]
+        cot.append(jnp.concatenate([all_ref[s + 32 : s + 36, :] for s in starts], axis=0))
         cam = [
             jnp.concatenate(
                 [jnp.broadcast_to(all_ref[s + 36 : s + 37, j : j + 1], (4, 128)) for s in starts], axis=0
@@ -419,70 +456,89 @@
 
 VMEM = pl.BlockSpec(memory_space=pltpu.VMEM)
 SMEM = pl.BlockSpec(memory_space=pltpu.SMEM)
-PARAMS = pltpu.CompilerParams(vmem_limit_bytes=24 * 1024 * 1024)
-
-
-def call(kernel, outs, args, scratch=(), in_specs=None):
+HBM = pl.BlockSpec(memory_space=pl.ANY)
+MIB = 1024 * 1024
+
+
+def call(kernel, outs, args, scratch=(), in_specs=None, limit=24):
     return pl.pallas_call(
         kernel,
         out_shape=[jax.ShapeDtypeStruct(s, d) for s, d in outs],
         in_specs=in_specs or [VMEM] * len(args),
         out_specs=[VMEM] * len(outs),
-        scratch_shapes=[pltpu.VMEM(s, F32) for s in scratch],
-        compiler_params=PARAMS,
+        scratch_shapes=list(scratch),
+        compiler_params=pltpu.CompilerParams(vmem_limit_bytes=limit * MIB),
     )(*args)
+
+
+def vmem(*shape, dtype=F32):
+    return pltpu.VMEM(shape, dtype)
 
 
 def route(owner, local, attributes, camera):
     return call(
         route_kernel,
-        [((OWNERS, 128), F32), ((1, TILES * SLOTS), I32), ((CAP, OWNERS), I32), ((16, G_DEV), F32)],
+        [((PLANES, 128), F32), ((PLANES, 128), I32), ((8, TILES * SLOTS), I32), ((40, 128), F32)],
         (owner, local, attributes, camera),
-        [(ATTR * 8, 128), (128, 128)],
+        [
+            vmem(1, TILES * SLOTS, dtype=I32), vmem(TILES, SLOTS, dtype=I32), vmem(ATTR, G_DEV), vmem(1, 6),
+            vmem(ATTR * 8, 128), pltpu.SemaphoreType.DMA((4,)),
+        ],
+        [HBM] * 4,
+        60,
     )
 
 
 def serve(asked, rows):
-    return call(serve_kernel, [((2 * OWNERS, 128), F32), ((CAP, OWNERS), I32)], (asked, rows))
-
-
-def composite(first_tile, got, owner, rank, inv, depth, cot):
-    big = (SLOTS * 8, 128)
+    return call(serve_kernel, [((9 * PLANES, 128), F32)], (asked, rows))[0]
+
+
+def composite(first_tile, got, place, inv, depth, cot):
+    big = vmem(SLOTS * 8, 128)
     return call(
         composite_kernel,
-        [((3, TILES, 256), F32), ((2 * OWNERS, 128), F32)],
-        (first_tile, got, owner, rank, inv, depth, cot),
-        [(16, TILES * SLOTS), big, big, big, (16, TILES * SLOTS), (8, 128)],
-        [SMEM] + [VMEM] * 6,
+        [((3, TILES, 256), F32), ((9 * PLANES, 128), F32)],
+        (first_tile, got, place, inv, depth, cot),
+        [vmem(16, TILES * SLOTS), big, big, big, vmem(16, TILES * SLOTS)],
+        [SMEM] + [VMEM] * 5,
     )
 
 
-def collect(back, ids, camera):
-    return call(collect_kernel, [((40 * VIEWS, 128), F32)], (back, ids, camera))[0]
-
-
-def pull_back(everything, attributes):
+def collect(back, asked, camera):
+    return call(collect_kernel, [((32 * 40, 128), F32)], (back, asked, camera))[0]
+
+
+def pull_back(parts, attributes):
     return call(
-        pull_kernel, [((ATTR, G_DEV), F32)], (everything, attributes), [(ATTR * 8, 128), (ATTR * 4, 128)]
+        pull_kernel,
+        [((ATTR, G_DEV), F32)],
+        (parts, attributes),
+        [vmem(ATTR * 8, 128), vmem(ATTR * 4, 128), vmem(40 * VIEWS, 128)],
     )[0]
 
 
-def exchange(x, axis="dev"):
-    return lax.all_to_all(x, axis, split_axis=0, concat_axis=0, tiled=True)
+def exchange(x, axis, groups):
+    return lax.all_to_all(x, axis, split_axis=0, concat_axis=0, tiled=True, axis_index_groups=groups)
+
+
+ACROSS = [[8 * z + r for z in range(PLANES)] for r in range(8)]
+WITHIN = [[8 * z + r for r in range(8)] for z in range(PLANES)]
+VIEWS_WITHIN = [[OWNERS * v + d for v in range(VIEWS) for d in group] for group in WITHIN]
 
 
 def per_device(attributes, camera, list_owner, list_local, term_depth, image_cot):
     owner = list_owner.reshape(1, -1)
-    asked, rank, inv, rows = route(owner, list_local[0], attributes, camera)
-    asked = exchange(asked.reshape(OWNERS, 1, 128)).reshape(OWNERS, 128)
-    sent, ids = serve(asked, rows)
-    got = exchange(sent.reshape(OWNERS, 2, 128)).reshape(2 * OWNERS, 128)
+    asked, inv, place, rows = route(owner, list_local[0], attributes, camera)
+    asked = exchange(asked.reshape(PLANES, 1, 128), "dev", ACROSS).reshape(PLANES, 128)
+    rows = lax.all_gather(rows, "dev", axis_index_groups=WITHIN, tiled=True)
+    sent = serve(asked, rows)
+    got = exchange(sent.reshape(PLANES, 1, 1152), "dev", ACROSS).reshape(9 * PLANES, 128)
     first_tile = (lax.axis_index("dev") * TILES).astype(I32).reshape(1)
-    image, grads = composite(first_tile, got, owner, rank, inv, term_depth[0], image_cot[0])
-    back = exchange(grads.reshape(OWNERS, 2, 128)).reshape(2 * OWNERS, 128)
-    mine = collect(back, ids, camera)
-    everything = exchange(mine.reshape(VIEWS, 40, 128), "view").reshape(VIEWS * 40, 128)
-    return image[None], pull_back(everything, attributes)
+    image, grads = composite(first_tile, got, place, inv, term_depth[0], image_cot[0])
+    back = exchange(grads.reshape(PLANES, 1, 1152), "dev", ACROSS).reshape(9 * PLANES, 128)
+    mine = collect(back, asked, camera)
+    parts = exchange(mine.reshape(32, 40, 128), ("view", "dev"), VIEWS_WITHIN).reshape(32 * 40, 128)
+    return image[None], pull_back(parts, attributes)
 
 
 def solution(mesh):

time: 102 us -> 103 us (level)
  starting transfers between devices: 5.8 us -> 27.6 us
  blocking collectives: 67.2 us -> 51.1 us
  waiting for transfers between devices: 16.1 us -> 11.8 us
  local copies, waits for them, and re-layouts: 3.65 us -> 1.36 us
  Pallas kernels: 7.8 us -> 9.65 us
    all_to_all x3 -> x2, blocking collectives: 67.2 us -> 37.1 us  [exchange(): lax.all_to_all(x, axis, split_axis=0, concat_axis=0, tiled=True, axis_ind...]
    all_to_all x1 -> x2, starting transfers between devices: 5.8 us -> 27.6 us  [exchange(): lax.all_to_all(x, axis, split_axis=0, concat_axis=0, tiled=True, axis_ind...]
    all_gather x0 -> x1, blocking collectives: none -> 14.1 us  [per_device(): rows = lax.all_gather(rows, 'dev', axis_index_groups=WITHIN, tiled=True)]
    all_to_all x1 -> x2, waiting for transfers between devices: 16.1 us -> 11.8 us  [exchange(): lax.all_to_all(x, axis, split_axis=0, concat_axis=0, tiled=True, axis_ind...]
    unnamed x16 -> x14, local copies, waits for them, and re-layouts: 3.65 us -> 1.36 us
    pallas_call x5, Pallas kernels: 7.8 us -> 9.65 us  [call(): pl.pallas_call(kernel, out_shape=[jax.ShapeDtypeStruct(s, d) for s, d in...]
  transfers between devices with their start and end apart: 1 -> 2, of which waited for: 1 -> 1; matrix products, arithmetic and copies ran while one was open for 0% -> 0% of each run, Pallas kernels for 0% -> 0%
where the time goes in v2:
time: 103 us; the launch traced here: 102 us
  blocking collectives  51.1 us (50%)
  starting transfers between devices  27.6 us (27%)
  waiting for transfers between devices  11.8 us (11%)
  Pallas kernels  9.65 us (9%)
  local copies, waits for them, and re-layouts  1.36 us (1%)
    all_to_all x2, blocking collectives, exchange(): lax.all_to_all(x, axis, split_axis=0, concat_axis=0, tiled=True, axis_ind...  37.1 us
    all_to_all x2, starting transfers between devices, exchange(): lax.all_to_all(x, axis, split_axis=0, concat_axis=0, tiled=True, axis_ind...  27.6 us
    all_gather x1, blocking collectives, per_device(): rows = lax.all_gather(rows, 'dev', axis_index_groups=WITHIN, tiled=True)  14.1 us
    all_to_all x2, waiting for transfers between devices, exchange(): lax.all_to_all(x, axis, split_axis=0, concat_axis=0, tiled=True, axis_ind...  11.8 us
    pallas_call x5, Pallas kernels, call(): pl.pallas_call(kernel, out_shape=[jax.ShapeDtypeStruct(s, d) for s, d in...  9.65 us
  transfers between devices with their start and end apart: 2, of which 1 were waited for; matrix products, arithmetic and copies ran while one was open for 0% of the time, Pallas kernels for 0%

profile of v2, /device:TPU:1, one launch (start us, length us, event | category | flops | bytes accessed | tf_op | source)
XLA Modules:
  0.0 102.3 jit_solution(11206946766860680653)
XLA Ops:
  0.6 2.0 %shard_map.77 = (f32[16,128]{1,0:T(8,128)}, s32[16,128]{1,0:T(8,128)}, s32[8,1024]{1,0:T(8,128)}, f32[40,128]{1,0:T(8,128)}) custom-call(s32[1,1024]{1,0:T(1,128)} %bitcast.26, s32[4,256]{1,0:T(4,128)} %bitcast.27, f32[59,512]{1,0:T(8,128)} %attr_ref.1, f32[1,6]{1,0:T(1,128)} %cam_ref.1), custom_call_target="tpu_custom_call" | custom-call | tf_op jit(solution)/shard_map/pallas_call | solution.py:464
  2.7 0.0 copy-start.6
  2.7 15.8 %all-to-all-start = ((f32[16,1,128]{2,1,0:T(1,128)}), f32[16,1,128]{2,1,0:T(1,128)S(1)}, u32[]{:S(2)}, u32[]{:S(2)}) async-start(f32[16,1,128]{2,1,0:T(1,128)} %bitcast.25), calls=%async_computation | async-start | bytes 16384 | tf_op jit(solution)/shard_map/all_to_all | solution.py:521
  18.5 0.0 copy-done.6
  18.5 14.1 %all_gather.3.rows_ref = f32[320,128]{1,0:T(8,128)S(1)} all-gather(f32[40,128]{1,0:T(8,128)S(1)} %copy-done.6), channel_id=1, replica_groups={{0,1,2,3,4,5,6,7},{8,9,10,11,12,13,14,15},{16,17,18,19,20,21,22,23},{24..., dimensions={0}, use_global_device_ids=true | all-gather | bytes 184320 | tf_op jit(solution)/shard_map/all_gather | solution.py:533
  32.6 0.0 all-to-all-done
  32.6 1.3 %shard_map.78 = f32[144,128]{1,0:T(8,128)} custom-call(f32[16,128]{1,0:T(8,128)S(1)} %bitcast.20, f32[320,128]{1,0:T(8,128)S(1)} %all_gather.3.rows_ref), custom_call_target="tpu_custom_call" | custom-call | tf_op jit(solution)/shard_map/pallas_call | solution.py:464
  33.9 0.0 copy-start.1
  33.9 0.0 copy-start.3
  33.9 11.9 %all-to-all-start.1 = ((f32[16,1,1152]{2,1,0:T(1,128)}), f32[16,1,1152]{2,1,0:T(1,128)S(1)}, u32[]{:S(2)}, u32[]{:S(2)}) async-start(f32[16,1,1152]{2,1,0:T(1,128)} %bitcast.6), calls=%async_computation.1 | async-start | bytes 147456 | tf_op jit(solution)/shard_map/all_to_all | solution.py:521
  45.8 0.0 copy-start.2
  45.8 11.8 %all-to-all-done.1 = f32[16,1,1152]{2,1,0:T(1,128)S(1)} async-done(((f32[16,1,1152]{2,1,0:T(1,128)}), f32[16,1,1152]{2,1,0:T(1,128)S(1)}, u32[]{:S(2)}, u32[]{:S(2)}) %all-to-all-start.1) | async-done | bytes 73760 | tf_op jit(solution)/shard_map/all_to_all | solution.py:521
  57.6 0.0 copy-start.4
  57.6 0.0 copy-done.1
  57.6 0.0 copy-done.3
  57.6 0.0 copy-done.2
  57.6 0.7 copy-done.4
  58.3 4.3 %shard_map.79 = (f32[3,4,256]{2,1,0:T(4,128)}, f32[144,128]{1,0:T(8,128)S(1)}) custom-call(s32[1]{0:T(128)} %bitcast.tile_ref, f32[144,128]{1,0:T(8,128)S(1)} %bitcast.19, s32[8,1024]{1,0:T(8,128)S(1)} %copy-done.1, s32[16,128]{1,0:T(8,128)S(1)} %copy-done.3, s32[4,256]{1,0:T(4,128)S(1)} %bitcast.24, f32[3,4,256]{2,1,0:T(4,128)S(1)} %bitcast.23), custom_call_target="tpu_custom_call" | custom-call | tf_op jit(solution)/shard_map/pallas_call | solution.py:464
  62.6 15.6 %all_to_all.20 = f32[16,1,1152]{2,1,0:T(1,128)S(1)} all-to-all(f32[16,1,1152]{2,1,0:T(1,128)S(1)} %bitcast.22), channel_id=1, replica_groups={{0,8,16,24,32,40,48,56,64,72,80,88,96,104,112,120},{1,9,17,25,33,41,49,..., dimensions={0} | all-to-all | bytes 147456 | tf_op jit(solution)/shard_map/all_to_all | solution.py:521
  78.2 0.0 copy-start.5
  78.2 0.7 copy-done.5
  78.8 0.8 shard_map.80
  79.7 0.0 copy-start
  79.7 21.5 %all_to_all.21 = f32[32,40,128]{2,1,0:T(8,128)S(1)} all-to-all(f32[32,40,128]{2,1,0:T(8,128)S(1)} %bitcast.16), channel_id=1, replica_groups={{0,1,2,3,4,5,6,7,128,129,130,131,132,133,134,135,256,257,258,259,260,26..., dimensions={0} | all-to-all | bytes 1310720 | tf_op jit(solution)/shard_map/all_to_all | solution.py:521
  101.2 0.0 copy-done
  101.2 1.1 %shard_map.81 = f32[59,512]{1,0:T(8,128)} custom-call(f32[1280,128]{1,0:T(8,128)S(1)} %bitcast.17, f32[59,512]{1,0:T(8,128)S(1)} %copy-done), custom_call_target="tpu_custom_call" | custom-call | tf_op jit(solution)/shard_map/pallas_call | solution.py:464
Async XLA Ops:
  2.7 15.8 %copy-start.6 = (f32[40,128]{1,0:T(8,128)S(1)}, f32[40,128]{1,0:T(8,128)}, u32[]{:S(2)}) copy-start(f32[40,128]{1,0:T(8,128)} %get-tuple-element.9) | copy-start | bytes 61444
  2.7 29.9 %all-to-all-start = ((f32[16,1,128]{2,1,0:T(1,128)}), f32[16,1,128]{2,1,0:T(1,128)S(1)}, u32[]{:S(2)}, u32[]{:S(2)}) async-start(f32[16,1,128]{2,1,0:T(1,128)} %bitcast.25), calls=%async_computation | async-start | bytes 16384 | tf_op jit(solution)/shard_map/all_to_all | solution.py:521
  33.9 23.7 %copy-start.1 = (s32[8,1024]{1,0:T(8,128)S(1)}, s32[8,1024]{1,0:T(8,128)}, u32[]{:S(2)}) copy-start(s32[8,1024]{1,0:T(8,128)} %get-tuple-element.10.place_ref) | copy-start | bytes 98308
  33.9 23.7 %copy-start.3 = (s32[16,128]{1,0:T(8,128)S(1)}, s32[16,128]{1,0:T(8,128)}, u32[]{:S(2)}) copy-start(s32[16,128]{1,0:T(8,128)} %get-tuple-element.11.inv_ref) | copy-start | bytes 24580
  33.9 23.7 %all-to-all-start.1 = ((f32[16,1,1152]{2,1,0:T(1,128)}), f32[16,1,1152]{2,1,0:T(1,128)S(1)}, u32[]{:S(2)}, u32[]{:S(2)}) async-start(f32[16,1,1152]{2,1,0:T(1,128)} %bitcast.6), calls=%async_computation.1 | async-start | bytes 147456 | tf_op jit(solution)/shard_map/all_to_all | solution.py:521
  45.8 11.9 %copy-start.2 = (f32[1,3,4,256]{3,2,1,0:T(4,128)S(1)}, f32[1,3,4,256]{3,2,1,0:T(4,128)}, u32[]{:S(2)}) copy-start(f32[1,3,4,256]{3,2,1,0:T(4,128)} %param.11) | copy-start | bytes 36868
  57.6 0.7 copy-start.4
  78.2 0.7 copy-start.5
  79.7 21.5 %copy-start = (f32[59,512]{1,0:T(8,128)S(1)}, f32[59,512]{1,0:T(8,128)}, u32[]{:S(2)}) copy-start(f32[59,512]{1,0:T(8,128)} %attr_ref.1) | copy-start | bytes 362500

commit v3 on v2

--- a/solution.py
+++ b/solution.py
@@ -10,7 +10,8 @@
 SLOTS = 256
 CAP = 16
 OWNERS = 128
-PLANES = 16
+PEERS = 32
+NEAR = 4
 G_DEV = 512
 ATTR = 59
 VIEWS = 4
@@ -150,7 +151,7 @@
 
 
 def route_kernel(
-    owner_hbm, local_hbm, attr_hbm, cam_hbm, asked_ref, inv_ref, place_ref, rows_ref,
+    tile_ref, owner_hbm, local_hbm, attr_hbm, cam_hbm, asked_ref, inv_ref, place_ref, rows_ref,
     owner_ref, local_ref, attr_ref, cam_ref, wide_ref, sem,
 ):
     pairs = [(owner_hbm, owner_ref), (local_hbm, local_ref), (attr_hbm, attr_ref), (cam_hbm, cam_ref)]
@@ -162,10 +163,10 @@
     ).astype(F32).astype(BF16)
     every = jnp.ones((SLOTS, SLOTS), BF16)
     oid = lax.broadcasted_iota(I32, (OWNERS, SLOTS), 0)
-    zid = lax.broadcasted_iota(I32, (PLANES, SLOTS), 0)
+    pid = lax.broadcasted_iota(I32, (PEERS, SLOTS), 0)
     lane = lax.broadcasted_iota(I32, (1, SLOTS), 1)
     base = jnp.zeros((OWNERS, SLOTS), F32)
-    table = jnp.zeros((4 * PLANES, 128), F32)
+    table = jnp.zeros((4 * PEERS, 128), F32)
     copies[0].wait()
     copies[1].wait()
     for t in range(TILES):
@@ -175,18 +176,19 @@
         count = dot(hot16, before, 1, 0) + base
         base = base + dot(hot16, every, 1, 0)
         rank = jnp.sum(hot * count, axis=0, keepdims=True).astype(I32)
-        plane = owner >> 3
-        lanes = (owner & 7) * CAP + rank
-        place_ref[0:1, SLOTS * t : SLOTS * (t + 1)] = plane
+        peer = (owner >> 3) * 2 + (owner & 1)
+        lanes = ((owner >> 1) & 3) * CAP + rank
+        place_ref[0:1, SLOTS * t : SLOTS * (t + 1)] = peer
         place_ref[1:2, SLOTS * t : SLOTS * (t + 1)] = lanes
-        hot_plane = (zid == plane).astype(F32)
-        hot_lane = (oid == lanes).astype(F32).astype(BF16)
+        hot_peer = (pid == peer).astype(F32)
+        hot_lane = ((oid & 63) == lanes).astype(F32).astype(BF16)
         local = local_ref[t : t + 1, :]
         slot = lane + (SLOTS * t + 1)
         parts = [local & 255, local >> 8, slot & 255, slot >> 8]
-        vals = jnp.concatenate([hot_plane * p.astype(F32) for p in parts], axis=0).astype(BF16)
+        vals = jnp.concatenate([hot_peer * p.astype(F32) for p in parts], axis=0).astype(BF16)
         table = table + dot(vals, hot_lane, 1, 1)
-    n = PLANES
+    place_ref[2:3, :] = jnp.full((1, TILES * SLOTS), tile_ref[0], I32)
+    n = PEERS
     asked_ref[...] = table[0:n] + 256.0 * table[n : 2 * n]
     inv_ref[...] = (table[2 * n : 3 * n] + 256.0 * table[3 * n :]).astype(I32)
     copies[2].wait()
@@ -203,48 +205,69 @@
     rows_ref[36:40, :] = jnp.zeros((4, 128), F32)
 
 
-def serve_kernel(asked_ref, rows_ref, out_ref):
+def serve_kernel(asked_ref, rows_ref, *refs):
+    kept, (out_ref, *outs) = refs[:5], refs[5:]
+    for src, dst in zip(kept, outs):
+        dst[...] = src[...]
+    blank = jnp.zeros((4, 128), F32)
     table = []
     for j in range(4):
-        part = [rows_ref[40 * r + 8 * j : 40 * r + 8 * j + 8, :] for r in range(8)]
-        part.append(rows_ref[pl.ds(32 + j, 8, stride=40), :])
+        part = [rows_ref[40 * r + 8 * j : 40 * r + 8 * j + 8, :] for r in range(NEAR)]
+        part += [rows_ref[pl.ds(32 + j, NEAR, stride=40), :], blank]
         table.append(jnp.concatenate(part, axis=0))
     table = [x.astype(F32) for x in split3(jnp.concatenate(table, axis=1))]
     table = jnp.concatenate(table + [jnp.zeros((8, G_DEV), F32)], axis=0).astype(BF16)
     lid = lax.broadcasted_iota(I32, (G_DEV, 256), 0)
     sub = lax.broadcasted_iota(I32, (8, 128), 0)
-    near = lax.broadcasted_iota(I32, (8, 128), 1) >> 4
-    for z in range(0, PLANES, 2):
-        ids = jnp.concatenate([asked_ref[z : z + 1, :], asked_ref[z + 1 : z + 2, :]], axis=1).astype(I32)
-        hot = (lid == ids).astype(F32).astype(BF16)
+    lane = lax.broadcasted_iota(I32, (8, 128), 1)
+    near, left = (lane & 63) >> 4, lane < 64
+    for n in range(0, PEERS, 4):
+        hot = (lid == pair_ids(asked_ref, n)).astype(F32).astype(BF16)
         got = dot(table, hot, 1, 0)
-        got = got[0:72] + got[72:144] + got[144:216]
+        got = got[0:40] + got[40:80] + got[80:120]
         for i in range(2):
             half = got[:, 128 * i : 128 * (i + 1)]
             main = half[0:8]
-            for r in range(1, 8):
+            for r in range(1, NEAR):
                 main = jnp.where(near == r, half[8 * r : 8 * (r + 1)], main)
-            out_ref[9 * (z + i) : 9 * (z + i) + 8, :] = main
-            last = jnp.sum(jnp.where(near == sub, half[64:72], 0.0), axis=0, keepdims=True)
-            out_ref[9 * (z + i) + 8 : 9 * (z + i) + 9, :] = last
+            turned = pltpu.roll(main, 64, 1)
+            last = jnp.sum(jnp.where(near == sub, half[32:40], 0.0), axis=0, keepdims=True)
+            at = 5 * (n + 2 * i)
+            out_ref[at : at + 4, :] = jnp.where(left[0:4], main[0:4], turned[4:8])
+            out_ref[at + 4 : at + 5, :] = last
+            out_ref[at + 5 : at + 9, :] = jnp.where(left[0:4], turned[0:4], main[4:8])
+            out_ref[at + 9 : at + 10, :] = pltpu.roll(jnp.broadcast_to(last, (8, 128)), 64, 1)[0:1]
+
+
+def pair_ids(asked_ref, n):
+    left = lax.broadcasted_iota(I32, (1, 128), 1) < 64
+    rows = [asked_ref[n + i : n + i + 1, :] for i in range(4)]
+    pairs = [jnp.where(left, rows[0], rows[1]), jnp.where(left, rows[2], rows[3])]
+    return jnp.concatenate(pairs, axis=1).astype(I32)
 
 
 def composite_kernel(
-    tile_ref, got_ref, place_ref, inv_ref, depth_ref, cot_ref, image_ref, out_ref,
+    got_ref, place_ref, inv_ref, depth_ref, cot_ref, image_ref, out_ref,
     par_ref, alpha_ref, pull_ref, weight_ref, grad_ref,
 ):
-    last = got_ref[pl.ds(8, PLANES, stride=9), :]
+    last = got_ref[pl.ds(4, PEERS, stride=5), :]
     sub = lax.broadcasted_iota(I32, (8, 128), 0)
+    tables = []
+    for n in range(PEERS):
+        rows = got_ref[5 * n : 5 * n + 4, :]
+        tables.append(jnp.concatenate([rows, rows], axis=0))
     for b in range(8):
-        plane = jnp.broadcast_to(place_ref[0:1, 128 * b : 128 * (b + 1)], (8, 128))
+        peer = jnp.broadcast_to(place_ref[0:1, 128 * b : 128 * (b + 1)], (8, 128))
         lanes = jnp.broadcast_to(place_ref[1:2, 128 * b : 128 * (b + 1)], (8, 128))
-        got = lane_gather(got_ref[0:8, :], lanes)
-        for z in range(1, PLANES):
-            got = jnp.where(plane == z, lane_gather(got_ref[9 * z : 9 * z + 8, :], lanes), got)
+        both = jnp.where(sub < 4, lanes, lanes + 64)
+        got = lane_gather(tables[0], both)
+        for n in range(1, PEERS):
+            got = jnp.where(peer == n, lane_gather(tables[n], both), got)
         par_ref[0:8, 128 * b : 128 * (b + 1)] = got
-        low = jnp.where(plane == sub, lane_gather(last[0:8], lanes), 0.0)
-        high = jnp.where(plane == sub + 8, lane_gather(last[8:16], lanes), 0.0)
-        par_ref[8:9, 128 * b : 128 * (b + 1)] = jnp.sum(low + high, axis=0, keepdims=True)
+        final = jnp.zeros((8, 128), F32)
+        for n in range(0, PEERS, 8):
+            final = final + jnp.where(peer == sub + n, lane_gather(last[n : n + 8], lanes), 0.0)
+        par_ref[8:9, 128 * b : 128 * (b + 1)] = jnp.sum(final, axis=0, keepdims=True)
 
     q = lax.broadcasted_iota(I32, (16, 128), 1)
     row16 = lax.broadcasted_iota(I32, (16, 128), 0)
@@ -266,8 +289,8 @@
     for t in range(TILES):
         par = [par_ref[c : c + 1, SLOTS * t : SLOTS * (t + 1)] for c in range(9)]
         u, w, ca, cb, cc, log_op = par[:6]
-        tile = tile_ref[0] + t
-        cx = ((tile % TILE_COLS) * 16 + 8).astype(F32) * ex - 0.5
+        tile = place_ref[2:3, 0:SLOTS] + t
+        cx = ((tile & (TILE_COLS - 1)) * 16 + 8).astype(F32) * ex - 0.5
         dx0 = cx - u
         A, B, C = -0.5 * LOG2E * ca, -LOG2E * cb, -0.5 * LOG2E * cc
         colors = jnp.concatenate([par[6], par[7], par[8], zero5], axis=0)
@@ -275,7 +298,7 @@
         dy0s = []
         for h in range(2):
             th = 4 * h + t
-            cy = ((tile // TILE_COLS) * 16 + 8 * h + 4).astype(F32) * ey - 0.5
+            cy = ((tile >> 4) * 16 + 8 * h + 4).astype(F32) * ey - 0.5
             dy0 = cy - w
             dy0s.append(dy0)
             coef = jnp.concatenate(
@@ -383,46 +406,55 @@
 
     tables = [grad_ref[0:8, 128 * j : 128 * (j + 1)] for j in range(8)]
     last = [jnp.broadcast_to(grad_ref[8:9, 128 * j : 128 * (j + 1)], (8, 128)) for j in range(8)]
-    for z in range(PLANES):
-        out_ref[9 * z : 9 * z + 8, :] = pick(tables, jnp.broadcast_to(inv[z : z + 1], (8, 128)))
-    more = jnp.concatenate([pick(last, inv[0:8]), pick(last, inv[8:16])], axis=0)
-    out_ref[pl.ds(8, PLANES, stride=9), :] = more
+    left = lax.broadcasted_iota(I32, (4, 128), 1) < 64
+    for n in range(PEERS):
+        got = pick(tables, jnp.broadcast_to(inv[n : n + 1], (8, 128)))
+        out_ref[5 * n : 5 * n + 4, :] = jnp.where(left, got[0:4], got[4:8])
+    more = [pick(last, inv[n : n + 8]) for n in range(0, PEERS, 8)]
+    out_ref[pl.ds(4, PEERS, stride=5), :] = jnp.concatenate(more, axis=0)
 
 
 def collect_kernel(back_ref, asked_ref, cam_ref, out_ref):
     lid = lax.broadcasted_iota(I32, (G_DEV, 256), 0)
     sub = lax.broadcasted_iota(I32, (8, 128), 0)
-    near = lax.broadcasted_iota(I32, (8, 128), 1) >> 4
-    acc = jnp.zeros((144, G_DEV), F32)
-    for z in range(0, PLANES, 2):
-        ids = jnp.concatenate([asked_ref[z : z + 1, :], asked_ref[z + 1 : z + 2, :]], axis=1).astype(I32)
-        hot = (lid == ids).astype(F32).astype(BF16)
-        left = []
+    lane = lax.broadcasted_iota(I32, (8, 128), 1)
+    near, left = (lane & 63) >> 4, lane < 64
+    acc = jnp.zeros((80, G_DEV), F32)
+    for n in range(0, PEERS, 4):
+        hot = (lid == pair_ids(asked_ref, n)).astype(F32).astype(BF16)
+        pairs = []
         for i in range(2):
-            at = 9 * (z + i)
-            main = [x.astype(F32) for x in split2(back_ref[at : at + 8, :])]
-            last = [x.astype(F32) for x in split2(jnp.broadcast_to(back_ref[at + 8 : at + 9, :], (8, 128)))]
+            at = 5 * (n + 2 * i)
+            one = jnp.concatenate([back_ref[at : at + 4, :]] * 2, axis=0)
+            two = jnp.concatenate([back_ref[at + 5 : at + 9, :]] * 2, axis=0)
+            other = jnp.where(left, pltpu.roll(one, 64, 1), two)
+            straight = jnp.where(left, one, pltpu.roll(two, 64, 1))
+            main = jnp.where(sub < 4, straight, other)
+            last_one = jnp.broadcast_to(back_ref[at + 4 : at + 5, :], (8, 128))
+            last_two = jnp.broadcast_to(back_ref[at + 9 : at + 10, :], (8, 128))
+            last = jnp.where(left, last_one, pltpu.roll(last_two, 64, 1))
             rows = []
-            for m, l in zip(main, last):
-                rows += [jnp.where(near == r, m, 0.0) for r in range(8)] + [jnp.where(near == sub, l, 0.0)]
-            left.append(jnp.concatenate(rows, axis=0).astype(BF16))
-        acc = acc + dot(jnp.concatenate(left, axis=1), hot, 1, 1)
-    rows = acc[0:72] + acc[72:144]
+            for m, l in zip(split2(main), split2(last)):
+                m, l = m.astype(F32), l.astype(F32)
+                rows += [jnp.where(near == r, m, 0.0) for r in range(NEAR)] + [jnp.where(near == sub, l, 0.0)]
+            pairs.append(jnp.concatenate(rows, axis=0).astype(BF16))
+        acc = acc + dot(jnp.concatenate(pairs, axis=1), hot, 1, 1)
+    rows = acc[0:40] + acc[40:80]
     cam = jnp.concatenate([cam_ref[...], jnp.zeros((1, 122), F32)], axis=1)
     tail = jnp.concatenate([cam, jnp.zeros((3, 128), F32)], axis=0)
-    for r in range(8):
+    for r in range(NEAR):
         part = [rows[8 * r : 8 * r + 8, 128 * j : 128 * (j + 1)] for j in range(4)]
-        part += [rows[64 + r : 65 + r, 128 * j : 128 * (j + 1)] for j in range(4)] + [tail]
+        part += [rows[32 + r : 33 + r, 128 * j : 128 * (j + 1)] for j in range(4)] + [tail]
         part = jnp.concatenate(part, axis=0)
         for v in range(VIEWS):
-            out_ref[40 * (8 * v + r) : 40 * (8 * v + r + 1), :] = part
+            out_ref[40 * (NEAR * v + r) : 40 * (NEAR * v + r + 1), :] = part
 
 
 def pull_kernel(parts_ref, attr_ref, out_ref, wide_ref, res_ref, all_ref):
     for v in range(VIEWS):
-        start = 320 * v
+        start = 40 * NEAR * v
         total = parts_ref[start : start + 36, :]
-        for r in range(1, 8):
+        for r in range(1, NEAR):
             total = total + parts_ref[start + 40 * r : start + 40 * r + 36, :]
         all_ref[40 * v : 40 * v + 36, :] = total
         all_ref[40 * v + 36 : 40 * v + 40, :] = parts_ref[start + 36 : start + 40, :]
@@ -475,37 +507,37 @@
     return pltpu.VMEM(shape, dtype)
 
 
-def route(owner, local, attributes, camera):
+def route(first_tile, owner, local, attributes, camera):
     return call(
         route_kernel,
-        [((PLANES, 128), F32), ((PLANES, 128), I32), ((8, TILES * SLOTS), I32), ((40, 128), F32)],
-        (owner, local, attributes, camera),
+        [((PEERS, 128), F32), ((PEERS, 128), I32), ((8, TILES * SLOTS), I32), ((40, 128), F32)],
+        (first_tile, owner, local, attributes, camera),
         [
             vmem(1, TILES * SLOTS, dtype=I32), vmem(TILES, SLOTS, dtype=I32), vmem(ATTR, G_DEV), vmem(1, 6),
             vmem(ATTR * 8, 128), pltpu.SemaphoreType.DMA((4,)),
         ],
-        [HBM] * 4,
+        [SMEM] + [HBM] * 4,
         60,
     )
 
 
-def serve(asked, rows):
-    return call(serve_kernel, [((9 * PLANES, 128), F32)], (asked, rows))[0]
-
-
-def composite(first_tile, got, place, inv, depth, cot):
+def serve(asked, rows, *kept):
+    outs = [((5 * PEERS, 128), F32)] + [(k.shape, k.dtype) for k in kept]
+    return call(serve_kernel, outs, (asked, rows, *kept))
+
+
+def composite(got, place, inv, depth, cot):
     big = vmem(SLOTS * 8, 128)
     return call(
         composite_kernel,
-        [((3, TILES, 256), F32), ((9 * PLANES, 128), F32)],
-        (first_tile, got, place, inv, depth, cot),
+        [((3, TILES, 256), F32), ((5 * PEERS, 128), F32)],
+        (got, place, inv, depth, cot),
         [vmem(16, TILES * SLOTS), big, big, big, vmem(16, TILES * SLOTS)],
-        [SMEM] + [VMEM] * 5,
     )
 
 
 def collect(back, asked, camera):
-    return call(collect_kernel, [((32 * 40, 128), F32)], (back, asked, camera))[0]
+    return call(collect_kernel, [((VIEWS * NEAR * 40, 128), F32)], (back, asked, camera))[0]
 
 
 def pull_back(parts, attributes):
@@ -521,24 +553,24 @@
     return lax.all_to_all(x, axis, split_axis=0, concat_axis=0, tiled=True, axis_index_groups=groups)
 
 
-ACROSS = [[8 * z + r for z in range(PLANES)] for r in range(8)]
-WITHIN = [[8 * z + r for r in range(8)] for z in range(PLANES)]
+ACROSS = [[8 * z + 2 * y + c for z in range(16) for c in range(2)] for y in range(NEAR)]
+WITHIN = [[8 * z + 2 * y + c for y in range(NEAR)] for z in range(16) for c in range(2)]
 VIEWS_WITHIN = [[OWNERS * v + d for v in range(VIEWS) for d in group] for group in WITHIN]
 
 
 def per_device(attributes, camera, list_owner, list_local, term_depth, image_cot):
     owner = list_owner.reshape(1, -1)
-    asked, inv, place, rows = route(owner, list_local[0], attributes, camera)
-    asked = exchange(asked.reshape(PLANES, 1, 128), "dev", ACROSS).reshape(PLANES, 128)
+    first_tile = (lax.axis_index("dev") * TILES).astype(I32).reshape(1)
+    asked, inv, place, rows = route(first_tile, owner, list_local[0], attributes, camera)
+    asked = exchange(asked.reshape(PEERS, 1, 128), "dev", ACROSS).reshape(PEERS, 128)
     rows = lax.all_gather(rows, "dev", axis_index_groups=WITHIN, tiled=True)
-    sent = serve(asked, rows)
-    got = exchange(sent.reshape(PLANES, 1, 1152), "dev", ACROSS).reshape(9 * PLANES, 128)
-    first_tile = (lax.axis_index("dev") * TILES).astype(I32).reshape(1)
-    image, grads = composite(first_tile, got, place, inv, term_depth[0], image_cot[0])
-    back = exchange(grads.reshape(PLANES, 1, 1152), "dev", ACROSS).reshape(9 * PLANES, 128)
+    sent, place, inv, depth, cot, camera = serve(asked, rows, place, inv, term_depth[0], image_cot[0], camera)
+    got = exchange(sent.reshape(PEERS, 1, 640), "dev", ACROSS).reshape(5 * PEERS, 128)
+    image, grads = composite(got, place, inv, depth, cot)
+    back = exchange(grads.reshape(PEERS, 1, 640), "dev", ACROSS).reshape(5 * PEERS, 128)
     mine = collect(back, asked, camera)
-    parts = exchange(mine.reshape(32, 40, 128), ("view", "dev"), VIEWS_WITHIN).reshape(32 * 40, 128)
-    return image[None], pull_back(parts, attributes)
+    parts = exchange(mine.reshape(VIEWS * NEAR, 40, 128), ("view", "dev"), VIEWS_WITHIN)
+    return image[None], pull_back(parts.reshape(VIEWS * NEAR * 40, 128), attributes)
 
 
 def solution(mesh):

time: 103 us -> 97.8 us (0.950)
  blocking collectives: 51.1 us -> 68.8 us
  starting transfers between devices: 27.6 us -> 16.8 us
  waiting for transfers between devices: 11.8 us -> 1.17 us
    all_to_all x2 -> x3, blocking collectives: 37.1 us -> 58.2 us  [exchange(): lax.all_to_all(x, axis, split_axis=0, concat_axis=0, tiled=True, axis_ind...]
    all_to_all x2 -> x1, starting transfers between devices: 27.6 us -> 16.8 us  [exchange(): lax.all_to_all(x, axis, split_axis=0, concat_axis=0, tiled=True, axis_ind...]
    all_to_all x2 -> x1, waiting for transfers between devices: 11.8 us -> 1.17 us  [exchange(): lax.all_to_all(x, axis, split_axis=0, concat_axis=0, tiled=True, axis_ind...]
    all_gather x1, blocking collectives: 14.1 us -> 10.5 us  [per_device(): rows = lax.all_gather(rows, 'dev', axis_index_groups=WITHIN, tiled=True)]
  transfers between devices with their start and end apart: 2 -> 1, of which waited for: 1 -> 1; matrix products, arithmetic and copies ran while one was open for 0% -> 0% of each run, Pallas kernels for 0% -> 0%
where the time goes in v3:
time: 97.8 us; the launch traced here: 97 us
  blocking collectives  68.8 us (70%)
  starting transfers between devices  16.8 us (17%)
  Pallas kernels  8.92 us (9%)
  waiting for transfers between devices  1.17 us (1%)
    all_to_all x3, blocking collectives, exchange(): lax.all_to_all(x, axis, split_axis=0, concat_axis=0, tiled=True, axis_ind...  58.2 us
    all_to_all x1, starting transfers between devices, exchange(): lax.all_to_all(x, axis, split_axis=0, concat_axis=0, tiled=True, axis_ind...  16.8 us
    all_gather x1, blocking collectives, per_device(): rows = lax.all_gather(rows, 'dev', axis_index_groups=WITHIN, tiled=True)  10.5 us
    pallas_call x5, Pallas kernels, call(): pl.pallas_call(kernel, out_shape=[jax.ShapeDtypeStruct(s, d) for s, d in...  8.92 us
  transfers between devices with their start and end apart: 1, of which 1 were waited for; matrix products, arithmetic and copies ran while one was open for 0% of the time, Pallas kernels for 0%

profile of v3, /device:TPU:1, one launch (start us, length us, event | category | flops | bytes accessed | tf_op | source)
XLA Modules:
  0.0 97.0 jit_solution(7507140855874013312)
XLA Ops:
  0.6 2.1 %shard_map.77 = (f32[32,128]{1,0:T(8,128)}, s32[32,128]{1,0:T(8,128)}, s32[8,1024]{1,0:T(8,128)}, f32[40,128]{1,0:T(8,128)}) custom-call(s32[1]{0:T(128)} %bitcast.tile_ref, s32[1,1024]{1,0:T(1,128)} %bitcast.27, s32[4,256]{1,0:T(4,128)} %bitcast.28, f32[59,512]{1,0:T(8,128)} %attr_ref.1, f32[1,6]{1,0:T(1,128)} %refs_4_.1), custom_call_target="tpu_custom_call" | custom-call | tf_op jit(solution)/shard_map/pallas_call | solution.py:496
  2.7 0.0 copy-start.6
  2.7 16.8 %all-to-all-start = ((f32[32,1,128]{2,1,0:T(1,128)}), f32[32,1,128]{2,1,0:T(1,128)S(1)}, u32[]{:S(2)}, u32[]{:S(2)}) async-start(f32[32,1,128]{2,1,0:T(1,128)} %bitcast.26), calls=%async_computation | async-start | bytes 32768 | tf_op jit(solution)/shard_map/all_to_all | solution.py:553
  19.5 0.0 copy-done.6
  19.5 0.0 copy-start.1
  19.5 0.0 copy-start.2
  19.5 0.0 copy-start.3
  19.5 10.5 %all_gather.3.rows_ref = f32[160,128]{1,0:T(8,128)S(1)} all-gather(f32[40,128]{1,0:T(8,128)S(1)} %copy-done.6), channel_id=1, replica_groups={{0,2,4,6},{1,3,5,7},{8,10,12,14},{9,11,13,15},{16,18,20,22},{17,19,21,2..., dimensions={0}, use_global_device_ids=true | all-gather | bytes 102400 | tf_op jit(solution)/shard_map/all_gather | solution.py:566
  30.1 1.2 %all-to-all-done = f32[32,1,128]{2,1,0:T(1,128)S(1)} async-done(((f32[32,1,128]{2,1,0:T(1,128)}), f32[32,1,128]{2,1,0:T(1,128)S(1)}, u32[]{:S(2)}, u32[]{:S(2)}) %all-to-all-start) | async-done | bytes 16416 | tf_op jit(solution)/shard_map/all_to_all | solution.py:553
  31.2 0.0 copy-start.4
  31.2 0.0 copy-start.5
  31.2 0.0 copy-done.1
  31.2 0.0 copy-done.2
  31.2 0.0 copy-done.3
  31.3 0.7 copy-done.4
  31.9 0.0 copy-done.5
  31.9 0.6 shard_map.78
  32.5 26.5 %all_to_all.20 = f32[32,1,640]{2,1,0:T(1,128)S(1)} all-to-all(f32[32,1,640]{2,1,0:T(1,128)S(1)} %bitcast.22), channel_id=1, replica_groups={{0,1,8,9,16,17,24,25,32,33,40,41,48,49,56,57,64,65,72,73,80,81,88,89,96..., dimensions={0} | all-to-all | bytes 163840 | tf_op jit(solution)/shard_map/all_to_all | solution.py:553
  59.0 4.4 %shard_map.79 = (f32[3,4,256]{2,1,0:T(4,128)}, f32[160,128]{1,0:T(8,128)S(1)}) custom-call(f32[160,128]{1,0:T(8,128)S(1)} %bitcast.18, s32[8,1024]{1,0:T(8,128)S(1)} %get-tuple-element.19.place_ref, s32[32,128]{1,0:T(8,128)S(1)} %get-tuple-element.20.inv_ref, s32[4,256]{1,0:T(4,128)S(1)} %get-tuple-element.21.depth_ref, ...), custom_call_target="tpu_custom_call" | custom-call | tf_op jit(solution)/shard_map/pallas_call | solution.py:496
  63.4 18.0 %all_to_all.21 = f32[32,1,640]{2,1,0:T(1,128)S(1)} all-to-all(f32[32,1,640]{2,1,0:T(1,128)S(1)} %bitcast.23), channel_id=1, replica_groups={{0,1,8,9,16,17,24,25,32,33,40,41,48,49,56,57,64,65,72,73,80,81,88,89,96..., dimensions={0} | all-to-all | bytes 163840 | tf_op jit(solution)/shard_map/all_to_all | solution.py:553
  81.4 0.8 shard_map.80
  82.2 0.0 copy-start
  82.3 13.7 %all_to_all.22 = f32[16,40,128]{2,1,0:T(8,128)S(1)} all-to-all(f32[16,40,128]{2,1,0:T(8,128)S(1)} %bitcast.16), channel_id=1, replica_groups={{0,2,4,6,128,130,132,134,256,258,260,262,384,386,388,390},{1,3,5,7,129,..., dimensions={0} | all-to-all | bytes 655360 | tf_op jit(solution)/shard_map/all_to_all | solution.py:553
  95.9 0.0 copy-done
  95.9 1.1 %shard_map.81 = f32[59,512]{1,0:T(8,128)} custom-call(f32[640,128]{1,0:T(8,128)S(1)} %bitcast.17, f32[59,512]{1,0:T(8,128)S(1)} %copy-done), custom_call_target="tpu_custom_call" | custom-call | tf_op jit(solution)/shard_map/pallas_call | solution.py:496
Async XLA Ops:
  2.7 16.8 %copy-start.6 = (f32[40,128]{1,0:T(8,128)S(1)}, f32[40,128]{1,0:T(8,128)}, u32[]{:S(2)}) copy-start(f32[40,128]{1,0:T(8,128)} %get-tuple-element.15) | copy-start | bytes 61444
  2.7 28.5 %all-to-all-start = ((f32[32,1,128]{2,1,0:T(1,128)}), f32[32,1,128]{2,1,0:T(1,128)S(1)}, u32[]{:S(2)}, u32[]{:S(2)}) async-start(f32[32,1,128]{2,1,0:T(1,128)} %bitcast.26), calls=%async_computation | async-start | bytes 32768 | tf_op jit(solution)/shard_map/all_to_all | solution.py:553
  19.5 11.8 %copy-start.1 = (s32[8,1024]{1,0:T(8,128)S(1)}, s32[8,1024]{1,0:T(8,128)}, u32[]{:S(2)}) copy-start(s32[8,1024]{1,0:T(8,128)} %get-tuple-element.16.refs_0_) | copy-start | bytes 98308
  19.5 11.7 %copy-start.2 = (s32[32,128]{1,0:T(8,128)S(1)}, s32[32,128]{1,0:T(8,128)}, u32[]{:S(2)}) copy-start(s32[32,128]{1,0:T(8,128)} %get-tuple-element.17.refs_1_) | copy-start | bytes 49156
  19.5 11.7 %copy-start.3 = (f32[1,3,4,256]{3,2,1,0:T(4,128)S(1)}, f32[1,3,4,256]{3,2,1,0:T(4,128)}, u32[]{:S(2)}) copy-start(f32[1,3,4,256]{3,2,1,0:T(4,128)} %param.11) | copy-start | bytes 36868
  31.2 0.7 copy-start.4
  31.2 0.7 copy-start.5
  82.2 13.7 %copy-start = (f32[59,512]{1,0:T(8,128)S(1)}, f32[59,512]{1,0:T(8,128)}, u32[]{:S(2)}) copy-start(f32[59,512]{1,0:T(8,128)} %attr_ref.1) | copy-start | bytes 362500

commit v4 on v3

--- a/solution.py
+++ b/solution.py
@@ -151,10 +151,14 @@
 
 
 def route_kernel(
-    tile_ref, owner_hbm, local_hbm, attr_hbm, cam_hbm, asked_ref, inv_ref, place_ref, rows_ref,
-    owner_ref, local_ref, attr_ref, cam_ref, wide_ref, sem,
+    tile_ref, owner_hbm, local_hbm, attr_hbm, cam_hbm, depth_hbm, cot_hbm,
+    asked_ref, inv_ref, place_ref, rows_ref, kept_ref,
+    owner_ref, local_ref, attr_ref, cam_ref, depth_ref, cot_ref, wide_ref, sem,
 ):
-    pairs = [(owner_hbm, owner_ref), (local_hbm, local_ref), (attr_hbm, attr_ref), (cam_hbm, cam_ref)]
+    pairs = [
+        (owner_hbm, owner_ref), (local_hbm, local_ref), (attr_hbm, attr_ref), (cam_hbm, cam_ref),
+        (depth_hbm, depth_ref), (cot_hbm, cot_ref),
+    ]
     copies = [pltpu.make_async_copy(src, dst, sem.at[n]) for n, (src, dst) in enumerate(pairs)]
     for copy in copies:
         copy.start()
@@ -167,8 +171,8 @@
     lane = lax.broadcasted_iota(I32, (1, SLOTS), 1)
     base = jnp.zeros((OWNERS, SLOTS), F32)
     table = jnp.zeros((4 * PEERS, 128), F32)
-    copies[0].wait()
-    copies[1].wait()
+    for copy in copies:
+        copy.wait()
     for t in range(TILES):
         owner = owner_ref[:, SLOTS * t : SLOTS * (t + 1)]
         hot = (oid == owner).astype(F32)
@@ -191,8 +195,12 @@
     n = PEERS
     asked_ref[...] = table[0:n] + 256.0 * table[n : 2 * n]
     inv_ref[...] = (table[2 * n : 3 * n] + 256.0 * table[3 * n :]).astype(I32)
-    copies[2].wait()
-    copies[3].wait()
+    for c in range(3):
+        kept_ref[4 * c : 4 * c + 4, :] = cot_ref[c]
+    kept_ref[12:16, :] = jnp.zeros((4, SLOTS), F32)
+    kept_ref[12:13, 0:6] = cam_ref[...]
+    for t in range(TILES):
+        place_ref[3:4, SLOTS * t : SLOTS * (t + 1)] = depth_ref[t : t + 1, :]
     spread_attributes(attr_ref, wide_ref)
     pos, logscale, quat, logit, sh = split_attributes(wide_ref)
     cam = [jnp.broadcast_to(cam_ref[:, j : j + 1], (8, 128)) for j in range(6)]
@@ -206,7 +214,7 @@
 
 
 def serve_kernel(asked_ref, rows_ref, *refs):
-    kept, (out_ref, *outs) = refs[:5], refs[5:]
+    kept, (out_ref, *outs) = refs[:3], refs[3:]
     for src, dst in zip(kept, outs):
         dst[...] = src[...]
     blank = jnp.zeros((4, 128), F32)
@@ -247,7 +255,7 @@
 
 
 def composite_kernel(
-    got_ref, place_ref, inv_ref, depth_ref, cot_ref, image_ref, out_ref,
+    got_ref, place_ref, inv_ref, kept_ref, image_ref, out_ref,
     par_ref, alpha_ref, pull_ref, weight_ref, grad_ref,
 ):
     last = got_ref[pl.ds(4, PEERS, stride=5), :]
@@ -296,69 +304,81 @@
         colors = jnp.concatenate([par[6], par[7], par[8], zero5], axis=0)
         chi, cmid, clo = [c.astype(F32) for c in split3(colors)]
         dy0s = []
+        coefs, pulls = [], []
         for h in range(2):
-            th = 4 * h + t
             cy = ((tile >> 4) * 16 + 8 * h + 4).astype(F32) * ey - 0.5
             dy0 = cy - w
             dy0s.append(dy0)
-            coef = jnp.concatenate(
-                [
-                    (A * dx0 + B * dy0) * dx0 + C * dy0 * dy0 + log_op,
-                    (2.0 * A * dx0 + B * dy0) * ex,
-                    (B * dx0 + 2.0 * C * dy0) * ey,
-                    A * (ex * ex),
-                    B * (ex * ey),
-                    C * (ey * ey),
-                    zero,
-                    zero,
-                ],
-                axis=0,
-            )
-            khi, kmid, klo = [k.astype(F32) for k in split3(coef)]
-            left = jnp.concatenate([khi, kmid, klo, chi, chi, chi, cmid, cmid, clo], axis=0)
-            left = jnp.concatenate([left, jnp.zeros((128 - 72, SLOTS), F32)], axis=0)
-            g = jnp.concatenate([cot_ref[c, t : t + 1, 128 * h : 128 * (h + 1)] for c in range(3)] + [blank[0:5]], axis=0)
-            ghi, gmid, glo = [x.astype(F32) for x in split3(g)]
-            cots.append((th, ghi, gmid))
-            right = jnp.concatenate(
-                [
-                    jnp.concatenate([mono8, mono8, mono8, blank, blank, blank, blank, blank, blank], axis=0),
-                    jnp.concatenate([blank, blank, blank, ghi, gmid, glo, ghi, gmid, ghi], axis=0),
-                ],
-                axis=1,
-            )
-            right = jnp.concatenate([right, jnp.zeros((128 - 72, 256), F32)], axis=0)
-            both = dot(jnp.transpose(left).astype(BF16), right.astype(BF16), 1, 0)
-            alpha_ref[pl.ds(th, SLOTS, stride=8), :] = both[:, :128]
-            pull_ref[pl.ds(th, SLOTS, stride=8), :] = both[:, 128:]
+            coef = [
+                (A * dx0 + B * dy0) * dx0 + C * dy0 * dy0 + log_op,
+                (2.0 * A * dx0 + B * dy0) * ex,
+                (B * dx0 + 2.0 * C * dy0) * ey,
+                A * (ex * ex),
+                B * (ex * ey),
+                C * (ey * ey),
+                zero,
+                zero,
+            ]
+            coefs += [k.astype(F32) for k in split3(jnp.concatenate(coef, axis=0))]
+            g = [kept_ref[4 * c + t : 4 * c + t + 1, 128 * h : 128 * (h + 1)] for c in range(3)]
+            ghi, gmid, glo = [x.astype(F32) for x in split3(jnp.concatenate(g + [blank[0:5]], axis=0))]
+            cots.append((4 * h + t, ghi, gmid))
+            pulls.append([ghi, gmid, glo, ghi, gmid, ghi])
+        left = coefs + [chi, chi, chi, cmid, cmid, clo] + [jnp.zeros((32, SLOTS), F32)]
+        left = jnp.transpose(jnp.concatenate(left, axis=0)).astype(BF16)
+        right = []
+        for h in range(2):
+            right.append([blank] * (3 * h) + [mono8] * 3 + [blank] * (13 - 3 * h))
+            right.append([blank] * 6 + pulls[h] + [blank] * 4)
+        right = jnp.concatenate([jnp.concatenate(r, axis=0) for r in right], axis=1).astype(BF16)
+        both = dot(left, right, 1, 0)
+        for h in range(2):
+            at = pl.ds(4 * h + t, SLOTS, stride=8)
+            alpha_ref[at, :] = both[:, 256 * h : 256 * h + 128]
+            pull_ref[at, :] = both[:, 256 * h + 128 : 256 * h + 256]
         geometry.append((ca, cb, cc, dx0, dy0s, chi, cmid))
 
-    depth = jnp.concatenate([depth_ref[:, 0:128], depth_ref[:, 128:256]], axis=0)
-    unroll = 8
-
-    def forward(j, trans):
+    depth = jnp.concatenate(
+        [place_ref[3:4, SLOTS * t + 128 * h : SLOTS * t + 128 * (h + 1)] for h in range(2) for t in range(TILES)], axis=0
+    )
+    segments, unroll = 4, 4
+    length = SLOTS // segments
+
+    def forward(j, state):
+        trans, behind = list(state[0]), list(state[1])
         for i in range(unroll):
-            s = j * unroll + i
-            at = pl.ds(pl.multiple_of(s * 8, 8), 8)
-            alpha = jnp.where(s < depth, jnp.exp2(alpha_ref[at, :]), 0.0)
-            weight = trans * alpha
-            alpha_ref[at, :] = alpha
-            weight_ref[at, :] = weight
-            trans = trans - weight
-        return trans
-
-    lax.fori_loop(0, SLOTS // unroll, forward, jnp.ones((8, 128), F32))
+            for n in range(segments):
+                s = n * length + j * unroll + i
+                at = pl.ds(pl.multiple_of(s * 8, 8), 8)
+                alpha = jnp.where(s < depth, jnp.exp2(alpha_ref[at, :]), 0.0)
+                weight = trans[n] * alpha
+                alpha_ref[at, :] = alpha
+                weight_ref[at, :] = weight
+                trans[n] = trans[n] - weight
+                behind[n] = behind[n] + weight * pull_ref[at, :]
+        return tuple(trans), tuple(behind)
+
+    ones, zeros = jnp.ones((8, 128), F32), jnp.zeros((8, 128), F32)
+    trans, behind = lax.fori_loop(0, length // unroll, forward, ((ones,) * segments, (zeros,) * segments))
+    starts, rest = [ones], [zeros]
+    for n in range(1, segments):
+        starts.append(starts[-1] * trans[n - 1])
+        rest.insert(0, behind[segments - n] + trans[segments - n] * rest[0])
 
     def backward(j, rest):
+        rest = list(rest)
         for i in range(unroll):
-            s = SLOTS - 1 - (j * unroll + i)
-            at = pl.ds(pl.multiple_of(s * 8, 8), 8)
-            more = pull_ref[at, :] - rest
-            rest = rest + alpha_ref[at, :] * more
-            pull_ref[at, :] = weight_ref[at, :] * more
-        return rest
-
-    lax.fori_loop(0, SLOTS // unroll, backward, jnp.zeros((8, 128), F32))
+            for n in range(segments):
+                s = (n + 1) * length - 1 - (j * unroll + i)
+                at = pl.ds(pl.multiple_of(s * 8, 8), 8)
+                more = pull_ref[at, :] - rest[n]
+                rest[n] = rest[n] + alpha_ref[at, :] * more
+                weight = starts[n] * weight_ref[at, :]
+                weight_ref[at, :] = weight
+                pull_ref[at, :] = weight * more
+        return tuple(rest)
+
+    lax.fori_loop(0, length // unroll, backward, tuple(rest))
 
     cots = {th: (ghi, gmid) for th, ghi, gmid in cots}
     for t in range(TILES):
@@ -414,7 +434,7 @@
     out_ref[pl.ds(4, PEERS, stride=5), :] = jnp.concatenate(more, axis=0)
 
 
-def collect_kernel(back_ref, asked_ref, cam_ref, out_ref):
+def collect_kernel(back_ref, asked_ref, kept_ref, out_ref):
     lid = lax.broadcasted_iota(I32, (G_DEV, 256), 0)
     sub = lax.broadcasted_iota(I32, (8, 128), 0)
     lane = lax.broadcasted_iota(I32, (8, 128), 1)
@@ -440,8 +460,7 @@
             pairs.append(jnp.concatenate(rows, axis=0).astype(BF16))
         acc = acc + dot(jnp.concatenate(pairs, axis=1), hot, 1, 1)
     rows = acc[0:40] + acc[40:80]
-    cam = jnp.concatenate([cam_ref[...], jnp.zeros((1, 122), F32)], axis=1)
-    tail = jnp.concatenate([cam, jnp.zeros((3, 128), F32)], axis=0)
+    tail = kept_ref[12:16, 0:128]
     for r in range(NEAR):
         part = [rows[8 * r : 8 * r + 8, 128 * j : 128 * (j + 1)] for j in range(4)]
         part += [rows[32 + r : 33 + r, 128 * j : 128 * (j + 1)] for j in range(4)] + [tail]
@@ -450,7 +469,8 @@
             out_ref[40 * (NEAR * v + r) : 40 * (NEAR * v + r + 1), :] = part
 
 
-def pull_kernel(parts_ref, attr_ref, out_ref, wide_ref, res_ref, all_ref):
+def pull_kernel(parts_ref, attr_ref, image_in_ref, out_ref, image_ref, wide_ref, res_ref, all_ref):
+    image_ref[...] = image_in_ref[...]
     for v in range(VIEWS):
         start = 40 * NEAR * v
         total = parts_ref[start : start + 36, :]
@@ -507,16 +527,18 @@
     return pltpu.VMEM(shape, dtype)
 
 
-def route(first_tile, owner, local, attributes, camera):
+def route(first_tile, owner, local, attributes, camera, depth, cot):
     return call(
         route_kernel,
-        [((PEERS, 128), F32), ((PEERS, 128), I32), ((8, TILES * SLOTS), I32), ((40, 128), F32)],
-        (first_tile, owner, local, attributes, camera),
+        [
+            ((PEERS, 128), F32), ((PEERS, 128), I32), ((8, TILES * SLOTS), I32), ((40, 128), F32), ((16, SLOTS), F32),
+        ],
+        (first_tile, owner, local, attributes, camera, depth, cot),
         [
             vmem(1, TILES * SLOTS, dtype=I32), vmem(TILES, SLOTS, dtype=I32), vmem(ATTR, G_DEV), vmem(1, 6),
-            vmem(ATTR * 8, 128), pltpu.SemaphoreType.DMA((4,)),
+            vmem(TILES, SLOTS, dtype=I32), vmem(3, TILES, SLOTS), vmem(ATTR * 8, 128), pltpu.SemaphoreType.DMA((6,)),
         ],
-        [SMEM] + [HBM] * 4,
+        [SMEM] + [HBM] * 6,
         60,
     )
 
@@ -526,27 +548,27 @@
     return call(serve_kernel, outs, (asked, rows, *kept))
 
 
-def composite(got, place, inv, depth, cot):
+def composite(got, place, inv, kept):
     big = vmem(SLOTS * 8, 128)
     return call(
         composite_kernel,
         [((3, TILES, 256), F32), ((5 * PEERS, 128), F32)],
-        (got, place, inv, depth, cot),
+        (got, place, inv, kept),
         [vmem(16, TILES * SLOTS), big, big, big, vmem(16, TILES * SLOTS)],
     )
 
 
-def collect(back, asked, camera):
-    return call(collect_kernel, [((VIEWS * NEAR * 40, 128), F32)], (back, asked, camera))[0]
-
-
-def pull_back(parts, attributes):
+def collect(back, asked, kept):
+    return call(collect_kernel, [((VIEWS * NEAR * 40, 128), F32)], (back, asked, kept))[0]
+
+
+def pull_back(parts, attributes, image):
     return call(
         pull_kernel,
-        [((ATTR, G_DEV), F32)],
-        (parts, attributes),
+        [((ATTR, G_DEV), F32), (image.shape, F32)],
+        (parts, attributes, image),
         [vmem(ATTR * 8, 128), vmem(ATTR * 4, 128), vmem(40 * VIEWS, 128)],
-    )[0]
+    )
 
 
 def exchange(x, axis, groups):
@@ -561,16 +583,19 @@
 def per_device(attributes, camera, list_owner, list_local, term_depth, image_cot):
     owner = list_owner.reshape(1, -1)
     first_tile = (lax.axis_index("dev") * TILES).astype(I32).reshape(1)
-    asked, inv, place, rows = route(first_tile, owner, list_local[0], attributes, camera)
+    asked, inv, place, rows, kept = route(
+        first_tile, owner, list_local[0], attributes, camera, term_depth[0], image_cot[0]
+    )
     asked = exchange(asked.reshape(PEERS, 1, 128), "dev", ACROSS).reshape(PEERS, 128)
     rows = lax.all_gather(rows, "dev", axis_index_groups=WITHIN, tiled=True)
-    sent, place, inv, depth, cot, camera = serve(asked, rows, place, inv, term_depth[0], image_cot[0], camera)
+    sent, place, inv, kept = serve(asked, rows, place, inv, kept)
     got = exchange(sent.reshape(PEERS, 1, 640), "dev", ACROSS).reshape(5 * PEERS, 128)
-    image, grads = composite(got, place, inv, depth, cot)
+    image, grads = composite(got, place, inv, kept)
     back = exchange(grads.reshape(PEERS, 1, 640), "dev", ACROSS).reshape(5 * PEERS, 128)
-    mine = collect(back, asked, camera)
+    mine = collect(back, asked, kept)
     parts = exchange(mine.reshape(VIEWS * NEAR, 40, 128), ("view", "dev"), VIEWS_WITHIN)
-    return image[None], pull_back(parts.reshape(VIEWS * NEAR * 40, 128), attributes)
+    grad, image = pull_back(parts.reshape(VIEWS * NEAR * 40, 128), attributes, image)
+    return image[None], grad
 
 
 def solution(mesh):

time: 97.8 us -> 96.5 us (0.987)
  no operation moved by 1% of the time
where the time goes in v4:
time: 96.5 us; the launch traced here: 95.8 us
  blocking collectives  68.7 us (71%)
  starting transfers between devices  16.8 us (17%)
  Pallas kernels  8.33 us (9%)
  waiting for transfers between devices  1.19 us (1%)
    all_to_all x3, blocking collectives, exchange(): lax.all_to_all(x, axis, split_axis=0, concat_axis=0, tiled=True, axis_ind...  58.2 us
    all_to_all x1, starting transfers between devices, exchange(): lax.all_to_all(x, axis, split_axis=0, concat_axis=0, tiled=True, axis_ind...  16.8 us
    all_gather x1, blocking collectives, per_device(): rows = lax.all_gather(rows, 'dev', axis_index_groups=WITHIN, tiled=True)  10.5 us
    pallas_call x5, Pallas kernels, call(): pl.pallas_call(kernel, out_shape=[jax.ShapeDtypeStruct(s, d) for s, d in...  8.33 us
  transfers between devices with their start and end apart: 1, of which 1 were waited for; matrix products, arithmetic and copies ran while one was open for 0% of the time, Pallas kernels for 0%

profile of v4, /device:TPU:1, one launch (start us, length us, event | category | flops | bytes accessed | tf_op | source)
XLA Modules:
  0.0 95.8 jit_solution(2556764630283240537)
XLA Ops:
  0.6 2.2 %shard_map.77 = (f32[32,128]{1,0:T(8,128)}, s32[32,128]{1,0:T(8,128)}, s32[8,1024]{1,0:T(8,128)}, f32[40,128]{1,0:T(8,128)}, f32[16,256]{1,0:T(8,128)}) custom-call(s32[1]{0:T(128)} %bitcast.tile_ref, s32[1,1024]{1,0:T(1,128)} %bitcast.26, s32[4,256]{1,0:T(4,128)} %bitcast.27, f32[59,512]{1,0:T(8,128)} %attr_ref.1, f32[1,6]{1,0:T(1,128)} %cam_hbm.1, ...), custom_call_target="tpu_custom_call" | custom-call | tf_op jit(solution)/shard_map/pallas_call | solution.py:516
  2.8 0.0 copy-start.4
  2.9 16.8 %all-to-all-start = ((f32[32,1,128]{2,1,0:T(1,128)}), f32[32,1,128]{2,1,0:T(1,128)S(1)}, u32[]{:S(2)}, u32[]{:S(2)}) async-start(f32[32,1,128]{2,1,0:T(1,128)} %bitcast.24), calls=%async_computation | async-start | bytes 32768 | tf_op jit(solution)/shard_map/all_to_all | solution.py:575
  19.6 0.0 copy-done.4
  19.6 0.0 copy-start.1
  19.6 0.0 copy-start.2
  19.7 0.0 copy-start.3
  19.7 10.5 %all_gather.3.rows_ref = f32[160,128]{1,0:T(8,128)S(1)} all-gather(f32[40,128]{1,0:T(8,128)S(1)} %copy-done.4), channel_id=1, replica_groups={{0,2,4,6},{1,3,5,7},{8,10,12,14},{9,11,13,15},{16,18,20,22},{17,19,21,2..., dimensions={0}, use_global_device_ids=true | all-gather | bytes 102400 | tf_op jit(solution)/shard_map/all_gather | solution.py:590
  30.2 1.2 %all-to-all-done = f32[32,1,128]{2,1,0:T(1,128)S(1)} async-done(((f32[32,1,128]{2,1,0:T(1,128)}), f32[32,1,128]{2,1,0:T(1,128)S(1)}, u32[]{:S(2)}, u32[]{:S(2)}) %all-to-all-start) | async-done | bytes 16416 | tf_op jit(solution)/shard_map/all_to_all | solution.py:575
  31.4 0.0 copy-done.1
  31.4 0.0 copy-done.2
  31.4 0.0 copy-done.3
  31.4 0.6 shard_map.78
  32.0 26.5 %all_to_all.20 = f32[32,1,640]{2,1,0:T(1,128)S(1)} all-to-all(f32[32,1,640]{2,1,0:T(1,128)S(1)} %bitcast.22), channel_id=1, replica_groups={{0,1,8,9,16,17,24,25,32,33,40,41,48,49,56,57,64,65,72,73,80,81,88,89,96..., dimensions={0} | all-to-all | bytes 163840 | tf_op jit(solution)/shard_map/all_to_all | solution.py:575
  58.5 3.6 %shard_map.79 = (f32[3,4,256]{2,1,0:T(4,128)S(1)}, f32[160,128]{1,0:T(8,128)S(1)}) custom-call(f32[160,128]{1,0:T(8,128)S(1)} %bitcast.19, s32[8,1024]{1,0:T(8,128)S(1)} %get-tuple-element.21.place_ref, s32[32,128]{1,0:T(8,128)S(1)} %get-tuple-element.22.inv_ref, f32[16,256]{1,0:T(8,128)S(1)} %get-tuple-element.23.kept_ref), custom_call_target="tpu_custom_call" | custom-call | tf_op jit(solution)/shard_map/pallas_call | solution.py:516
  62.2 18.0 %all_to_all.21 = f32[32,1,640]{2,1,0:T(1,128)S(1)} all-to-all(f32[32,1,640]{2,1,0:T(1,128)S(1)} %bitcast.23), channel_id=1, replica_groups={{0,1,8,9,16,17,24,25,32,33,40,41,48,49,56,57,64,65,72,73,80,81,88,89,96..., dimensions={0} | all-to-all | bytes 163840 | tf_op jit(solution)/shard_map/all_to_all | solution.py:575
  80.2 0.8 shard_map.80
  81.0 0.0 copy-start
  81.0 13.7 %all_to_all.22 = f32[16,40,128]{2,1,0:T(8,128)S(1)} all-to-all(f32[16,40,128]{2,1,0:T(8,128)S(1)} %bitcast.17), channel_id=1, replica_groups={{0,2,4,6,128,130,132,134,256,258,260,262,384,386,388,390},{1,3,5,7,129,..., dimensions={0} | all-to-all | bytes 655360 | tf_op jit(solution)/shard_map/all_to_all | solution.py:575
  94.7 0.0 copy-done
  94.7 1.1 %shard_map.81 = (f32[59,512]{1,0:T(8,128)}, f32[3,4,256]{2,1,0:T(4,128)}) custom-call(f32[640,128]{1,0:T(8,128)S(1)} %bitcast.16, f32[59,512]{1,0:T(8,128)S(1)} %copy-done, f32[3,4,256]{2,1,0:T(4,128)S(1)} %get-tuple-element.25.image_in_ref), custom_call_target="tpu_custom_call" | custom-call | tf_op jit(solution)/shard_map/pallas_call | solution.py:516
Async XLA Ops:
  2.8 16.8 %copy-start.4 = (f32[40,128]{1,0:T(8,128)S(1)}, f32[40,128]{1,0:T(8,128)}, u32[]{:S(2)}) copy-start(f32[40,128]{1,0:T(8,128)} %get-tuple-element.16) | copy-start | bytes 61444
  2.9 28.5 %all-to-all-start = ((f32[32,1,128]{2,1,0:T(1,128)}), f32[32,1,128]{2,1,0:T(1,128)S(1)}, u32[]{:S(2)}, u32[]{:S(2)}) async-start(f32[32,1,128]{2,1,0:T(1,128)} %bitcast.24), calls=%async_computation | async-start | bytes 32768 | tf_op jit(solution)/shard_map/all_to_all | solution.py:575
  19.6 11.8 %copy-start.1 = (s32[8,1024]{1,0:T(8,128)S(1)}, s32[8,1024]{1,0:T(8,128)}, u32[]{:S(2)}) copy-start(s32[8,1024]{1,0:T(8,128)} %get-tuple-element.17.refs_0_) | copy-start | bytes 98308
  19.6 11.8 %copy-start.2 = (s32[32,128]{1,0:T(8,128)S(1)}, s32[32,128]{1,0:T(8,128)}, u32[]{:S(2)}) copy-start(s32[32,128]{1,0:T(8,128)} %get-tuple-element.18.refs_1_) | copy-start | bytes 49156
  19.7 11.8 %copy-start.3 = (f32[16,256]{1,0:T(8,128)S(1)}, f32[16,256]{1,0:T(8,128)}, u32[]{:S(2)}) copy-start(f32[16,256]{1,0:T(8,128)} %get-tuple-element.19.refs_2_) | copy-start | bytes 49156
  81.0 13.7 %copy-start = (f32[59,512]{1,0:T(8,128)S(1)}, f32[59,512]{1,0:T(8,128)}, u32[]{:S(2)}) copy-start(f32[59,512]{1,0:T(8,128)} %attr_ref.1) | copy-start | bytes 362500

commit v5 on v4

--- a/solution.py
+++ b/solution.py
@@ -12,6 +12,8 @@
 OWNERS = 128
 PEERS = 32
 NEAR = 4
+PLANES = 16
+RANKS = 8
 G_DEV = 512
 ATTR = 59
 VIEWS = 4
@@ -152,8 +154,8 @@
 
 def route_kernel(
     tile_ref, owner_hbm, local_hbm, attr_hbm, cam_hbm, depth_hbm, cot_hbm,
-    asked_ref, inv_ref, place_ref, rows_ref, kept_ref,
-    owner_ref, local_ref, attr_ref, cam_ref, depth_ref, cot_ref, wide_ref, sem,
+    asked_ref, inv_ref, place_ref, rows_ref, kept_ref, names_ref,
+    owner_ref, local_ref, attr_ref, cam_ref, depth_ref, cot_ref, wide_ref, tmp_ref, sem,
 ):
     pairs = [
         (owner_hbm, owner_ref), (local_hbm, local_ref), (attr_hbm, attr_ref), (cam_hbm, cam_ref),
@@ -170,7 +172,9 @@
     pid = lax.broadcasted_iota(I32, (PEERS, SLOTS), 0)
     lane = lax.broadcasted_iota(I32, (1, SLOTS), 1)
     base = jnp.zeros((OWNERS, SLOTS), F32)
+    gid = lax.broadcasted_iota(I32, (2 * RANKS, SLOTS), 0)
     table = jnp.zeros((4 * PEERS, 128), F32)
+    request = jnp.zeros((4 * RANKS, 128), F32)
     for copy in copies:
         copy.wait()
     for t in range(TILES):
@@ -180,20 +184,26 @@
         count = dot(hot16, before, 1, 0) + base
         base = base + dot(hot16, every, 1, 0)
         rank = jnp.sum(hot * count, axis=0, keepdims=True).astype(I32)
+        local = local_ref[t : t + 1, :]
+        local_parts = [local & 255, local >> 8]
+        slot = lane + (SLOTS * t + 1)
+        group = (owner & 7) * 2 + (owner >> 6)
+        lanes = ((owner >> 3) & 7) * CAP + rank
+        place_ref[0:1, SLOTS * t : SLOTS * (t + 1)] = group
+        place_ref[1:2, SLOTS * t : SLOTS * (t + 1)] = lanes
+        hot_group = (gid == group).astype(F32)
+        vals = jnp.concatenate([hot_group * p.astype(F32) for p in local_parts], axis=0).astype(BF16)
+        request = request + dot(vals, (oid == lanes).astype(F32).astype(BF16), 1, 1)
         peer = (owner >> 3) * 2 + (owner & 1)
         lanes = ((owner >> 1) & 3) * CAP + rank
-        place_ref[0:1, SLOTS * t : SLOTS * (t + 1)] = peer
-        place_ref[1:2, SLOTS * t : SLOTS * (t + 1)] = lanes
         hot_peer = (pid == peer).astype(F32)
-        hot_lane = ((oid & 63) == lanes).astype(F32).astype(BF16)
-        local = local_ref[t : t + 1, :]
-        slot = lane + (SLOTS * t + 1)
-        parts = [local & 255, local >> 8, slot & 255, slot >> 8]
+        parts = local_parts + [slot & 255, slot >> 8]
         vals = jnp.concatenate([hot_peer * p.astype(F32) for p in parts], axis=0).astype(BF16)
-        table = table + dot(vals, hot_lane, 1, 1)
+        table = table + dot(vals, ((oid & 63) == lanes).astype(F32).astype(BF16), 1, 1)
     place_ref[2:3, :] = jnp.full((1, TILES * SLOTS), tile_ref[0], I32)
     n = PEERS
-    asked_ref[...] = table[0:n] + 256.0 * table[n : 2 * n]
+    asked_ref[...] = request[0 : 2 * RANKS] + 256.0 * request[2 * RANKS :]
+    names_ref[...] = table[0:n] + 256.0 * table[n : 2 * n]
     inv_ref[...] = (table[2 * n : 3 * n] + 256.0 * table[3 * n :]).astype(I32)
     for c in range(3):
         kept_ref[4 * c : 4 * c + 4, :] = cot_ref[c]
@@ -208,74 +218,71 @@
     log_opacity = -LOG2E * jnp.log(1.0 + jnp.exp(-logit))
     rows = rows[:5] + [log_opacity] + rows[5:]
     for c in range(8):
-        rows_ref[pl.ds(c, 4, stride=8), :] = rows[c][0:4]
-    rows_ref[32:36, :] = rows[8][0:4]
-    rows_ref[36:40, :] = jnp.zeros((4, 128), F32)
-
-
-def serve_kernel(asked_ref, rows_ref, *refs):
-    kept, (out_ref, *outs) = refs[:3], refs[3:]
+        tmp_ref[pl.ds(c, 4, stride=8), :] = rows[c][0:4]
+    tmp_ref[32:36, :] = rows[8][0:4]
+    tmp_ref[36:40, :] = jnp.zeros((4, 128), F32)
+    rows = tmp_ref[...]
+    for z in range(PLANES):
+        rows_ref[40 * z : 40 * (z + 1), :] = rows
+
+
+def serve_kernel(tile_ref, asked_ref, rows_ref, *refs):
+    kept, (out_ref, *outs) = refs[:4], refs[4:]
     for src, dst in zip(kept, outs):
         dst[...] = src[...]
-    blank = jnp.zeros((4, 128), F32)
-    table = []
-    for j in range(4):
-        part = [rows_ref[40 * r + 8 * j : 40 * r + 8 * j + 8, :] for r in range(NEAR)]
-        part += [rows_ref[pl.ds(32 + j, NEAR, stride=40), :], blank]
-        table.append(jnp.concatenate(part, axis=0))
-    table = [x.astype(F32) for x in split3(jnp.concatenate(table, axis=1))]
-    table = jnp.concatenate(table + [jnp.zeros((8, G_DEV), F32)], axis=0).astype(BF16)
+    mine = 2 * ((tile_ref[0] // TILES) & (RANKS - 1))
     lid = lax.broadcasted_iota(I32, (G_DEV, 256), 0)
     sub = lax.broadcasted_iota(I32, (8, 128), 0)
-    lane = lax.broadcasted_iota(I32, (8, 128), 1)
-    near, left = (lane & 63) >> 4, lane < 64
-    for n in range(0, PEERS, 4):
-        hot = (lid == pair_ids(asked_ref, n)).astype(F32).astype(BF16)
-        got = dot(table, hot, 1, 0)
-        got = got[0:40] + got[40:80] + got[80:120]
-        for i in range(2):
-            half = got[:, 128 * i : 128 * (i + 1)]
-            main = half[0:8]
-            for r in range(1, NEAR):
-                main = jnp.where(near == r, half[8 * r : 8 * (r + 1)], main)
-            turned = pltpu.roll(main, 64, 1)
-            last = jnp.sum(jnp.where(near == sub, half[32:40], 0.0), axis=0, keepdims=True)
-            at = 5 * (n + 2 * i)
-            out_ref[at : at + 4, :] = jnp.where(left[0:4], main[0:4], turned[4:8])
-            out_ref[at + 4 : at + 5, :] = last
-            out_ref[at + 5 : at + 9, :] = jnp.where(left[0:4], turned[0:4], main[4:8])
-            out_ref[at + 9 : at + 10, :] = pltpu.roll(jnp.broadcast_to(last, (8, 128)), 64, 1)[0:1]
-
-
-def pair_ids(asked_ref, n):
-    left = lax.broadcasted_iota(I32, (1, 128), 1) < 64
-    rows = [asked_ref[n + i : n + i + 1, :] for i in range(4)]
-    pairs = [jnp.where(left, rows[0], rows[1]), jnp.where(left, rows[2], rows[3])]
-    return jnp.concatenate(pairs, axis=1).astype(I32)
+    near = lax.broadcasted_iota(I32, (8, 128), 1) >> 4
+    for half in range(2):
+        start = 320 * half
+        table = []
+        for j in range(4):
+            part = [rows_ref[start + 40 * r + 8 * j : start + 40 * r + 8 * j + 8, :] for r in range(8)]
+            part.append(rows_ref[pl.ds(start + 32 + j, 8, stride=40), :])
+            table.append(jnp.concatenate(part, axis=0))
+        table = [x.astype(F32) for x in split3(jnp.concatenate(table, axis=1))]
+        table = jnp.concatenate(table + [jnp.zeros((8, G_DEV), F32)], axis=0).astype(BF16)
+        for r in range(0, RANKS, 2):
+            ids = [asked_ref[pl.ds(16 * (r + i) + mine + half, 1), :] for i in range(2)]
+            hot = (lid == jnp.concatenate(ids, axis=1).astype(I32)).astype(F32).astype(BF16)
+            got = dot(table, hot, 1, 0)
+            got = got[0:72] + got[72:144] + got[144:216]
+            for i in range(2):
+                part = got[:, 128 * i : 128 * (i + 1)]
+                main = part[0:8]
+                for n in range(1, 8):
+                    main = jnp.where(near == n, part[8 * n : 8 * (n + 1)], main)
+                at = 9 * (2 * (r + i) + half)
+                out_ref[at : at + 8, :] = main
+                last = jnp.sum(jnp.where(near == sub, part[64:72], 0.0), axis=0, keepdims=True)
+                out_ref[at + 8 : at + 9, :] = last
+
+
+def pair_ids(back_ref, n):
+    left = lax.broadcasted_iota(I32, (8, 128), 1) < 64
+    rows = [jnp.broadcast_to(back_ref[5 * (n + i) + 4 : 5 * (n + i) + 5, :], (8, 128)) for i in range(4)]
+    pairs = [jnp.where(left, pltpu.roll(rows[i], 64, 1), rows[i + 1]) for i in (0, 2)]
+    return jnp.concatenate(pairs, axis=1)[0:1].astype(I32)
 
 
 def composite_kernel(
-    got_ref, place_ref, inv_ref, kept_ref, image_ref, out_ref,
+    got_ref, place_ref, inv_ref, kept_ref, names_ref, image_ref, out_ref,
     par_ref, alpha_ref, pull_ref, weight_ref, grad_ref,
 ):
-    last = got_ref[pl.ds(4, PEERS, stride=5), :]
+    groups = 2 * RANKS
+    last = got_ref[pl.ds(8, groups, stride=9), :]
     sub = lax.broadcasted_iota(I32, (8, 128), 0)
-    tables = []
-    for n in range(PEERS):
-        rows = got_ref[5 * n : 5 * n + 4, :]
-        tables.append(jnp.concatenate([rows, rows], axis=0))
     for b in range(8):
-        peer = jnp.broadcast_to(place_ref[0:1, 128 * b : 128 * (b + 1)], (8, 128))
+        group = jnp.broadcast_to(place_ref[0:1, 128 * b : 128 * (b + 1)], (8, 128))
         lanes = jnp.broadcast_to(place_ref[1:2, 128 * b : 128 * (b + 1)], (8, 128))
-        both = jnp.where(sub < 4, lanes, lanes + 64)
-        got = lane_gather(tables[0], both)
-        for n in range(1, PEERS):
-            got = jnp.where(peer == n, lane_gather(tables[n], both), got)
+        got = lane_gather(got_ref[0:8, :], lanes)
+        for n in range(1, groups):
+            got = jnp.where(group == n, lane_gather(got_ref[9 * n : 9 * n + 8, :], lanes), got)
         par_ref[0:8, 128 * b : 128 * (b + 1)] = got
-        final = jnp.zeros((8, 128), F32)
-        for n in range(0, PEERS, 8):
-            final = final + jnp.where(peer == sub + n, lane_gather(last[n : n + 8], lanes), 0.0)
-        par_ref[8:9, 128 * b : 128 * (b + 1)] = jnp.sum(final, axis=0, keepdims=True)
+        low = jnp.where(group == sub, lane_gather(last[0:8], lanes), 0.0)
+        high = jnp.where(group == sub + 8, lane_gather(last[8:16], lanes), 0.0)
+        par_ref[8:9, 128 * b : 128 * (b + 1)] = jnp.sum(low + high, axis=0, keepdims=True)
 
     q = lax.broadcasted_iota(I32, (16, 128), 1)
     row16 = lax.broadcasted_iota(I32, (16, 128), 0)
@@ -431,17 +438,18 @@
         got = pick(tables, jnp.broadcast_to(inv[n : n + 1], (8, 128)))
         out_ref[5 * n : 5 * n + 4, :] = jnp.where(left, got[0:4], got[4:8])
     more = [pick(last, inv[n : n + 8]) for n in range(0, PEERS, 8)]
-    out_ref[pl.ds(4, PEERS, stride=5), :] = jnp.concatenate(more, axis=0)
-
-
-def collect_kernel(back_ref, asked_ref, kept_ref, out_ref):
+    left = lax.broadcasted_iota(I32, (PEERS, 128), 1) < 64
+    out_ref[pl.ds(4, PEERS, stride=5), :] = jnp.where(left, jnp.concatenate(more, axis=0), names_ref[...])
+
+
+def collect_kernel(back_ref, kept_ref, out_ref):
     lid = lax.broadcasted_iota(I32, (G_DEV, 256), 0)
     sub = lax.broadcasted_iota(I32, (8, 128), 0)
     lane = lax.broadcasted_iota(I32, (8, 128), 1)
     near, left = (lane & 63) >> 4, lane < 64
     acc = jnp.zeros((80, G_DEV), F32)
     for n in range(0, PEERS, 4):
-        hot = (lid == pair_ids(asked_ref, n)).astype(F32).astype(BF16)
+        hot = (lid == pair_ids(back_ref, n)).astype(F32).astype(BF16)
         pairs = []
         for i in range(2):
             at = 5 * (n + 2 * i)
@@ -531,35 +539,37 @@
     return call(
         route_kernel,
         [
-            ((PEERS, 128), F32), ((PEERS, 128), I32), ((8, TILES * SLOTS), I32), ((40, 128), F32), ((16, SLOTS), F32),
+            ((2 * RANKS, 128), F32), ((PEERS, 128), I32), ((8, TILES * SLOTS), I32), ((40 * PLANES, 128), F32),
+            ((16, SLOTS), F32), ((PEERS, 128), F32),
         ],
         (first_tile, owner, local, attributes, camera, depth, cot),
         [
             vmem(1, TILES * SLOTS, dtype=I32), vmem(TILES, SLOTS, dtype=I32), vmem(ATTR, G_DEV), vmem(1, 6),
-            vmem(TILES, SLOTS, dtype=I32), vmem(3, TILES, SLOTS), vmem(ATTR * 8, 128), pltpu.SemaphoreType.DMA((6,)),
+            vmem(TILES, SLOTS, dtype=I32), vmem(3, TILES, SLOTS), vmem(ATTR * 8, 128), vmem(40, 128),
+            pltpu.SemaphoreType.DMA((6,)),
         ],
         [SMEM] + [HBM] * 6,
         60,
     )
 
 
-def serve(asked, rows, *kept):
-    outs = [((5 * PEERS, 128), F32)] + [(k.shape, k.dtype) for k in kept]
-    return call(serve_kernel, outs, (asked, rows, *kept))
-
-
-def composite(got, place, inv, kept):
+def serve(first_tile, asked, rows, *kept):
+    outs = [((18 * RANKS, 128), F32)] + [(k.shape, k.dtype) for k in kept]
+    return call(serve_kernel, outs, (first_tile, asked, rows, *kept), (), [SMEM] + [VMEM] * (2 + len(kept)))
+
+
+def composite(got, place, inv, kept, names):
     big = vmem(SLOTS * 8, 128)
     return call(
         composite_kernel,
         [((3, TILES, 256), F32), ((5 * PEERS, 128), F32)],
-        (got, place, inv, kept),
+        (got, place, inv, kept, names),
         [vmem(16, TILES * SLOTS), big, big, big, vmem(16, TILES * SLOTS)],
     )
 
 
-def collect(back, asked, kept):
-    return call(collect_kernel, [((VIEWS * NEAR * 40, 128), F32)], (back, asked, kept))[0]
+def collect(back, kept):
+    return call(collect_kernel, [((VIEWS * NEAR * 40, 128), F32)], (back, kept))[0]
 
 
 def pull_back(parts, attributes, image):
@@ -575,24 +585,26 @@
     return lax.all_to_all(x, axis, split_axis=0, concat_axis=0, tiled=True, axis_index_groups=groups)
 
 
-ACROSS = [[8 * z + 2 * y + c for z in range(16) for c in range(2)] for y in range(NEAR)]
-WITHIN = [[8 * z + 2 * y + c for y in range(NEAR)] for z in range(16) for c in range(2)]
+ALONG = [[8 * z + r for z in range(PLANES)] for r in range(RANKS)]
+PLANE = [[8 * z + r for r in range(RANKS)] for z in range(PLANES)]
+ACROSS = [[8 * z + 2 * y + c for z in range(PLANES) for c in range(2)] for y in range(NEAR)]
+WITHIN = [[8 * z + 2 * y + c for y in range(NEAR)] for z in range(PLANES) for c in range(2)]
 VIEWS_WITHIN = [[OWNERS * v + d for v in range(VIEWS) for d in group] for group in WITHIN]
 
 
 def per_device(attributes, camera, list_owner, list_local, term_depth, image_cot):
     owner = list_owner.reshape(1, -1)
     first_tile = (lax.axis_index("dev") * TILES).astype(I32).reshape(1)
-    asked, inv, place, rows, kept = route(
+    asked, inv, place, rows, kept, names = route(
         first_tile, owner, list_local[0], attributes, camera, term_depth[0], image_cot[0]
     )
-    asked = exchange(asked.reshape(PEERS, 1, 128), "dev", ACROSS).reshape(PEERS, 128)
-    rows = lax.all_gather(rows, "dev", axis_index_groups=WITHIN, tiled=True)
-    sent, place, inv, kept = serve(asked, rows, place, inv, kept)
-    got = exchange(sent.reshape(PEERS, 1, 640), "dev", ACROSS).reshape(5 * PEERS, 128)
-    image, grads = composite(got, place, inv, kept)
+    rows = exchange(rows.reshape(PLANES, 40, 128), "dev", ALONG).reshape(PLANES * 40, 128)
+    asked = lax.all_gather(asked, "dev", axis_index_groups=PLANE, tiled=True)
+    sent, place, inv, kept, names = serve(first_tile, asked, rows, place, inv, kept, names)
+    got = exchange(sent.reshape(RANKS, 1, 2304), "dev", PLANE).reshape(18 * RANKS, 128)
+    image, grads = composite(got, place, inv, kept, names)
     back = exchange(grads.reshape(PEERS, 1, 640), "dev", ACROSS).reshape(5 * PEERS, 128)
-    mine = collect(back, asked, kept)
+    mine = collect(back, kept)
     parts = exchange(mine.reshape(VIEWS * NEAR, 40, 128), ("view", "dev"), VIEWS_WITHIN)
     grad, image = pull_back(parts.reshape(VIEWS * NEAR * 40, 128), attributes, image)
     return image[None], grad

time: 96.5 us -> 89.8 us (0.931)
  blocking collectives: 68.7 us -> 62.7 us
  starting transfers between devices: 16.8 us -> 15.8 us
    all_to_all x3, blocking collectives: 58.2 us -> 48.5 us  [exchange(): lax.all_to_all(x, axis, split_axis=0, concat_axis=0, tiled=True, axis_ind...]
    all_gather x1, blocking collectives: 10.5 us -> 14.2 us  [per_device(): asked = lax.all_gather(asked, 'dev', axis_index_groups=PLANE, tiled=True)]
    all_to_all x1, starting transfers between devices: 16.8 us -> 15.8 us  [exchange(): lax.all_to_all(x, axis, split_axis=0, concat_axis=0, tiled=True, axis_ind...]
where the time goes in v5:
time: 89.8 us; the launch traced here: 89 us
  blocking collectives  62.7 us (70%)
  starting transfers between devices  15.8 us (18%)
  Pallas kernels  8.81 us (10%)
  waiting for transfers between devices  1.01 us (1%)
    all_to_all x3, blocking collectives, exchange(): lax.all_to_all(x, axis, split_axis=0, concat_axis=0, tiled=True, axis_ind...  48.5 us
    all_to_all x1, starting transfers between devices, exchange(): lax.all_to_all(x, axis, split_axis=0, concat_axis=0, tiled=True, axis_ind...  15.8 us
    all_gather x1, blocking collectives, per_device(): asked = lax.all_gather(asked, 'dev', axis_index_groups=PLANE, tiled=True)  14.2 us
    pallas_call x5, Pallas kernels, call(): pl.pallas_call(kernel, out_shape=[jax.ShapeDtypeStruct(s, d) for s, d in...  8.81 us
  transfers between devices with their start and end apart: 1, of which 1 were waited for; matrix products, arithmetic and copies ran while one was open for 0% of the time, Pallas kernels for 0%

profile of v5, /device:TPU:1, one launch (start us, length us, event | category | flops | bytes accessed | tf_op | source)
XLA Modules:
  0.0 89.0 jit_solution(9787683657668143024)
XLA Ops:
  0.6 2.7 %shard_map.77 = (f32[16,128]{1,0:T(8,128)}, s32[32,128]{1,0:T(8,128)}, s32[8,1024]{1,0:T(8,128)}, f32[640,128]{1,0:T(8,128)}, f32[16,256]{1,0:T(8,128)}, /*index=5*/f32[32,128]{1,0:T(8,128)}) custom-call(s32[1]{0:T(128)} %bitcast.tile_ref, s32[1,1024]{1,0:T(1,128)} %bitcast.23, s32[4,256]{1,0:T(4,128)} %bitcast.24, f32[59,512]{1,0:T(8,128)} %attr_ref.1, ...), custom_call_target="tpu_custom_call" | custom-call | tf_op jit(solution)/shard_map/pallas_call | solution.py:524
  3.4 0.0 copy-start.5
  3.4 15.8 %all-to-all-start = ((f32[16,40,128]{2,1,0:T(8,128)}), f32[16,40,128]{2,1,0:T(8,128)S(1)}, u32[]{:S(2)}, u32[]{:S(2)}) async-start(f32[16,40,128]{2,1,0:T(8,128)} %bitcast.21), calls=%async_computation | async-start | bytes 655360 | tf_op jit(solution)/shard_map/all_to_all | solution.py:585
  19.1 0.0 copy-done.5
  19.1 0.0 copy-start.1
  19.2 0.0 copy-start.2
  19.2 0.0 copy-start.3
  19.2 0.0 copy-start.4
  19.2 14.2 %all_gather.3.asked_ref = f32[128,128]{1,0:T(8,128)S(1)} all-gather(f32[16,128]{1,0:T(8,128)S(1)} %copy-done.5), channel_id=1, replica_groups={{0,1,2,3,4,5,6,7},{8,9,10,11,12,13,14,15},{16,17,18,19,20,21,22,23},{24..., dimensions={0}, use_global_device_ids=true | all-gather | bytes 73728 | tf_op jit(solution)/shard_map/all_gather | solution.py:602
  33.4 1.0 %all-to-all-done = f32[16,40,128]{2,1,0:T(8,128)S(1)} async-done(((f32[16,40,128]{2,1,0:T(8,128)}), f32[16,40,128]{2,1,0:T(8,128)S(1)}, u32[]{:S(2)}, u32[]{:S(2)}) %all-to-all-start) | async-done | bytes 327712 | tf_op jit(solution)/shard_map/all_to_all | solution.py:585
  34.4 0.0 copy-done.1
  34.4 0.0 copy-done.2
  34.4 0.0 copy-done.3
  34.4 0.0 copy-done.4
  34.4 0.8 shard_map.78
  35.2 15.7 %all_to_all.20 = f32[8,1,2304]{2,1,0:T(1,128)S(1)} all-to-all(f32[8,1,2304]{2,1,0:T(1,128)S(1)} %bitcast.20), channel_id=1, replica_groups={{0,1,2,3,4,5,6,7},{8,9,10,11,12,13,14,15},{16,17,18,19,20,21,22,23},{24..., dimensions={0} | all-to-all | bytes 147456 | tf_op jit(solution)/shard_map/all_to_all | solution.py:585
  50.8 3.4 %shard_map.79 = (f32[3,4,256]{2,1,0:T(4,128)S(1)}, f32[160,128]{1,0:T(8,128)S(1)}) custom-call(f32[144,128]{1,0:T(8,128)S(1)} %bitcast.18, s32[8,1024]{1,0:T(8,128)S(1)} %get-tuple-element.24.place_ref, s32[32,128]{1,0:T(8,128)S(1)} %get-tuple-element.25.inv_ref, f32[16,256]{1,0:T(8,128)S(1)} %get-tuple-element.26.kept_ref, ...), custom_call_target="tpu_custom_call" | custom-call | tf_op jit(solution)/shard_map/pallas_call | solution.py:524
  54.2 20.5 %all_to_all.21 = f32[32,1,640]{2,1,0:T(1,128)S(1)} all-to-all(f32[32,1,640]{2,1,0:T(1,128)S(1)} %bitcast.19), channel_id=1, replica_groups={{0,1,8,9,16,17,24,25,32,33,40,41,48,49,56,57,64,65,72,73,80,81,88,89,96..., dimensions={0} | all-to-all | bytes 163840 | tf_op jit(solution)/shard_map/all_to_all | solution.py:585
  74.7 0.8 shard_map.80
  75.6 0.0 copy-start
  75.6 12.3 %all_to_all.22 = f32[16,40,128]{2,1,0:T(8,128)S(1)} all-to-all(f32[16,40,128]{2,1,0:T(8,128)S(1)} %bitcast.16), channel_id=1, replica_groups={{0,2,4,6,128,130,132,134,256,258,260,262,384,386,388,390},{1,3,5,7,129,..., dimensions={0} | all-to-all | bytes 655360 | tf_op jit(solution)/shard_map/all_to_all | solution.py:585
  87.9 0.0 copy-done
  87.9 1.1 %shard_map.81 = (f32[59,512]{1,0:T(8,128)}, f32[3,4,256]{2,1,0:T(4,128)}) custom-call(f32[640,128]{1,0:T(8,128)S(1)} %bitcast.15, f32[59,512]{1,0:T(8,128)S(1)} %copy-done, f32[3,4,256]{2,1,0:T(4,128)S(1)} %get-tuple-element.29.image_in_ref), custom_call_target="tpu_custom_call" | custom-call | tf_op jit(solution)/shard_map/pallas_call | solution.py:524
Async XLA Ops:
  3.4 15.8 %copy-start.5 = (f32[16,128]{1,0:T(8,128)S(1)}, f32[16,128]{1,0:T(8,128)}, u32[]{:S(2)}) copy-start(f32[16,128]{1,0:T(8,128)} %get-tuple-element.17) | copy-start | bytes 24580
  3.4 31.0 %all-to-all-start = ((f32[16,40,128]{2,1,0:T(8,128)}), f32[16,40,128]{2,1,0:T(8,128)S(1)}, u32[]{:S(2)}, u32[]{:S(2)}) async-start(f32[16,40,128]{2,1,0:T(8,128)} %bitcast.21), calls=%async_computation | async-start | bytes 655360 | tf_op jit(solution)/shard_map/all_to_all | solution.py:585
  19.1 15.2 %copy-start.1 = (s32[8,1024]{1,0:T(8,128)S(1)}, s32[8,1024]{1,0:T(8,128)}, u32[]{:S(2)}) copy-start(s32[8,1024]{1,0:T(8,128)} %get-tuple-element.19.refs_0_) | copy-start | bytes 98308
  19.2 15.2 %copy-start.2 = (s32[32,128]{1,0:T(8,128)S(1)}, s32[32,128]{1,0:T(8,128)}, u32[]{:S(2)}) copy-start(s32[32,128]{1,0:T(8,128)} %get-tuple-element.20.refs_1_) | copy-start | bytes 49156
  19.2 15.2 %copy-start.3 = (f32[16,256]{1,0:T(8,128)S(1)}, f32[16,256]{1,0:T(8,128)}, u32[]{:S(2)}) copy-start(f32[16,256]{1,0:T(8,128)} %get-tuple-element.21.refs_2_) | copy-start | bytes 49156
  19.2 15.2 %copy-start.4 = (f32[32,128]{1,0:T(8,128)S(1)}, f32[32,128]{1,0:T(8,128)}, u32[]{:S(2)}) copy-start(f32[32,128]{1,0:T(8,128)} %get-tuple-element.22.refs_3_) | copy-start | bytes 49156
  75.6 12.3 %copy-start = (f32[59,512]{1,0:T(8,128)S(1)}, f32[59,512]{1,0:T(8,128)}, u32[]{:S(2)}) copy-start(f32[59,512]{1,0:T(8,128)} %attr_ref.1) | copy-start | bytes 362500

commit v6 on v5

--- a/solution.py
+++ b/solution.py
@@ -154,8 +154,8 @@
 
 def route_kernel(
     tile_ref, owner_hbm, local_hbm, attr_hbm, cam_hbm, depth_hbm, cot_hbm,
-    asked_ref, inv_ref, place_ref, rows_ref, kept_ref, names_ref,
-    owner_ref, local_ref, attr_ref, cam_ref, depth_ref, cot_ref, wide_ref, tmp_ref, sem,
+    near_ref, far_ref, inv_ref, place_ref, rows_hbm, kept_ref, names_ref,
+    owner_ref, local_ref, attr_ref, cam_ref, depth_ref, cot_ref, wide_ref, tmp_ref, rows_ref, sem,
 ):
     pairs = [
         (owner_hbm, owner_ref), (local_hbm, local_ref), (attr_hbm, attr_ref), (cam_hbm, cam_ref),
@@ -164,6 +164,23 @@
     copies = [pltpu.make_async_copy(src, dst, sem.at[n]) for n, (src, dst) in enumerate(pairs)]
     for copy in copies:
         copy.start()
+    copies[2].wait()
+    copies[3].wait()
+    spread_attributes(attr_ref, wide_ref)
+    pos, logscale, quat, logit, sh = split_attributes(wide_ref)
+    cam = [jnp.broadcast_to(cam_ref[:, j : j + 1], (8, 128)) for j in range(6)]
+    rows = project(pos, logscale, quat, sh, camera_terms(cam[:3], cam[3:]))
+    log_opacity = -LOG2E * jnp.log(1.0 + jnp.exp(-logit))
+    rows = rows[:5] + [log_opacity] + rows[5:]
+    for c in range(8):
+        tmp_ref[pl.ds(c, 4, stride=8), :] = rows[c][0:4]
+    tmp_ref[32:36, :] = rows[8][0:4]
+    tmp_ref[36:40, :] = jnp.zeros((4, 128), F32)
+    rows = tmp_ref[...]
+    for z in range(PLANES):
+        rows_ref[40 * z : 40 * (z + 1), :] = rows
+    rows_copy = pltpu.make_async_copy(rows_ref, rows_hbm, sem.at[6])
+    rows_copy.start()
     before = (
         lax.broadcasted_iota(I32, (SLOTS, SLOTS), 0) < lax.broadcasted_iota(I32, (SLOTS, SLOTS), 1)
     ).astype(F32).astype(BF16)
@@ -175,8 +192,9 @@
     gid = lax.broadcasted_iota(I32, (2 * RANKS, SLOTS), 0)
     table = jnp.zeros((4 * PEERS, 128), F32)
     request = jnp.zeros((4 * RANKS, 128), F32)
-    for copy in copies:
-        copy.wait()
+    for n in (0, 1, 4, 5):
+        copies[n].wait()
+    core = (tile_ref[0] // TILES) & 1
     for t in range(TILES):
         owner = owner_ref[:, SLOTS * t : SLOTS * (t + 1)]
         hot = (oid == owner).astype(F32)
@@ -191,7 +209,7 @@
         lanes = ((owner >> 3) & 7) * CAP + rank
         place_ref[0:1, SLOTS * t : SLOTS * (t + 1)] = group
         place_ref[1:2, SLOTS * t : SLOTS * (t + 1)] = lanes
-        hot_group = (gid == group).astype(F32)
+        hot_group = (gid == ((owner & 1) ^ core) * 8 + (owner & 6) + (owner >> 6)).astype(F32)
         vals = jnp.concatenate([hot_group * p.astype(F32) for p in local_parts], axis=0).astype(BF16)
         request = request + dot(vals, (oid == lanes).astype(F32).astype(BF16), 1, 1)
         peer = (owner >> 3) * 2 + (owner & 1)
@@ -202,7 +220,8 @@
         table = table + dot(vals, ((oid & 63) == lanes).astype(F32).astype(BF16), 1, 1)
     place_ref[2:3, :] = jnp.full((1, TILES * SLOTS), tile_ref[0], I32)
     n = PEERS
-    asked_ref[...] = request[0 : 2 * RANKS] + 256.0 * request[2 * RANKS :]
+    near_ref[...] = request[0:8] + 256.0 * request[16:24]
+    far_ref[...] = request[8:16] + 256.0 * request[24:32]
     names_ref[...] = table[0:n] + 256.0 * table[n : 2 * n]
     inv_ref[...] = (table[2 * n : 3 * n] + 256.0 * table[3 * n :]).astype(I32)
     for c in range(3):
@@ -211,26 +230,15 @@
     kept_ref[12:13, 0:6] = cam_ref[...]
     for t in range(TILES):
         place_ref[3:4, SLOTS * t : SLOTS * (t + 1)] = depth_ref[t : t + 1, :]
-    spread_attributes(attr_ref, wide_ref)
-    pos, logscale, quat, logit, sh = split_attributes(wide_ref)
-    cam = [jnp.broadcast_to(cam_ref[:, j : j + 1], (8, 128)) for j in range(6)]
-    rows = project(pos, logscale, quat, sh, camera_terms(cam[:3], cam[3:]))
-    log_opacity = -LOG2E * jnp.log(1.0 + jnp.exp(-logit))
-    rows = rows[:5] + [log_opacity] + rows[5:]
-    for c in range(8):
-        tmp_ref[pl.ds(c, 4, stride=8), :] = rows[c][0:4]
-    tmp_ref[32:36, :] = rows[8][0:4]
-    tmp_ref[36:40, :] = jnp.zeros((4, 128), F32)
-    rows = tmp_ref[...]
-    for z in range(PLANES):
-        rows_ref[40 * z : 40 * (z + 1), :] = rows
+    rows_copy.wait()
 
 
 def serve_kernel(tile_ref, asked_ref, rows_ref, *refs):
     kept, (out_ref, *outs) = refs[:4], refs[4:]
     for src, dst in zip(kept, outs):
         dst[...] = src[...]
-    mine = 2 * ((tile_ref[0] // TILES) & (RANKS - 1))
+    dev = tile_ref[0] // TILES
+    core, mine = dev & 1, dev & 6
     lid = lax.broadcasted_iota(I32, (G_DEV, 256), 0)
     sub = lax.broadcasted_iota(I32, (8, 128), 0)
     near = lax.broadcasted_iota(I32, (8, 128), 1) >> 4
@@ -244,7 +252,7 @@
         table = [x.astype(F32) for x in split3(jnp.concatenate(table, axis=1))]
         table = jnp.concatenate(table + [jnp.zeros((8, G_DEV), F32)], axis=0).astype(BF16)
         for r in range(0, RANKS, 2):
-            ids = [asked_ref[pl.ds(16 * (r + i) + mine + half, 1), :] for i in range(2)]
+            ids = [asked_ref[pl.ds(8 * r + 8 * (i ^ core) + mine + half, 1), :] for i in range(2)]
             hot = (lid == jnp.concatenate(ids, axis=1).astype(I32)).astype(F32).astype(BF16)
             got = dot(table, hot, 1, 0)
             got = got[0:72] + got[72:144] + got[144:216]
@@ -520,12 +528,12 @@
 MIB = 1024 * 1024
 
 
-def call(kernel, outs, args, scratch=(), in_specs=None, limit=24):
+def call(kernel, outs, args, scratch=(), in_specs=None, out_specs=None, limit=24):
     return pl.pallas_call(
         kernel,
         out_shape=[jax.ShapeDtypeStruct(s, d) for s, d in outs],
         in_specs=in_specs or [VMEM] * len(args),
-        out_specs=[VMEM] * len(outs),
+        out_specs=out_specs or [VMEM] * len(outs),
         scratch_shapes=list(scratch),
         compiler_params=pltpu.CompilerParams(vmem_limit_bytes=limit * MIB),
     )(*args)
@@ -539,16 +547,17 @@
     return call(
         route_kernel,
         [
-            ((2 * RANKS, 128), F32), ((PEERS, 128), I32), ((8, TILES * SLOTS), I32), ((40 * PLANES, 128), F32),
+            ((8, 128), F32), ((8, 128), F32), ((PEERS, 128), I32), ((8, TILES * SLOTS), I32), ((40 * PLANES, 128), F32),
             ((16, SLOTS), F32), ((PEERS, 128), F32),
         ],
         (first_tile, owner, local, attributes, camera, depth, cot),
         [
             vmem(1, TILES * SLOTS, dtype=I32), vmem(TILES, SLOTS, dtype=I32), vmem(ATTR, G_DEV), vmem(1, 6),
             vmem(TILES, SLOTS, dtype=I32), vmem(3, TILES, SLOTS), vmem(ATTR * 8, 128), vmem(40, 128),
-            pltpu.SemaphoreType.DMA((6,)),
+            vmem(40 * PLANES, 128), pltpu.SemaphoreType.DMA((7,)),
         ],
         [SMEM] + [HBM] * 6,
+        [VMEM] * 4 + [HBM] + [VMEM] * 2,
         60,
     )
 
@@ -595,11 +604,12 @@
 def per_device(attributes, camera, list_owner, list_local, term_depth, image_cot):
     owner = list_owner.reshape(1, -1)
     first_tile = (lax.axis_index("dev") * TILES).astype(I32).reshape(1)
-    asked, inv, place, rows, kept, names = route(
+    near, far, inv, place, rows, kept, names = route(
         first_tile, owner, list_local[0], attributes, camera, term_depth[0], image_cot[0]
     )
     rows = exchange(rows.reshape(PLANES, 40, 128), "dev", ALONG).reshape(PLANES * 40, 128)
-    asked = lax.all_gather(asked, "dev", axis_index_groups=PLANE, tiled=True)
+    far = lax.ppermute(far, "dev", [(d, d ^ 1) for d in range(OWNERS)])
+    asked = lax.all_gather(jnp.concatenate([near, far]), "dev", axis_index_groups=WITHIN, tiled=True)
     sent, place, inv, kept, names = serve(first_tile, asked, rows, place, inv, kept, names)
     got = exchange(sent.reshape(RANKS, 1, 2304), "dev", PLANE).reshape(18 * RANKS, 128)
     image, grads = composite(got, place, inv, kept, names)

time: 89.8 us -> 90.2 us (level)
  blocking collectives: 62.7 us -> 58.5 us
  starting transfers between devices: 15.8 us -> 18.7 us
  waiting for transfers between devices: 1.01 us -> 2.4 us
    all_gather x1, blocking collectives: 14.2 us -> 9.93 us  [per_device(): lax.all_gather(jnp.concatenate([near, far]), 'dev', axis_index_groups=WIT...]
    ppermute x0 -> x1, starting transfers between devices: none -> 2.86 us  [per_device(): far = lax.ppermute(far, 'dev', [(d, d ^ 1) for d in range(OWNERS)])]
  transfers between devices with their start and end apart: 1 -> 2, of which waited for: 1 -> 2; matrix products, arithmetic and copies ran while one was open for 0% -> 0% of each run, Pallas kernels for 0% -> 0%
where the time goes in v6:
time: 90.2 us; the launch traced here: 89.3 us
  blocking collectives  58.5 us (65%)
  starting transfers between devices  18.7 us (21%)
  Pallas kernels  8.94 us (10%)
  waiting for transfers between devices  2.4 us (3%)
    all_to_all x3, blocking collectives, exchange(): lax.all_to_all(x, axis, split_axis=0, concat_axis=0, tiled=True, axis_ind...  48.5 us
    all_to_all x1, starting transfers between devices, exchange(): lax.all_to_all(x, axis, split_axis=0, concat_axis=0, tiled=True, axis_ind...  15.9 us
    all_gather x1, blocking collectives, per_device(): lax.all_gather(jnp.concatenate([near, far]), 'dev', axis_index_groups=WIT...  9.93 us
    pallas_call x5, Pallas kernels, call(): pl.pallas_call(kernel, out_shape=[jax.ShapeDtypeStruct(s, d) for s, d in...  8.94 us
    ppermute x1, starting transfers between devices, per_device(): far = lax.ppermute(far, 'dev', [(d, d ^ 1) for d in range(OWNERS)])  2.86 us
  transfers between devices with their start and end apart: 2, of which 2 were waited for; matrix products, arithmetic and copies ran while one was open for 0% of the time, Pallas kernels for 0%

profile of v6, /device:TPU:1, one launch (start us, length us, event | category | flops | bytes accessed | tf_op | source)
XLA Modules:
  0.0 89.3 jit_solution(18254506590496113211)
XLA Ops:
  0.6 2.8 %shard_map.77 = (f32[8,128]{1,0:T(8,128)}, f32[8,128]{1,0:T(8,128)}, s32[32,128]{1,0:T(8,128)}, s32[8,1024]{1,0:T(8,128)}, f32[640,128]{1,0:T(8,128)}, /*index=5*/f32[16,256]{1,0:T(8,128)}, f32[32,128]{1,0:T(8,128)}) custom-call(s32[1]{0:T(128)} %bitcast.tile_ref, s32[1,1024]{1,0:T(1,128)} %bitcast.23, s32[4,256]{1,0:T(4,128)} %bitcast.24, ...), custom_call_target="tpu_custom_call" | custom-call | tf_op jit(solution)/shard_map/pallas_call | solution.py:532
  3.5 0.0 copy-start.6
  3.5 0.0 copy-start.5
  3.5 0.0 copy-start.4
  3.5 15.9 %all-to-all-start = ((f32[16,40,128]{2,1,0:T(8,128)}), f32[16,40,128]{2,1,0:T(8,128)S(1)}, u32[]{:S(2)}, u32[]{:S(2)}) async-start(f32[16,40,128]{2,1,0:T(8,128)} %bitcast.21), calls=%async_computation | async-start | bytes 655360 | tf_op jit(solution)/shard_map/all_to_all | solution.py:594
  19.4 0.0 copy-done.6
  19.4 2.9 %collective-permute-start = (f32[8,128]{1,0:T(8,128)S(1)}, f32[8,128]{1,0:T(8,128)S(1)}, u32[]{:S(2)}, u32[]{:S(2)}) collective-permute-start(f32[8,128]{1,0:T(8,128)S(1)} %copy-done.6), channel_id=1, source_target_pairs={{0,1},{1,0},{2,3},{3,2},{4,5},{5,4},{6,7},{7,6},{8,9},{9,8},{10,11... | collective-permute-start | bytes 12296 | tf_op jit(solution)/shard_map/ppermute | solution.py:611
  22.3 0.8 collective-permute-done
  23.1 0.0 copy-done.5
  23.1 0.0 copy-start.1
  23.1 0.0 copy-start.2
  23.1 0.0 copy-start.3
  23.1 9.9 %all_gather.3.asked_ref = f32[64,128]{1,0:T(8,128)S(1)} all-gather(f32[16,128]{1,0:T(8,128)S(1)} %pad_maximum_fusion), channel_id=1, replica_groups={{0,2,4,6},{1,3,5,7},{8,10,12,14},{9,11,13,15},{16,18,20,22},{17,19,21,2..., dimensions={0}, use_global_device_ids=true | all-gather | bytes 40960 | tf_op jit(solution)/shard_map/all_gather | solution.py:612
  33.0 1.6 %all-to-all-done = f32[16,40,128]{2,1,0:T(8,128)S(1)} async-done(((f32[16,40,128]{2,1,0:T(8,128)}), f32[16,40,128]{2,1,0:T(8,128)S(1)}, u32[]{:S(2)}, u32[]{:S(2)}) %all-to-all-start) | async-done | bytes 327712 | tf_op jit(solution)/shard_map/all_to_all | solution.py:594
  34.6 0.0 copy-done.4
  34.6 0.0 copy-done.1
  34.6 0.0 copy-done.2
  34.6 0.0 copy-done.3
  34.7 0.8 shard_map.78
  35.4 15.7 %all_to_all.20 = f32[8,1,2304]{2,1,0:T(1,128)S(1)} all-to-all(f32[8,1,2304]{2,1,0:T(1,128)S(1)} %bitcast.20), channel_id=1, replica_groups={{0,1,2,3,4,5,6,7},{8,9,10,11,12,13,14,15},{16,17,18,19,20,21,22,23},{24..., dimensions={0} | all-to-all | bytes 147456 | tf_op jit(solution)/shard_map/all_to_all | solution.py:594
  51.1 3.4 %shard_map.79 = (f32[3,4,256]{2,1,0:T(4,128)S(1)}, f32[160,128]{1,0:T(8,128)S(1)}) custom-call(f32[144,128]{1,0:T(8,128)S(1)} %bitcast.18, s32[8,1024]{1,0:T(8,128)S(1)} %get-tuple-element.26.place_ref, s32[32,128]{1,0:T(8,128)S(1)} %get-tuple-element.27.inv_ref, f32[16,256]{1,0:T(8,128)S(1)} %get-tuple-element.28.kept_ref, ...), custom_call_target="tpu_custom_call" | custom-call | tf_op jit(solution)/shard_map/pallas_call | solution.py:532
  54.5 20.5 %all_to_all.21 = f32[32,1,640]{2,1,0:T(1,128)S(1)} all-to-all(f32[32,1,640]{2,1,0:T(1,128)S(1)} %bitcast.19), channel_id=1, replica_groups={{0,1,8,9,16,17,24,25,32,33,40,41,48,49,56,57,64,65,72,73,80,81,88,89,96..., dimensions={0} | all-to-all | bytes 163840 | tf_op jit(solution)/shard_map/all_to_all | solution.py:594
  75.0 0.9 shard_map.80
  75.9 0.0 copy-start
  75.9 12.3 %all_to_all.22 = f32[16,40,128]{2,1,0:T(8,128)S(1)} all-to-all(f32[16,40,128]{2,1,0:T(8,128)S(1)} %bitcast.16), channel_id=1, replica_groups={{0,2,4,6,128,130,132,134,256,258,260,262,384,386,388,390},{1,3,5,7,129,..., dimensions={0} | all-to-all | bytes 655360 | tf_op jit(solution)/shard_map/all_to_all | solution.py:594
  88.2 0.0 copy-done
  88.2 1.1 %shard_map.81 = (f32[59,512]{1,0:T(8,128)}, f32[3,4,256]{2,1,0:T(4,128)}) custom-call(f32[640,128]{1,0:T(8,128)S(1)} %bitcast.15, f32[59,512]{1,0:T(8,128)S(1)} %copy-done, f32[3,4,256]{2,1,0:T(4,128)S(1)} %get-tuple-element.31.image_in_ref), custom_call_target="tpu_custom_call" | custom-call | tf_op jit(solution)/shard_map/pallas_call | solution.py:532
  (1 shorter events, 0.0 us)
Async XLA Ops:
  3.5 15.9 %copy-start.6 = (f32[8,128]{1,0:T(8,128)S(1)}, f32[8,128]{1,0:T(8,128)}, u32[]{:S(2)}) copy-start(f32[8,128]{1,0:T(8,128)} %get-tuple-element.19) | copy-start | bytes 12292
  3.5 19.6 %copy-start.5 = (f32[8,128]{1,0:T(8,128)S(1)}, f32[8,128]{1,0:T(8,128)}, u32[]{:S(2)}) copy-start(f32[8,128]{1,0:T(8,128)} %get-tuple-element.18) | copy-start | bytes 12292
  3.5 31.1 %copy-start.4 = (f32[32,128]{1,0:T(8,128)S(1)}, f32[32,128]{1,0:T(8,128)}, u32[]{:S(2)}) copy-start(f32[32,128]{1,0:T(8,128)} %get-tuple-element.24.refs_3_) | copy-start | bytes 49156
  3.5 31.1 %all-to-all-start = ((f32[16,40,128]{2,1,0:T(8,128)}), f32[16,40,128]{2,1,0:T(8,128)S(1)}, u32[]{:S(2)}, u32[]{:S(2)}) async-start(f32[16,40,128]{2,1,0:T(8,128)} %bitcast.21), calls=%async_computation | async-start | bytes 655360 | tf_op jit(solution)/shard_map/all_to_all | solution.py:594
  19.4 3.7 %collective-permute-start = (f32[8,128]{1,0:T(8,128)S(1)}, f32[8,128]{1,0:T(8,128)S(1)}, u32[]{:S(2)}, u32[]{:S(2)}) collective-permute-start(f32[8,128]{1,0:T(8,128)S(1)} %copy-done.6), channel_id=1, source_target_pairs={{0,1},{1,0},{2,3},{3,2},{4,5},{5,4},{6,7},{7,6},{8,9},{9,8},{10,11... | collective-permute-start | bytes 12296 | tf_op jit(solution)/shard_map/ppermute | solution.py:611
  23.1 11.5 %copy-start.1 = (s32[8,1024]{1,0:T(8,128)S(1)}, s32[8,1024]{1,0:T(8,128)}, u32[]{:S(2)}) copy-start(s32[8,1024]{1,0:T(8,128)} %get-tuple-element.21.refs_0_) | copy-start | bytes 98308
  23.1 11.5 %copy-start.2 = (s32[32,128]{1,0:T(8,128)S(1)}, s32[32,128]{1,0:T(8,128)}, u32[]{:S(2)}) copy-start(s32[32,128]{1,0:T(8,128)} %get-tuple-element.22.refs_1_) | copy-start | bytes 49156
  23.1 11.5 %copy-start.3 = (f32[16,256]{1,0:T(8,128)S(1)}, f32[16,256]{1,0:T(8,128)}, u32[]{:S(2)}) copy-start(f32[16,256]{1,0:T(8,128)} %get-tuple-element.23.refs_2_) | copy-start | bytes 49156
  75.9 12.3 %copy-start = (f32[59,512]{1,0:T(8,128)S(1)}, f32[59,512]{1,0:T(8,128)}, u32[]{:S(2)}) copy-start(f32[59,512]{1,0:T(8,128)} %attr_ref.1) | copy-start | bytes 362500

commit v7 on v6

--- a/solution.py
+++ b/solution.py
@@ -14,6 +14,7 @@
 NEAR = 4
 PLANES = 16
 RANKS = 8
+SEGMENTS = 4
 G_DEV = 512
 ATTR = 59
 VIEWS = 4
@@ -154,8 +155,8 @@
 
 def route_kernel(
     tile_ref, owner_hbm, local_hbm, attr_hbm, cam_hbm, depth_hbm, cot_hbm,
-    near_ref, far_ref, inv_ref, place_ref, rows_hbm, kept_ref, names_ref,
-    owner_ref, local_ref, attr_ref, cam_ref, depth_ref, cot_ref, wide_ref, tmp_ref, rows_ref, sem,
+    near_ref, far_ref, inv_ref, place_ref, rows_ref, kept_ref, names_ref,
+    owner_ref, local_ref, attr_ref, cam_ref, depth_ref, cot_ref, wide_ref, tmp_ref, sem,
 ):
     pairs = [
         (owner_hbm, owner_ref), (local_hbm, local_ref), (attr_hbm, attr_ref), (cam_hbm, cam_ref),
@@ -164,8 +165,8 @@
     copies = [pltpu.make_async_copy(src, dst, sem.at[n]) for n, (src, dst) in enumerate(pairs)]
     for copy in copies:
         copy.start()
-    copies[2].wait()
-    copies[3].wait()
+    for copy in copies:
+        copy.wait()
     spread_attributes(attr_ref, wide_ref)
     pos, logscale, quat, logit, sh = split_attributes(wide_ref)
     cam = [jnp.broadcast_to(cam_ref[:, j : j + 1], (8, 128)) for j in range(6)]
@@ -175,12 +176,9 @@
     for c in range(8):
         tmp_ref[pl.ds(c, 4, stride=8), :] = rows[c][0:4]
     tmp_ref[32:36, :] = rows[8][0:4]
-    tmp_ref[36:40, :] = jnp.zeros((4, 128), F32)
     rows = tmp_ref[...]
     for z in range(PLANES):
-        rows_ref[40 * z : 40 * (z + 1), :] = rows
-    rows_copy = pltpu.make_async_copy(rows_ref, rows_hbm, sem.at[6])
-    rows_copy.start()
+        rows_ref[36 * z : 36 * (z + 1), :] = rows
     before = (
         lax.broadcasted_iota(I32, (SLOTS, SLOTS), 0) < lax.broadcasted_iota(I32, (SLOTS, SLOTS), 1)
     ).astype(F32).astype(BF16)
@@ -192,8 +190,6 @@
     gid = lax.broadcasted_iota(I32, (2 * RANKS, SLOTS), 0)
     table = jnp.zeros((4 * PEERS, 128), F32)
     request = jnp.zeros((4 * RANKS, 128), F32)
-    for n in (0, 1, 4, 5):
-        copies[n].wait()
     core = (tile_ref[0] // TILES) & 1
     for t in range(TILES):
         owner = owner_ref[:, SLOTS * t : SLOTS * (t + 1)]
@@ -230,7 +226,6 @@
     kept_ref[12:13, 0:6] = cam_ref[...]
     for t in range(TILES):
         place_ref[3:4, SLOTS * t : SLOTS * (t + 1)] = depth_ref[t : t + 1, :]
-    rows_copy.wait()
 
 
 def serve_kernel(tile_ref, asked_ref, rows_ref, *refs):
@@ -243,11 +238,11 @@
     sub = lax.broadcasted_iota(I32, (8, 128), 0)
     near = lax.broadcasted_iota(I32, (8, 128), 1) >> 4
     for half in range(2):
-        start = 320 * half
+        start = 288 * half
         table = []
         for j in range(4):
-            part = [rows_ref[start + 40 * r + 8 * j : start + 40 * r + 8 * j + 8, :] for r in range(8)]
-            part.append(rows_ref[pl.ds(start + 32 + j, 8, stride=40), :])
+            part = [rows_ref[start + 36 * r + 8 * j : start + 36 * r + 8 * j + 8, :] for r in range(8)]
+            part.append(rows_ref[pl.ds(start + 32 + j, 8, stride=36), :])
             table.append(jnp.concatenate(part, axis=0))
         table = [x.astype(F32) for x in split3(jnp.concatenate(table, axis=1))]
         table = jnp.concatenate(table + [jnp.zeros((8, G_DEV), F32)], axis=0).astype(BF16)
@@ -356,44 +351,35 @@
     depth = jnp.concatenate(
         [place_ref[3:4, SLOTS * t + 128 * h : SLOTS * t + 128 * (h + 1)] for h in range(2) for t in range(TILES)], axis=0
     )
-    segments, unroll = 4, 4
+    segments = SEGMENTS
     length = SLOTS // segments
 
-    def forward(j, state):
-        trans, behind = list(state[0]), list(state[1])
-        for i in range(unroll):
-            for n in range(segments):
-                s = n * length + j * unroll + i
-                at = pl.ds(pl.multiple_of(s * 8, 8), 8)
-                alpha = jnp.where(s < depth, jnp.exp2(alpha_ref[at, :]), 0.0)
-                weight = trans[n] * alpha
-                alpha_ref[at, :] = alpha
-                weight_ref[at, :] = weight
-                trans[n] = trans[n] - weight
-                behind[n] = behind[n] + weight * pull_ref[at, :]
-        return tuple(trans), tuple(behind)
-
     ones, zeros = jnp.ones((8, 128), F32), jnp.zeros((8, 128), F32)
-    trans, behind = lax.fori_loop(0, length // unroll, forward, ((ones,) * segments, (zeros,) * segments))
+    trans, behind = [ones] * segments, [zeros] * segments
+    for i in range(length):
+        for n in range(segments):
+            s = n * length + i
+            at = slice(8 * s, 8 * s + 8)
+            alpha = jnp.where(s < depth, jnp.exp2(alpha_ref[at, :]), 0.0)
+            weight = trans[n] * alpha
+            alpha_ref[at, :] = alpha
+            weight_ref[at, :] = weight
+            trans[n] = trans[n] - weight
+            behind[n] = behind[n] + weight * pull_ref[at, :]
     starts, rest = [ones], [zeros]
     for n in range(1, segments):
         starts.append(starts[-1] * trans[n - 1])
         rest.insert(0, behind[segments - n] + trans[segments - n] * rest[0])
 
-    def backward(j, rest):
-        rest = list(rest)
-        for i in range(unroll):
-            for n in range(segments):
-                s = (n + 1) * length - 1 - (j * unroll + i)
-                at = pl.ds(pl.multiple_of(s * 8, 8), 8)
-                more = pull_ref[at, :] - rest[n]
-                rest[n] = rest[n] + alpha_ref[at, :] * more
-                weight = starts[n] * weight_ref[at, :]
-                weight_ref[at, :] = weight
-                pull_ref[at, :] = weight * more
-        return tuple(rest)
-
-    lax.fori_loop(0, length // unroll, backward, tuple(rest))
+    for i in range(length):
+        for n in range(segments):
+            s = (n + 1) * length - 1 - i
+            at = slice(8 * s, 8 * s + 8)
+            more = pull_ref[at, :] - rest[n]
+            rest[n] = rest[n] + alpha_ref[at, :] * more
+            weight = starts[n] * weight_ref[at, :]
+            weight_ref[at, :] = weight
+            pull_ref[at, :] = weight * more
 
     cots = {th: (ghi, gmid) for th, ghi, gmid in cots}
     for t in range(TILES):
@@ -528,12 +514,12 @@
 MIB = 1024 * 1024
 
 
-def call(kernel, outs, args, scratch=(), in_specs=None, out_specs=None, limit=24):
+def call(kernel, outs, args, scratch=(), in_specs=None, limit=24):
     return pl.pallas_call(
         kernel,
         out_shape=[jax.ShapeDtypeStruct(s, d) for s, d in outs],
         in_specs=in_specs or [VMEM] * len(args),
-        out_specs=out_specs or [VMEM] * len(outs),
+        out_specs=[VMEM] * len(outs),
         scratch_shapes=list(scratch),
         compiler_params=pltpu.CompilerParams(vmem_limit_bytes=limit * MIB),
     )(*args)
@@ -547,18 +533,17 @@
     return call(
         route_kernel,
         [
-            ((8, 128), F32), ((8, 128), F32), ((PEERS, 128), I32), ((8, TILES * SLOTS), I32), ((40 * PLANES, 128), F32),
+            ((8, 128), F32), ((8, 128), F32), ((PEERS, 128), I32), ((8, TILES * SLOTS), I32), ((36 * PLANES, 128), F32),
             ((16, SLOTS), F32), ((PEERS, 128), F32),
         ],
         (first_tile, owner, local, attributes, camera, depth, cot),
         [
             vmem(1, TILES * SLOTS, dtype=I32), vmem(TILES, SLOTS, dtype=I32), vmem(ATTR, G_DEV), vmem(1, 6),
-            vmem(TILES, SLOTS, dtype=I32), vmem(3, TILES, SLOTS), vmem(ATTR * 8, 128), vmem(40, 128),
-            vmem(40 * PLANES, 128), pltpu.SemaphoreType.DMA((7,)),
+            vmem(TILES, SLOTS, dtype=I32), vmem(3, TILES, SLOTS), vmem(ATTR * 8, 128), vmem(36, 128),
+            pltpu.SemaphoreType.DMA((6,)),
         ],
         [SMEM] + [HBM] * 6,
-        [VMEM] * 4 + [HBM] + [VMEM] * 2,
-        60,
+        limit=60,
     )
 
 
@@ -607,7 +592,7 @@
     near, far, inv, place, rows, kept, names = route(
         first_tile, owner, list_local[0], attributes, camera, term_depth[0], image_cot[0]
     )
-    rows = exchange(rows.reshape(PLANES, 40, 128), "dev", ALONG).reshape(PLANES * 40, 128)
+    rows = exchange(rows.reshape(PLANES, 1, 4608), "dev", ALONG).reshape(PLANES * 36, 128)
     far = lax.ppermute(far, "dev", [(d, d ^ 1) for d in range(OWNERS)])
     asked = lax.all_gather(jnp.concatenate([near, far]), "dev", axis_index_groups=WITHIN, tiled=True)
     sent, place, inv, kept, names = serve(first_tile, asked, rows, place, inv, kept, names)

time: 90.2 us -> 89 us (0.987)
  waiting for transfers between devices: 2.4 us -> 0.93 us
  blocking collectives: 58.5 us -> 59.9 us
  Pallas kernels: 8.94 us -> 7.78 us
    all_to_all x3, blocking collectives: 48.5 us -> 50 us  [exchange(): lax.all_to_all(x, axis, split_axis=0, concat_axis=0, tiled=True, axis_ind...]
    all_to_all x1, waiting for transfers between devices: 1.6 us -> 0.13 us  [exchange(): lax.all_to_all(x, axis, split_axis=0, concat_axis=0, tiled=True, axis_ind...]
    pallas_call x5, Pallas kernels: 8.94 us -> 7.78 us  [call(): pl.pallas_call(kernel, out_shape=[jax.ShapeDtypeStruct(s, d) for s, d in...]
where the time goes in v7:
time: 89 us; the launch traced here: 88.2 us
  blocking collectives  59.9 us (67%)
  starting transfers between devices  18.8 us (21%)
  Pallas kernels  7.78 us (9%)
  waiting for transfers between devices  0.93 us (1%)
    all_to_all x3, blocking collectives, exchange(): lax.all_to_all(x, axis, split_axis=0, concat_axis=0, tiled=True, axis_ind...  50 us
    all_to_all x1, starting transfers between devices, exchange(): lax.all_to_all(x, axis, split_axis=0, concat_axis=0, tiled=True, axis_ind...  15.9 us
    all_gather x1, blocking collectives, per_device(): lax.all_gather(jnp.concatenate([near, far]), 'dev', axis_index_groups=WIT...  9.93 us
    pallas_call x5, Pallas kernels, call(): pl.pallas_call(kernel, out_shape=[jax.ShapeDtypeStruct(s, d) for s, d in...  7.78 us
    ppermute x1, starting transfers between devices, per_device(): far = lax.ppermute(far, 'dev', [(d, d ^ 1) for d in range(OWNERS)])  2.86 us
  transfers between devices with their start and end apart: 2, of which 2 were waited for; matrix products, arithmetic and copies ran while one was open for 0% of the time, Pallas kernels for 0%

profile of v7, /device:TPU:1, one launch (start us, length us, event | category | flops | bytes accessed | tf_op | source)
XLA Modules:
  0.0 88.2 jit_solution(5557594725240252358)
XLA Ops:
  0.6 2.7 %shard_map.77 = (f32[8,128]{1,0:T(8,128)}, f32[8,128]{1,0:T(8,128)}, s32[32,128]{1,0:T(8,128)}, s32[8,1024]{1,0:T(8,128)}, f32[576,128]{1,0:T(8,128)}, /*index=5*/f32[16,256]{1,0:T(8,128)}, f32[32,128]{1,0:T(8,128)}) custom-call(s32[1]{0:T(128)} %bitcast.tile_ref, s32[1,1024]{1,0:T(1,128)} %bitcast.23, s32[4,256]{1,0:T(4,128)} %bitcast.24, ...), custom_call_target="tpu_custom_call" | custom-call | tf_op jit(solution)/shard_map/pallas_call | solution.py:518
  3.3 0.0 copy-start.6
  3.3 0.0 copy-start.5
  3.3 0.0 copy-start.4
  3.4 15.9 %all-to-all-start = ((f32[16,1,4608]{2,1,0:T(1,128)}), f32[16,1,4608]{2,1,0:T(1,128)S(1)}, u32[]{:S(2)}, u32[]{:S(2)}) async-start(f32[16,1,4608]{2,1,0:T(1,128)} %bitcast.21), calls=%async_computation | async-start | bytes 589824 | tf_op jit(solution)/shard_map/all_to_all | solution.py:579
  19.3 0.0 copy-done.6
  19.3 2.9 %collective-permute-start = (f32[8,128]{1,0:T(8,128)S(1)}, f32[8,128]{1,0:T(8,128)S(1)}, u32[]{:S(2)}, u32[]{:S(2)}) collective-permute-start(f32[8,128]{1,0:T(8,128)S(1)} %copy-done.6), channel_id=1, source_target_pairs={{0,1},{1,0},{2,3},{3,2},{4,5},{5,4},{6,7},{7,6},{8,9},{9,8},{10,11... | collective-permute-start | bytes 12296 | tf_op jit(solution)/shard_map/ppermute | solution.py:596
  22.1 0.8 collective-permute-done
  22.9 0.0 copy-done.5
  22.9 0.0 copy-start.1
  22.9 0.0 copy-start.2
  22.9 0.0 copy-start.3
  23.0 9.9 %all_gather.3.asked_ref = f32[64,128]{1,0:T(8,128)S(1)} all-gather(f32[16,128]{1,0:T(8,128)S(1)} %pad_maximum_fusion), channel_id=1, replica_groups={{0,2,4,6},{1,3,5,7},{8,10,12,14},{9,11,13,15},{16,18,20,22},{17,19,21,2..., dimensions={0}, use_global_device_ids=true | all-gather | bytes 40960 | tf_op jit(solution)/shard_map/all_gather | solution.py:597
  32.9 0.1 all-to-all-done
  33.0 0.0 copy-done.4
  33.0 0.0 copy-done.1
  33.0 0.0 copy-done.2
  33.0 0.0 copy-done.3
  33.0 0.8 shard_map.78
  33.8 15.6 %all_to_all.20 = f32[8,1,2304]{2,1,0:T(1,128)S(1)} all-to-all(f32[8,1,2304]{2,1,0:T(1,128)S(1)} %bitcast.20), channel_id=1, replica_groups={{0,1,2,3,4,5,6,7},{8,9,10,11,12,13,14,15},{16,17,18,19,20,21,22,23},{24..., dimensions={0} | all-to-all | bytes 147456 | tf_op jit(solution)/shard_map/all_to_all | solution.py:579
  49.4 2.4 %shard_map.79 = (f32[3,4,256]{2,1,0:T(4,128)S(1)}, f32[160,128]{1,0:T(8,128)S(1)}) custom-call(f32[144,128]{1,0:T(8,128)S(1)} %bitcast.18, s32[8,1024]{1,0:T(8,128)S(1)} %get-tuple-element.26.place_ref, s32[32,128]{1,0:T(8,128)S(1)} %get-tuple-element.27.inv_ref, f32[16,256]{1,0:T(8,128)S(1)} %get-tuple-element.28.kept_ref, ...), custom_call_target="tpu_custom_call" | custom-call | tf_op jit(solution)/shard_map/pallas_call | solution.py:518
  51.8 22.0 %all_to_all.21 = f32[32,1,640]{2,1,0:T(1,128)S(1)} all-to-all(f32[32,1,640]{2,1,0:T(1,128)S(1)} %bitcast.19), channel_id=1, replica_groups={{0,1,8,9,16,17,24,25,32,33,40,41,48,49,56,57,64,65,72,73,80,81,88,89,96..., dimensions={0} | all-to-all | bytes 163840 | tf_op jit(solution)/shard_map/all_to_all | solution.py:579
  73.9 0.8 shard_map.80
  74.7 0.0 copy-start
  74.7 12.3 %all_to_all.22 = f32[16,40,128]{2,1,0:T(8,128)S(1)} all-to-all(f32[16,40,128]{2,1,0:T(8,128)S(1)} %bitcast.15), channel_id=1, replica_groups={{0,2,4,6,128,130,132,134,256,258,260,262,384,386,388,390},{1,3,5,7,129,..., dimensions={0} | all-to-all | bytes 655360 | tf_op jit(solution)/shard_map/all_to_all | solution.py:579
  87.1 0.0 copy-done
  87.1 1.1 %shard_map.81 = (f32[59,512]{1,0:T(8,128)}, f32[3,4,256]{2,1,0:T(4,128)}) custom-call(f32[640,128]{1,0:T(8,128)S(1)} %bitcast.14, f32[59,512]{1,0:T(8,128)S(1)} %copy-done, f32[3,4,256]{2,1,0:T(4,128)S(1)} %get-tuple-element.31.image_in_ref), custom_call_target="tpu_custom_call" | custom-call | tf_op jit(solution)/shard_map/pallas_call | solution.py:518
  (1 shorter events, 0.0 us)
Async XLA Ops:
  3.3 15.9 %copy-start.6 = (f32[8,128]{1,0:T(8,128)S(1)}, f32[8,128]{1,0:T(8,128)}, u32[]{:S(2)}) copy-start(f32[8,128]{1,0:T(8,128)} %get-tuple-element.19) | copy-start | bytes 12292
  3.3 19.6 %copy-start.5 = (f32[8,128]{1,0:T(8,128)S(1)}, f32[8,128]{1,0:T(8,128)}, u32[]{:S(2)}) copy-start(f32[8,128]{1,0:T(8,128)} %get-tuple-element.18) | copy-start | bytes 12292
  3.3 29.7 %copy-start.4 = (f32[32,128]{1,0:T(8,128)S(1)}, f32[32,128]{1,0:T(8,128)}, u32[]{:S(2)}) copy-start(f32[32,128]{1,0:T(8,128)} %get-tuple-element.24.refs_3_) | copy-start | bytes 49156
  3.4 29.7 %all-to-all-start = ((f32[16,1,4608]{2,1,0:T(1,128)}), f32[16,1,4608]{2,1,0:T(1,128)S(1)}, u32[]{:S(2)}, u32[]{:S(2)}) async-start(f32[16,1,4608]{2,1,0:T(1,128)} %bitcast.21), calls=%async_computation | async-start | bytes 589824 | tf_op jit(solution)/shard_map/all_to_all | solution.py:579
  19.3 3.7 %collective-permute-start = (f32[8,128]{1,0:T(8,128)S(1)}, f32[8,128]{1,0:T(8,128)S(1)}, u32[]{:S(2)}, u32[]{:S(2)}) collective-permute-start(f32[8,128]{1,0:T(8,128)S(1)} %copy-done.6), channel_id=1, source_target_pairs={{0,1},{1,0},{2,3},{3,2},{4,5},{5,4},{6,7},{7,6},{8,9},{9,8},{10,11... | collective-permute-start | bytes 12296 | tf_op jit(solution)/shard_map/ppermute | solution.py:596
  22.9 10.1 %copy-start.1 = (s32[8,1024]{1,0:T(8,128)S(1)}, s32[8,1024]{1,0:T(8,128)}, u32[]{:S(2)}) copy-start(s32[8,1024]{1,0:T(8,128)} %get-tuple-element.21.refs_0_) | copy-start | bytes 98308
  22.9 10.1 %copy-start.2 = (s32[32,128]{1,0:T(8,128)S(1)}, s32[32,128]{1,0:T(8,128)}, u32[]{:S(2)}) copy-start(s32[32,128]{1,0:T(8,128)} %get-tuple-element.22.refs_1_) | copy-start | bytes 49156
  22.9 10.1 %copy-start.3 = (f32[16,256]{1,0:T(8,128)S(1)}, f32[16,256]{1,0:T(8,128)}, u32[]{:S(2)}) copy-start(f32[16,256]{1,0:T(8,128)} %get-tuple-element.23.refs_2_) | copy-start | bytes 49156
  74.7 12.4 %copy-start = (f32[59,512]{1,0:T(8,128)S(1)}, f32[59,512]{1,0:T(8,128)}, u32[]{:S(2)}) copy-start(f32[59,512]{1,0:T(8,128)} %attr_ref.1) | copy-start | bytes 362500

commit v8 on v7

--- a/solution.py
+++ b/solution.py
@@ -155,8 +155,8 @@
 
 def route_kernel(
     tile_ref, owner_hbm, local_hbm, attr_hbm, cam_hbm, depth_hbm, cot_hbm,
-    near_ref, far_ref, inv_ref, place_ref, rows_ref, kept_ref, names_ref,
-    owner_ref, local_ref, attr_ref, cam_ref, depth_ref, cot_ref, wide_ref, tmp_ref, sem,
+    near_ref, far_ref, inv_ref, place_ref, rows_hbm, kept_ref, names_ref,
+    owner_ref, local_ref, attr_ref, cam_ref, depth_ref, cot_ref, wide_ref, tmp_ref, rows_ref, sem,
 ):
     pairs = [
         (owner_hbm, owner_ref), (local_hbm, local_ref), (attr_hbm, attr_ref), (cam_hbm, cam_ref),
@@ -165,8 +165,8 @@
     copies = [pltpu.make_async_copy(src, dst, sem.at[n]) for n, (src, dst) in enumerate(pairs)]
     for copy in copies:
         copy.start()
-    for copy in copies:
-        copy.wait()
+    copies[2].wait()
+    copies[3].wait()
     spread_attributes(attr_ref, wide_ref)
     pos, logscale, quat, logit, sh = split_attributes(wide_ref)
     cam = [jnp.broadcast_to(cam_ref[:, j : j + 1], (8, 128)) for j in range(6)]
@@ -179,6 +179,10 @@
     rows = tmp_ref[...]
     for z in range(PLANES):
         rows_ref[36 * z : 36 * (z + 1), :] = rows
+    rows_copy = pltpu.make_async_copy(rows_ref, rows_hbm, sem.at[6])
+    rows_copy.start()
+    for n in (0, 1, 4, 5):
+        copies[n].wait()
     before = (
         lax.broadcasted_iota(I32, (SLOTS, SLOTS), 0) < lax.broadcasted_iota(I32, (SLOTS, SLOTS), 1)
     ).astype(F32).astype(BF16)
@@ -226,12 +230,13 @@
     kept_ref[12:13, 0:6] = cam_ref[...]
     for t in range(TILES):
         place_ref[3:4, SLOTS * t : SLOTS * (t + 1)] = depth_ref[t : t + 1, :]
-
-
-def serve_kernel(tile_ref, asked_ref, rows_ref, *refs):
-    kept, (out_ref, *outs) = refs[:4], refs[4:]
-    for src, dst in zip(kept, outs):
-        dst[...] = src[...]
+    rows_copy.wait()
+
+
+def serve_kernel(tile_ref, rows_ref, *refs):
+    asks, (out_ref, asked_ref) = refs[:NEAR], refs[NEAR:]
+    for k in range(NEAR):
+        asked_ref[16 * k : 16 * (k + 1), :] = asks[k][...]
     dev = tile_ref[0] // TILES
     core, mine = dev & 1, dev & 6
     lid = lax.broadcasted_iota(I32, (G_DEV, 256), 0)
@@ -247,7 +252,8 @@
         table = [x.astype(F32) for x in split3(jnp.concatenate(table, axis=1))]
         table = jnp.concatenate(table + [jnp.zeros((8, G_DEV), F32)], axis=0).astype(BF16)
         for r in range(0, RANKS, 2):
-            ids = [asked_ref[pl.ds(8 * r + 8 * (i ^ core) + mine + half, 1), :] for i in range(2)]
+            start_row = 16 * (((mine - r) >> 1) & (NEAR - 1)) + mine + half
+            ids = [asked_ref[pl.ds(start_row + 8 * (i ^ core), 1), :] for i in range(2)]
             hot = (lid == jnp.concatenate(ids, axis=1).astype(I32)).astype(F32).astype(BF16)
             got = dot(table, hot, 1, 0)
             got = got[0:72] + got[72:144] + got[144:216]
@@ -514,15 +520,19 @@
 MIB = 1024 * 1024
 
 
-def call(kernel, outs, args, scratch=(), in_specs=None, limit=24):
+def call(kernel, outs, args, scratch=(), in_specs=None, out_specs=None, limit=24):
     return pl.pallas_call(
         kernel,
         out_shape=[jax.ShapeDtypeStruct(s, d) for s, d in outs],
         in_specs=in_specs or [VMEM] * len(args),
-        out_specs=[VMEM] * len(outs),
+        out_specs=out_specs or [VMEM] * len(outs),
         scratch_shapes=list(scratch),
         compiler_params=pltpu.CompilerParams(vmem_limit_bytes=limit * MIB),
     )(*args)
+
+
+def in_hbm(x):
+    return pltpu.with_memory_space_constraint(x, pltpu.HBM)
 
 
 def vmem(*shape, dtype=F32):
@@ -536,20 +546,21 @@
             ((8, 128), F32), ((8, 128), F32), ((PEERS, 128), I32), ((8, TILES * SLOTS), I32), ((36 * PLANES, 128), F32),
             ((16, SLOTS), F32), ((PEERS, 128), F32),
         ],
-        (first_tile, owner, local, attributes, camera, depth, cot),
+        (first_tile, *[in_hbm(x) for x in (owner, local, attributes, camera, depth, cot)]),
         [
             vmem(1, TILES * SLOTS, dtype=I32), vmem(TILES, SLOTS, dtype=I32), vmem(ATTR, G_DEV), vmem(1, 6),
             vmem(TILES, SLOTS, dtype=I32), vmem(3, TILES, SLOTS), vmem(ATTR * 8, 128), vmem(36, 128),
-            pltpu.SemaphoreType.DMA((6,)),
+            vmem(36 * PLANES, 128), pltpu.SemaphoreType.DMA((7,)),
         ],
         [SMEM] + [HBM] * 6,
-        limit=60,
+        [VMEM] * 4 + [HBM] + [VMEM] * 2,
     )
 
 
-def serve(first_tile, asked, rows, *kept):
-    outs = [((18 * RANKS, 128), F32)] + [(k.shape, k.dtype) for k in kept]
-    return call(serve_kernel, outs, (first_tile, asked, rows, *kept), (), [SMEM] + [VMEM] * (2 + len(kept)))
+def serve(first_tile, rows, asks):
+    return call(
+        serve_kernel, [((18 * RANKS, 128), F32)], (first_tile, rows, *asks), [vmem(16 * NEAR, 128)], [SMEM] + [VMEM] * 5
+    )[0]
 
 
 def composite(got, place, inv, kept, names):
@@ -594,8 +605,10 @@
     )
     rows = exchange(rows.reshape(PLANES, 1, 4608), "dev", ALONG).reshape(PLANES * 36, 128)
     far = lax.ppermute(far, "dev", [(d, d ^ 1) for d in range(OWNERS)])
-    asked = lax.all_gather(jnp.concatenate([near, far]), "dev", axis_index_groups=WITHIN, tiled=True)
-    sent, place, inv, kept, names = serve(first_tile, asked, rows, place, inv, kept, names)
+    asks = [jnp.concatenate([near, far])]
+    for k in range(1, NEAR):
+        asks.append(lax.ppermute(asks[0], "dev", [(d, d // 8 * 8 + (d + 2 * k) % 8) for d in range(OWNERS)]))
+    sent = serve(first_tile, rows, asks)
     got = exchange(sent.reshape(RANKS, 1, 2304), "dev", PLANE).reshape(18 * RANKS, 128)
     image, grads = composite(got, place, inv, kept, names)
     back = exchange(grads.reshape(PEERS, 1, 640), "dev", ACROSS).reshape(5 * PEERS, 128)

time: 89 us -> 89.6 us (level)
  blocking collectives: 59.9 us -> 49 us
  starting transfers between devices: 18.8 us -> 29.3 us
  waiting for transfers between devices: 0.93 us -> 2.48 us
    ppermute x0 -> x3, starting transfers between devices: none -> 10.7 us  [per_device(): lax.ppermute(asks[0], 'dev', [(d, d // 8 * 8 + (d + 2 * k) % 8) for d in...]
    all_gather x1 -> x0, blocking collectives: 9.93 us -> none  [per_device(): lax.all_gather(jnp.concatenate([near, far]), 'dev', axis_index_groups=WIT...]
    ppermute x0 -> x3, waiting for transfers between devices: none -> 1.69 us  [per_device(): lax.ppermute(asks[0], 'dev', [(d, d // 8 * 8 + (d + 2 * k) % 8) for d in...]
    all_to_all x3, blocking collectives: 50 us -> 49 us  [exchange(): lax.all_to_all(x, axis, split_axis=0, concat_axis=0, tiled=True, axis_ind...]
  transfers between devices with their start and end apart: 2 -> 5, of which waited for: 2 -> 2; matrix products, arithmetic and copies ran while one was open for 0% -> 0% of each run, Pallas kernels for 0% -> 0%
where the time goes in v8:
time: 89.6 us; the launch traced here: 88.8 us
  blocking collectives  49 us (55%)
  starting transfers between devices  29.3 us (33%)
  Pallas kernels  7.28 us (8%)
  waiting for transfers between devices  2.48 us (3%)
    all_to_all x3, blocking collectives, exchange(): lax.all_to_all(x, axis, split_axis=0, concat_axis=0, tiled=True, axis_ind...  49 us
    all_to_all x1, starting transfers between devices, exchange(): lax.all_to_all(x, axis, split_axis=0, concat_axis=0, tiled=True, axis_ind...  15.8 us
    ppermute x3, starting transfers between devices, per_device(): lax.ppermute(asks[0], 'dev', [(d, d // 8 * 8 + (d + 2 * k) % 8) for d in...  10.7 us
    pallas_call x5, Pallas kernels, call(): pl.pallas_call(kernel, out_shape=[jax.ShapeDtypeStruct(s, d) for s, d in...  7.28 us
    ppermute x1, starting transfers between devices, per_device(): far = lax.ppermute(far, 'dev', [(d, d ^ 1) for d in range(OWNERS)])  2.87 us
  transfers between devices with their start and end apart: 5, of which 2 were waited for; matrix products, arithmetic and copies ran while one was open for 0% of the time, Pallas kernels for 0%

profile of v8, /device:TPU:1, one launch (start us, length us, event | category | flops | bytes accessed | tf_op | source)
XLA Modules:
  0.0 88.8 jit_solution(4660128100491380075)
XLA Ops:
  0.6 2.2 %shard_map.77 = (f32[8,128]{1,0:T(8,128)S(1)}, f32[8,128]{1,0:T(8,128)S(1)}, s32[32,128]{1,0:T(8,128)S(1)}, s32[8,1024]{1,0:T(8,128)S(1)}, f32[576,128]{1,0:T(8,...) custom-call(s32[1]{0:T(128)} %bitcast.tile_ref, s32[1,1024]{1,0:T(1,128)} %bitcast.22, s32[4,256]{1,0:T(4,128)} %bitcast.23, ...), custom_call_target="tpu_custom_call" | custom-call | tf_op jit(solution)/shard_map/pallas_call | solution.py:524
  2.8 15.8 %all-to-all-start = ((f32[16,1,4608]{2,1,0:T(1,128)}), f32[16,1,4608]{2,1,0:T(1,128)S(1)}, u32[]{:S(2)}, u32[]{:S(2)}) async-start(f32[16,1,4608]{2,1,0:T(1,128)} %bitcast.5), calls=%async_computation | async-start | bytes 589824 | tf_op jit(solution)/shard_map/all_to_all | solution.py:590
  18.6 2.9 %collective-permute-start = (f32[8,128]{1,0:T(8,128)S(1)}, f32[8,128]{1,0:T(8,128)S(1)}, u32[]{:S(2)}, u32[]{:S(2)}) collective-permute-start(f32[8,128]{1,0:T(8,128)S(1)} %get-tuple-element.15), channel_id=1, source_target_pairs={{0,1},{1,0},{2,3},{3,2},{4,5},{5,4},{6,7},{7,6},{8,9},{9,8},{10,11... | collective-permute-start | bytes 12296 | tf_op jit(solution)/shard_map/ppermute | solution.py:607
  21.5 0.8 collective-permute-done
  22.3 3.2 %collective-permute-start.1 = (f32[16,128]{1,0:T(8,128)S(1)}, f32[16,128]{1,0:T(8,128)S(1)}, u32[]{:S(2)}, u32[]{:S(2)}) collective-permute-start(f32[16,128]{1,0:T(8,128)S(1)} %constant_dynamic-update-slice_fusion.refs_0_), channel_id=1, source_target_pairs={{0,2},{1,3},{2,4},{3,5},{4,6},{5,7},{6,0},{7,1},{8,10},{9,11},{10,... | collective-permute-start | bytes 24584 | tf_op jit(solution)/shard_map/ppermute | solution.py:610
  25.5 4.5 %collective-permute-start.2 = (f32[16,128]{1,0:T(8,128)S(1)}, f32[16,128]{1,0:T(8,128)S(1)}, u32[]{:S(2)}, u32[]{:S(2)}) collective-permute-start(f32[16,128]{1,0:T(8,128)S(1)} %constant_dynamic-update-slice_fusion.refs_0_), channel_id=1, source_target_pairs={{0,4},{1,5},{2,6},{3,7},{4,0},{5,1},{6,2},{7,3},{8,12},{9,13},{10,... | collective-permute-start | bytes 24584 | tf_op jit(solution)/shard_map/ppermute | solution.py:610
  30.0 3.0 %collective-permute-start.3 = (f32[16,128]{1,0:T(8,128)S(1)}, f32[16,128]{1,0:T(8,128)S(1)}, u32[]{:S(2)}, u32[]{:S(2)}) collective-permute-start(f32[16,128]{1,0:T(8,128)S(1)} %constant_dynamic-update-slice_fusion.refs_0_), channel_id=1, source_target_pairs={{0,6},{1,7},{2,0},{3,1},{4,2},{5,3},{6,4},{7,5},{8,14},{9,15},{10,... | collective-permute-start | bytes 24584 | tf_op jit(solution)/shard_map/ppermute | solution.py:610
  33.0 0.0 collective-permute-done.1.refs_1_
  33.0 0.0 collective-permute-done.2.refs_2_
  33.0 1.7 %collective-permute-done.3.refs_3_ = f32[16,128]{1,0:T(8,128)S(1)} collective-permute-done((f32[16,128]{1,0:T(8,128)S(1)}, f32[16,128]{1,0:T(8,128)S(1)}, u32[]{:S(2)}, u32[]{:S(2)}) %collective-permute-start.3) | collective-permute-done | bytes 8224 | tf_op jit(solution)/shard_map/ppermute | solution.py:610
  34.7 0.0 all-to-all-done
  34.7 0.7 shard_map.78
  35.5 13.3 %all_to_all.20 = f32[8,1,2304]{2,1,0:T(1,128)S(1)} all-to-all(f32[8,1,2304]{2,1,0:T(1,128)S(1)} %bitcast.19), channel_id=1, replica_groups={{0,1,2,3,4,5,6,7},{8,9,10,11,12,13,14,15},{16,17,18,19,20,21,22,23},{24..., dimensions={0} | all-to-all | bytes 147456 | tf_op jit(solution)/shard_map/all_to_all | solution.py:590
  48.7 2.4 %shard_map.79 = (f32[3,4,256]{2,1,0:T(4,128)S(1)}, f32[160,128]{1,0:T(8,128)S(1)}) custom-call(f32[144,128]{1,0:T(8,128)S(1)} %bitcast.18, s32[8,1024]{1,0:T(8,128)S(1)} %get-tuple-element.16.place_ref, s32[32,128]{1,0:T(8,128)S(1)} %get-tuple-element.17.inv_ref, f32[16,256]{1,0:T(8,128)S(1)} %get-tuple-element.18.kept_ref, ...), custom_call_target="tpu_custom_call" | custom-call | tf_op jit(solution)/shard_map/pallas_call | solution.py:524
  51.1 23.4 %all_to_all.21 = f32[32,1,640]{2,1,0:T(1,128)S(1)} all-to-all(f32[32,1,640]{2,1,0:T(1,128)S(1)} %bitcast.20), channel_id=1, replica_groups={{0,1,8,9,16,17,24,25,32,33,40,41,48,49,56,57,64,65,72,73,80,81,88,89,96..., dimensions={0} | all-to-all | bytes 163840 | tf_op jit(solution)/shard_map/all_to_all | solution.py:590
  74.5 0.8 shard_map.80
  75.3 0.0 copy-start
  75.3 12.3 %all_to_all.22 = f32[16,40,128]{2,1,0:T(8,128)S(1)} all-to-all(f32[16,40,128]{2,1,0:T(8,128)S(1)} %bitcast.15), channel_id=1, replica_groups={{0,2,4,6,128,130,132,134,256,258,260,262,384,386,388,390},{1,3,5,7,129,..., dimensions={0} | all-to-all | bytes 655360 | tf_op jit(solution)/shard_map/all_to_all | solution.py:590
  87.7 0.0 copy-done
  87.7 1.1 %shard_map.81 = (f32[59,512]{1,0:T(8,128)}, f32[3,4,256]{2,1,0:T(4,128)}) custom-call(f32[640,128]{1,0:T(8,128)S(1)} %bitcast.14, f32[59,512]{1,0:T(8,128)S(1)} %copy-done, f32[3,4,256]{2,1,0:T(4,128)S(1)} %get-tuple-element.21.image_in_ref), custom_call_target="tpu_custom_call" | custom-call | tf_op jit(solution)/shard_map/pallas_call | solution.py:524
  (2 shorter events, 0.0 us)
Async XLA Ops:
  2.8 31.9 %all-to-all-start = ((f32[16,1,4608]{2,1,0:T(1,128)}), f32[16,1,4608]{2,1,0:T(1,128)S(1)}, u32[]{:S(2)}, u32[]{:S(2)}) async-start(f32[16,1,4608]{2,1,0:T(1,128)} %bitcast.5), calls=%async_computation | async-start | bytes 589824 | tf_op jit(solution)/shard_map/all_to_all | solution.py:590
  18.6 3.7 %collective-permute-start = (f32[8,128]{1,0:T(8,128)S(1)}, f32[8,128]{1,0:T(8,128)S(1)}, u32[]{:S(2)}, u32[]{:S(2)}) collective-permute-start(f32[8,128]{1,0:T(8,128)S(1)} %get-tuple-element.15), channel_id=1, source_target_pairs={{0,1},{1,0},{2,3},{3,2},{4,5},{5,4},{6,7},{7,6},{8,9},{9,8},{10,11... | collective-permute-start | bytes 12296 | tf_op jit(solution)/shard_map/ppermute | solution.py:607
  22.3 10.7 %collective-permute-start.1 = (f32[16,128]{1,0:T(8,128)S(1)}, f32[16,128]{1,0:T(8,128)S(1)}, u32[]{:S(2)}, u32[]{:S(2)}) collective-permute-start(f32[16,128]{1,0:T(8,128)S(1)} %constant_dynamic-update-slice_fusion.refs_0_), channel_id=1, source_target_pairs={{0,2},{1,3},{2,4},{3,5},{4,6},{5,7},{6,0},{7,1},{8,10},{9,11},{10,... | collective-permute-start | bytes 24584 | tf_op jit(solution)/shard_map/ppermute | solution.py:610
  25.5 7.5 %collective-permute-start.2 = (f32[16,128]{1,0:T(8,128)S(1)}, f32[16,128]{1,0:T(8,128)S(1)}, u32[]{:S(2)}, u32[]{:S(2)}) collective-permute-start(f32[16,128]{1,0:T(8,128)S(1)} %constant_dynamic-update-slice_fusion.refs_0_), channel_id=1, source_target_pairs={{0,4},{1,5},{2,6},{3,7},{4,0},{5,1},{6,2},{7,3},{8,12},{9,13},{10,... | collective-permute-start | bytes 24584 | tf_op jit(solution)/shard_map/ppermute | solution.py:610
  30.0 4.7 %collective-permute-start.3 = (f32[16,128]{1,0:T(8,128)S(1)}, f32[16,128]{1,0:T(8,128)S(1)}, u32[]{:S(2)}, u32[]{:S(2)}) collective-permute-start(f32[16,128]{1,0:T(8,128)S(1)} %constant_dynamic-update-slice_fusion.refs_0_), channel_id=1, source_target_pairs={{0,6},{1,7},{2,0},{3,1},{4,2},{5,3},{6,4},{7,5},{8,14},{9,15},{10,... | collective-permute-start | bytes 24584 | tf_op jit(solution)/shard_map/ppermute | solution.py:610
  75.3 12.3 %copy-start = (f32[59,512]{1,0:T(8,128)S(1)}, f32[59,512]{1,0:T(8,128)}, u32[]{:S(2)}) copy-start(f32[59,512]{1,0:T(8,128)} %attr_ref.1) | copy-start | bytes 362500

commit v9 on v8

--- a/solution.py
+++ b/solution.py
@@ -155,7 +155,7 @@
 
 def route_kernel(
     tile_ref, owner_hbm, local_hbm, attr_hbm, cam_hbm, depth_hbm, cot_hbm,
-    near_ref, far_ref, inv_ref, place_ref, rows_hbm, kept_ref, names_ref,
+    asked_ref, inv_ref, place_ref, rows_hbm, kept_ref, names_ref,
     owner_ref, local_ref, attr_ref, cam_ref, depth_ref, cot_ref, wide_ref, tmp_ref, rows_ref, sem,
 ):
     pairs = [
@@ -194,7 +194,6 @@
     gid = lax.broadcasted_iota(I32, (2 * RANKS, SLOTS), 0)
     table = jnp.zeros((4 * PEERS, 128), F32)
     request = jnp.zeros((4 * RANKS, 128), F32)
-    core = (tile_ref[0] // TILES) & 1
     for t in range(TILES):
         owner = owner_ref[:, SLOTS * t : SLOTS * (t + 1)]
         hot = (oid == owner).astype(F32)
@@ -209,7 +208,7 @@
         lanes = ((owner >> 3) & 7) * CAP + rank
         place_ref[0:1, SLOTS * t : SLOTS * (t + 1)] = group
         place_ref[1:2, SLOTS * t : SLOTS * (t + 1)] = lanes
-        hot_group = (gid == ((owner & 1) ^ core) * 8 + (owner & 6) + (owner >> 6)).astype(F32)
+        hot_group = (gid == group).astype(F32)
         vals = jnp.concatenate([hot_group * p.astype(F32) for p in local_parts], axis=0).astype(BF16)
         request = request + dot(vals, (oid == lanes).astype(F32).astype(BF16), 1, 1)
         peer = (owner >> 3) * 2 + (owner & 1)
@@ -220,8 +219,7 @@
         table = table + dot(vals, ((oid & 63) == lanes).astype(F32).astype(BF16), 1, 1)
     place_ref[2:3, :] = jnp.full((1, TILES * SLOTS), tile_ref[0], I32)
     n = PEERS
-    near_ref[...] = request[0:8] + 256.0 * request[16:24]
-    far_ref[...] = request[8:16] + 256.0 * request[24:32]
+    asked_ref[...] = request[0 : 2 * RANKS] + 256.0 * request[2 * RANKS :]
     names_ref[...] = table[0:n] + 256.0 * table[n : 2 * n]
     inv_ref[...] = (table[2 * n : 3 * n] + 256.0 * table[3 * n :]).astype(I32)
     for c in range(3):
@@ -233,12 +231,8 @@
     rows_copy.wait()
 
 
-def serve_kernel(tile_ref, rows_ref, *refs):
-    asks, (out_ref, asked_ref) = refs[:NEAR], refs[NEAR:]
-    for k in range(NEAR):
-        asked_ref[16 * k : 16 * (k + 1), :] = asks[k][...]
-    dev = tile_ref[0] // TILES
-    core, mine = dev & 1, dev & 6
+def serve_kernel(tile_ref, asked_ref, rows_ref, out_ref):
+    mine = 2 * ((tile_ref[0] // TILES) & (RANKS - 1))
     lid = lax.broadcasted_iota(I32, (G_DEV, 256), 0)
     sub = lax.broadcasted_iota(I32, (8, 128), 0)
     near = lax.broadcasted_iota(I32, (8, 128), 1) >> 4
@@ -252,8 +246,7 @@
         table = [x.astype(F32) for x in split3(jnp.concatenate(table, axis=1))]
         table = jnp.concatenate(table + [jnp.zeros((8, G_DEV), F32)], axis=0).astype(BF16)
         for r in range(0, RANKS, 2):
-            start_row = 16 * (((mine - r) >> 1) & (NEAR - 1)) + mine + half
-            ids = [asked_ref[pl.ds(start_row + 8 * (i ^ core), 1), :] for i in range(2)]
+            ids = [asked_ref[pl.ds(16 * (r + i) + mine + half, 1), :] for i in range(2)]
             hot = (lid == jnp.concatenate(ids, axis=1).astype(I32)).astype(F32).astype(BF16)
             got = dot(table, hot, 1, 0)
             got = got[0:72] + got[72:144] + got[144:216]
@@ -543,7 +536,7 @@
     return call(
         route_kernel,
         [
-            ((8, 128), F32), ((8, 128), F32), ((PEERS, 128), I32), ((8, TILES * SLOTS), I32), ((36 * PLANES, 128), F32),
+            ((2 * RANKS, 128), F32), ((PEERS, 128), I32), ((8, TILES * SLOTS), I32), ((36 * PLANES, 128), F32),
             ((16, SLOTS), F32), ((PEERS, 128), F32),
         ],
         (first_tile, *[in_hbm(x) for x in (owner, local, attributes, camera, depth, cot)]),
@@ -553,13 +546,13 @@
             vmem(36 * PLANES, 128), pltpu.SemaphoreType.DMA((7,)),
         ],
         [SMEM] + [HBM] * 6,
-        [VMEM] * 4 + [HBM] + [VMEM] * 2,
+        [VMEM] * 3 + [HBM] + [VMEM] * 2,
     )
 
 
-def serve(first_tile, rows, asks):
+def serve(first_tile, asked, rows):
     return call(
-        serve_kernel, [((18 * RANKS, 128), F32)], (first_tile, rows, *asks), [vmem(16 * NEAR, 128)], [SMEM] + [VMEM] * 5
+        serve_kernel, [((18 * RANKS, 128), F32)], (first_tile, asked, rows), (), [SMEM] + [VMEM] * 2
     )[0]
 
 
@@ -600,15 +593,12 @@
 def per_device(attributes, camera, list_owner, list_local, term_depth, image_cot):
     owner = list_owner.reshape(1, -1)
     first_tile = (lax.axis_index("dev") * TILES).astype(I32).reshape(1)
-    near, far, inv, place, rows, kept, names = route(
+    asked, inv, place, rows, kept, names = route(
         first_tile, owner, list_local[0], attributes, camera, term_depth[0], image_cot[0]
     )
     rows = exchange(rows.reshape(PLANES, 1, 4608), "dev", ALONG).reshape(PLANES * 36, 128)
-    far = lax.ppermute(far, "dev", [(d, d ^ 1) for d in range(OWNERS)])
-    asks = [jnp.concatenate([near, far])]
-    for k in range(1, NEAR):
-        asks.append(lax.ppermute(asks[0], "dev", [(d, d // 8 * 8 + (d + 2 * k) % 8) for d in range(OWNERS)]))
-    sent = serve(first_tile, rows, asks)
+    asked = lax.all_gather(asked, "dev", axis_index_groups=PLANE, tiled=True)
+    sent = serve(first_tile, asked, rows)
     got = exchange(sent.reshape(RANKS, 1, 2304), "dev", PLANE).reshape(18 * RANKS, 128)
     image, grads = composite(got, place, inv, kept, names)
     back = exchange(grads.reshape(PEERS, 1, 640), "dev", ACROSS).reshape(5 * PEERS, 128)

time: 89.6 us -> 86.8 us (0.969)
  starting transfers between devices: 29.3 us -> 15.8 us
  blocking collectives: 49 us -> 62.3 us
  waiting for transfers between devices: 2.48 us -> 0.01 us
    all_gather x0 -> x1, blocking collectives: none -> 14 us  [per_device(): asked = lax.all_gather(asked, 'dev', axis_index_groups=PLANE, tiled=True)]
    ppermute x4 -> x0, starting transfers between devices: 13.6 us -> none  [the longest x3 10.7 us: per_device(): lax.ppermute(asks[0], 'dev', [(d, d // 8 * 8 + (d + 2 * k) % 8) for d in...]
    ppermute x4 -> x0, waiting for transfers between devices: 2.48 us -> none  [the longest x3 1.69 us: per_device(): lax.ppermute(asks[0], 'dev', [(d, d // 8 * 8 + (d + 2 * k) % 8) for d in...]
  transfers between devices with their start and end apart: 5 -> 1, of which waited for: 2 -> 0; matrix products, arithmetic and copies ran while one was open for 0% -> 0% of each run, Pallas kernels for 0% -> 0%
where the time goes in v9:
time: 86.8 us; the launch traced here: 86.1 us
  blocking collectives  62.3 us (72%)
  starting transfers between devices  15.8 us (18%)
  Pallas kernels  7.31 us (8%)
    all_to_all x3, blocking collectives, exchange(): lax.all_to_all(x, axis, split_axis=0, concat_axis=0, tiled=True, axis_ind...  48.3 us
    all_to_all x1, starting transfers between devices, exchange(): lax.all_to_all(x, axis, split_axis=0, concat_axis=0, tiled=True, axis_ind...  15.8 us
    all_gather x1, blocking collectives, per_device(): asked = lax.all_gather(asked, 'dev', axis_index_groups=PLANE, tiled=True)  14 us
    pallas_call x5, Pallas kernels, call(): pl.pallas_call(kernel, out_shape=[jax.ShapeDtypeStruct(s, d) for s, d in...  7.31 us
  transfers between devices with their start and end apart: 1, of which 0 were waited for; matrix products, arithmetic and copies ran while one was open for 0% of the time, Pallas kernels for 0%

profile of v9, /device:TPU:1, one launch (start us, length us, event | category | flops | bytes accessed | tf_op | source)
XLA Modules:
  0.0 86.1 jit_solution(13380534357606149052)
XLA Ops:
  0.6 2.2 %shard_map.77 = (f32[16,128]{1,0:T(8,128)S(1)}, s32[32,128]{1,0:T(8,128)S(1)}, s32[8,1024]{1,0:T(8,128)S(1)}, f32[576,128]{1,0:T(8,128)}, f32[16,256]{1,0:T(8,128)S(1)}, /*index=5*/f32[32,128]{1,0:T(8,128)S(1)}) custom-call(s32[1]{0:T(128)} %bitcast.tile_ref, s32[1,1024]{1,0:T(1,128)} %bitcast.22, s32[4,256]{1,0:T(4,128)} %bitcast.23, f32[59,512]{1,0:T(8,128)} %attr_ref.1, ...), custom_call_target="tpu_custom_call" | custom-call | tf_op jit(solution)/shard_map/pallas_call | solution.py:517
  2.9 15.8 %all-to-all-start = ((f32[16,1,4608]{2,1,0:T(1,128)}), f32[16,1,4608]{2,1,0:T(1,128)S(1)}, u32[]{:S(2)}, u32[]{:S(2)}) async-start(f32[16,1,4608]{2,1,0:T(1,128)} %bitcast.5), calls=%async_computation | async-start | bytes 589824 | tf_op jit(solution)/shard_map/all_to_all | solution.py:583
  18.6 14.0 %all_gather.3.asked_ref = f32[128,128]{1,0:T(8,128)S(1)} all-gather(f32[16,128]{1,0:T(8,128)S(1)} %get-tuple-element.12), channel_id=1, replica_groups={{0,1,2,3,4,5,6,7},{8,9,10,11,12,13,14,15},{16,17,18,19,20,21,22,23},{24..., dimensions={0}, use_global_device_ids=true | all-gather | bytes 73728 | tf_op jit(solution)/shard_map/all_gather | solution.py:600
  32.7 0.0 all-to-all-done
  32.7 0.8 shard_map.78
  33.4 15.4 %all_to_all.20 = f32[8,1,2304]{2,1,0:T(1,128)S(1)} all-to-all(f32[8,1,2304]{2,1,0:T(1,128)S(1)} %bitcast.19), channel_id=1, replica_groups={{0,1,2,3,4,5,6,7},{8,9,10,11,12,13,14,15},{16,17,18,19,20,21,22,23},{24..., dimensions={0} | all-to-all | bytes 147456 | tf_op jit(solution)/shard_map/all_to_all | solution.py:583
  48.8 2.4 %shard_map.79 = (f32[3,4,256]{2,1,0:T(4,128)S(1)}, f32[160,128]{1,0:T(8,128)S(1)}) custom-call(f32[144,128]{1,0:T(8,128)S(1)} %bitcast.18, s32[8,1024]{1,0:T(8,128)S(1)} %get-tuple-element.14.place_ref, s32[32,128]{1,0:T(8,128)S(1)} %get-tuple-element.15.inv_ref, f32[16,256]{1,0:T(8,128)S(1)} %get-tuple-element.16.kept_ref, ...), custom_call_target="tpu_custom_call" | custom-call | tf_op jit(solution)/shard_map/pallas_call | solution.py:517
  51.2 20.6 %all_to_all.21 = f32[32,1,640]{2,1,0:T(1,128)S(1)} all-to-all(f32[32,1,640]{2,1,0:T(1,128)S(1)} %bitcast.20), channel_id=1, replica_groups={{0,1,8,9,16,17,24,25,32,33,40,41,48,49,56,57,64,65,72,73,80,81,88,89,96..., dimensions={0} | all-to-all | bytes 163840 | tf_op jit(solution)/shard_map/all_to_all | solution.py:583
  71.8 0.9 shard_map.80
  72.6 0.0 copy-start
  72.6 12.3 %all_to_all.22 = f32[16,40,128]{2,1,0:T(8,128)S(1)} all-to-all(f32[16,40,128]{2,1,0:T(8,128)S(1)} %bitcast.15), channel_id=1, replica_groups={{0,2,4,6,128,130,132,134,256,258,260,262,384,386,388,390},{1,3,5,7,129,..., dimensions={0} | all-to-all | bytes 655360 | tf_op jit(solution)/shard_map/all_to_all | solution.py:583
  85.0 0.0 copy-done
  85.0 1.1 %shard_map.81 = (f32[59,512]{1,0:T(8,128)}, f32[3,4,256]{2,1,0:T(4,128)}) custom-call(f32[640,128]{1,0:T(8,128)S(1)} %bitcast.14, f32[59,512]{1,0:T(8,128)S(1)} %copy-done, f32[3,4,256]{2,1,0:T(4,128)S(1)} %get-tuple-element.19.image_in_ref), custom_call_target="tpu_custom_call" | custom-call | tf_op jit(solution)/shard_map/pallas_call | solution.py:517
Async XLA Ops:
  2.9 29.8 %all-to-all-start = ((f32[16,1,4608]{2,1,0:T(1,128)}), f32[16,1,4608]{2,1,0:T(1,128)S(1)}, u32[]{:S(2)}, u32[]{:S(2)}) async-start(f32[16,1,4608]{2,1,0:T(1,128)} %bitcast.5), calls=%async_computation | async-start | bytes 589824 | tf_op jit(solution)/shard_map/all_to_all | solution.py:583
  72.6 12.3 %copy-start = (f32[59,512]{1,0:T(8,128)S(1)}, f32[59,512]{1,0:T(8,128)}, u32[]{:S(2)}) copy-start(f32[59,512]{1,0:T(8,128)} %attr_ref.1) | copy-start | bytes 362500

commit v10 on v9

--- a/solution.py
+++ b/solution.py
@@ -14,7 +14,8 @@
 NEAR = 4
 PLANES = 16
 RANKS = 8
-SEGMENTS = 4
+SEGMENTS = 8
+RING = (0, 2, 4, 6, 7, 5, 3, 1)
 G_DEV = 512
 ATTR = 59
 VIEWS = 4
@@ -233,7 +234,7 @@
 
 def serve_kernel(tile_ref, asked_ref, rows_ref, out_ref):
     mine = 2 * ((tile_ref[0] // TILES) & (RANKS - 1))
-    lid = lax.broadcasted_iota(I32, (G_DEV, 256), 0)
+    lid = lax.broadcasted_iota(I32, (G_DEV, 256), 0).astype(jnp.int16)
     sub = lax.broadcasted_iota(I32, (8, 128), 0)
     near = lax.broadcasted_iota(I32, (8, 128), 1) >> 4
     for half in range(2):
@@ -246,8 +247,8 @@
         table = [x.astype(F32) for x in split3(jnp.concatenate(table, axis=1))]
         table = jnp.concatenate(table + [jnp.zeros((8, G_DEV), F32)], axis=0).astype(BF16)
         for r in range(0, RANKS, 2):
-            ids = [asked_ref[pl.ds(16 * (r + i) + mine + half, 1), :] for i in range(2)]
-            hot = (lid == jnp.concatenate(ids, axis=1).astype(I32)).astype(F32).astype(BF16)
+            ids = [asked_ref[pl.ds(16 * RING.index(r + i) + mine + half, 1), :] for i in range(2)]
+            hot = one_hot(lid, jnp.concatenate(ids, axis=1).astype(I32))
             got = dot(table, hot, 1, 0)
             got = got[0:72] + got[72:144] + got[144:216]
             for i in range(2):
@@ -259,6 +260,12 @@
                 out_ref[at : at + 8, :] = main
                 last = jnp.sum(jnp.where(near == sub, part[64:72], 0.0), axis=0, keepdims=True)
                 out_ref[at + 8 : at + 9, :] = last
+
+
+def one_hot(lid, ids):
+    ids = jnp.broadcast_to(ids, (16, 256)).astype(jnp.int16)
+    same = lid == jnp.concatenate([ids] * (G_DEV // 16), axis=0)
+    return jnp.where(same, jnp.ones(lid.shape, BF16), jnp.zeros(lid.shape, BF16))
 
 
 def pair_ids(back_ref, n):
@@ -436,13 +443,13 @@
 
 
 def collect_kernel(back_ref, kept_ref, out_ref):
-    lid = lax.broadcasted_iota(I32, (G_DEV, 256), 0)
+    lid = lax.broadcasted_iota(I32, (G_DEV, 256), 0).astype(jnp.int16)
     sub = lax.broadcasted_iota(I32, (8, 128), 0)
     lane = lax.broadcasted_iota(I32, (8, 128), 1)
     near, left = (lane & 63) >> 4, lane < 64
     acc = jnp.zeros((80, G_DEV), F32)
     for n in range(0, PEERS, 4):
-        hot = (lid == pair_ids(back_ref, n)).astype(F32).astype(BF16)
+        hot = one_hot(lid, pair_ids(back_ref, n))
         pairs = []
         for i in range(2):
             at = 5 * (n + 2 * i)
@@ -585,6 +592,7 @@
 
 ALONG = [[8 * z + r for z in range(PLANES)] for r in range(RANKS)]
 PLANE = [[8 * z + r for r in range(RANKS)] for z in range(PLANES)]
+AROUND = [[8 * z + r for r in RING] for z in range(PLANES)]
 ACROSS = [[8 * z + 2 * y + c for z in range(PLANES) for c in range(2)] for y in range(NEAR)]
 WITHIN = [[8 * z + 2 * y + c for y in range(NEAR)] for z in range(PLANES) for c in range(2)]
 VIEWS_WITHIN = [[OWNERS * v + d for v in range(VIEWS) for d in group] for group in WITHIN]
@@ -597,7 +605,7 @@
         first_tile, owner, list_local[0], attributes, camera, term_depth[0], image_cot[0]
     )
     rows = exchange(rows.reshape(PLANES, 1, 4608), "dev", ALONG).reshape(PLANES * 36, 128)
-    asked = lax.all_gather(asked, "dev", axis_index_groups=PLANE, tiled=True)
+    asked = lax.all_gather(asked, "dev", axis_index_groups=AROUND, tiled=True)
     sent = serve(first_tile, asked, rows)
     got = exchange(sent.reshape(RANKS, 1, 2304), "dev", PLANE).reshape(18 * RANKS, 128)
     image, grads = composite(got, place, inv, kept, names)

time: 86.8 us -> 92.8 us (1.069)
  blocking collectives: 62.3 us -> 68.5 us
    all_gather x1, blocking collectives: 14 us -> 20.1 us  [per_device(): asked = lax.all_gather(asked, 'dev', axis_index_groups=AROUND, tiled=True)]
where the time goes in v10:
time: 92.8 us; the launch traced here: 92.1 us
  blocking collectives  68.5 us (74%)
  starting transfers between devices  15.8 us (17%)
  Pallas kernels  7.18 us (8%)
    all_to_all x3, blocking collectives, exchange(): lax.all_to_all(x, axis, split_axis=0, concat_axis=0, tiled=True, axis_ind...  48.4 us
    all_gather x1, blocking collectives, per_device(): asked = lax.all_gather(asked, 'dev', axis_index_groups=AROUND, tiled=True)  20.1 us
    all_to_all x1, starting transfers between devices, exchange(): lax.all_to_all(x, axis, split_axis=0, concat_axis=0, tiled=True, axis_ind...  15.8 us
    pallas_call x5, Pallas kernels, call(): pl.pallas_call(kernel, out_shape=[jax.ShapeDtypeStruct(s, d) for s, d in...  7.18 us
  transfers between devices with their start and end apart: 1, of which 0 were waited for; matrix products, arithmetic and copies ran while one was open for 0% of the time, Pallas kernels for 0%

profile of v10, /device:TPU:1, one launch (start us, length us, event | category | flops | bytes accessed | tf_op | source)
XLA Modules:
  0.0 92.1 jit_solution(5492119586922192533)
XLA Ops:
  0.6 2.2 %shard_map.77 = (f32[16,128]{1,0:T(8,128)S(1)}, s32[32,128]{1,0:T(8,128)S(1)}, s32[8,1024]{1,0:T(8,128)S(1)}, f32[576,128]{1,0:T(8,128)}, f32[16,256]{1,0:T(8,128)S(1)}, /*index=5*/f32[32,128]{1,0:T(8,128)S(1)}) custom-call(s32[1]{0:T(128)} %bitcast.tile_ref, s32[1,1024]{1,0:T(1,128)} %bitcast.22, s32[4,256]{1,0:T(4,128)} %bitcast.23, f32[59,512]{1,0:T(8,128)} %attr_ref.1, ...), custom_call_target="tpu_custom_call" | custom-call | tf_op jit(solution)/shard_map/pallas_call | solution.py:524
  2.9 15.8 %all-to-all-start = ((f32[16,1,4608]{2,1,0:T(1,128)}), f32[16,1,4608]{2,1,0:T(1,128)S(1)}, u32[]{:S(2)}, u32[]{:S(2)}) async-start(f32[16,1,4608]{2,1,0:T(1,128)} %bitcast.5), calls=%async_computation | async-start | bytes 589824 | tf_op jit(solution)/shard_map/all_to_all | solution.py:590
  18.6 20.1 %all_gather.3.asked_ref = f32[128,128]{1,0:T(8,128)S(1)} all-gather(f32[16,128]{1,0:T(8,128)S(1)} %get-tuple-element.12), channel_id=1, replica_groups={{0,2,4,6,7,5,3,1},{8,10,12,14,15,13,11,9},{16,18,20,22,23,21,19,17},{24..., dimensions={0}, use_global_device_ids=true | all-gather | bytes 73728 | tf_op jit(solution)/shard_map/all_gather | solution.py:608
  38.8 0.0 all-to-all-done
  38.8 0.7 shard_map.78
  39.4 9.7 %all_to_all.20 = f32[8,1,2304]{2,1,0:T(1,128)S(1)} all-to-all(f32[8,1,2304]{2,1,0:T(1,128)S(1)} %bitcast.19), channel_id=1, replica_groups={{0,1,2,3,4,5,6,7},{8,9,10,11,12,13,14,15},{16,17,18,19,20,21,22,23},{24..., dimensions={0} | all-to-all | bytes 147456 | tf_op jit(solution)/shard_map/all_to_all | solution.py:590
  49.1 2.3 %shard_map.79 = (f32[3,4,256]{2,1,0:T(4,128)S(1)}, f32[160,128]{1,0:T(8,128)S(1)}) custom-call(f32[144,128]{1,0:T(8,128)S(1)} %bitcast.18, s32[8,1024]{1,0:T(8,128)S(1)} %get-tuple-element.14.place_ref, s32[32,128]{1,0:T(8,128)S(1)} %get-tuple-element.15.inv_ref, f32[16,256]{1,0:T(8,128)S(1)} %get-tuple-element.16.kept_ref, ...), custom_call_target="tpu_custom_call" | custom-call | tf_op jit(solution)/shard_map/pallas_call | solution.py:524
  51.5 26.4 %all_to_all.21 = f32[32,1,640]{2,1,0:T(1,128)S(1)} all-to-all(f32[32,1,640]{2,1,0:T(1,128)S(1)} %bitcast.20), channel_id=1, replica_groups={{0,1,8,9,16,17,24,25,32,33,40,41,48,49,56,57,64,65,72,73,80,81,88,89,96..., dimensions={0} | all-to-all | bytes 163840 | tf_op jit(solution)/shard_map/all_to_all | solution.py:590
  77.8 0.8 shard_map.80
  78.7 0.0 copy-start
  78.7 12.3 %all_to_all.22 = f32[16,40,128]{2,1,0:T(8,128)S(1)} all-to-all(f32[16,40,128]{2,1,0:T(8,128)S(1)} %bitcast.15), channel_id=1, replica_groups={{0,2,4,6,128,130,132,134,256,258,260,262,384,386,388,390},{1,3,5,7,129,..., dimensions={0} | all-to-all | bytes 655360 | tf_op jit(solution)/shard_map/all_to_all | solution.py:590
  91.0 0.0 copy-done
  91.0 1.1 %shard_map.81 = (f32[59,512]{1,0:T(8,128)}, f32[3,4,256]{2,1,0:T(4,128)}) custom-call(f32[640,128]{1,0:T(8,128)S(1)} %bitcast.14, f32[59,512]{1,0:T(8,128)S(1)} %copy-done, f32[3,4,256]{2,1,0:T(4,128)S(1)} %get-tuple-element.19.image_in_ref), custom_call_target="tpu_custom_call" | custom-call | tf_op jit(solution)/shard_map/pallas_call | solution.py:524
Async XLA Ops:
  2.9 35.9 %all-to-all-start = ((f32[16,1,4608]{2,1,0:T(1,128)}), f32[16,1,4608]{2,1,0:T(1,128)S(1)}, u32[]{:S(2)}, u32[]{:S(2)}) async-start(f32[16,1,4608]{2,1,0:T(1,128)} %bitcast.5), calls=%async_computation | async-start | bytes 589824 | tf_op jit(solution)/shard_map/all_to_all | solution.py:590
  78.7 12.3 %copy-start = (f32[59,512]{1,0:T(8,128)S(1)}, f32[59,512]{1,0:T(8,128)}, u32[]{:S(2)}) copy-start(f32[59,512]{1,0:T(8,128)} %attr_ref.1) | copy-start | bytes 362500

commit v11 on v10

--- a/solution.py
+++ b/solution.py
@@ -15,7 +15,6 @@
 PLANES = 16
 RANKS = 8
 SEGMENTS = 8
-RING = (0, 2, 4, 6, 7, 5, 3, 1)
 G_DEV = 512
 ATTR = 59
 VIEWS = 4
@@ -247,7 +246,7 @@
         table = [x.astype(F32) for x in split3(jnp.concatenate(table, axis=1))]
         table = jnp.concatenate(table + [jnp.zeros((8, G_DEV), F32)], axis=0).astype(BF16)
         for r in range(0, RANKS, 2):
-            ids = [asked_ref[pl.ds(16 * RING.index(r + i) + mine + half, 1), :] for i in range(2)]
+            ids = [asked_ref[pl.ds(16 * (r + i) + mine + half, 1), :] for i in range(2)]
             hot = one_hot(lid, jnp.concatenate(ids, axis=1).astype(I32))
             got = dot(table, hot, 1, 0)
             got = got[0:72] + got[72:144] + got[144:216]
@@ -592,7 +591,6 @@
 
 ALONG = [[8 * z + r for z in range(PLANES)] for r in range(RANKS)]
 PLANE = [[8 * z + r for r in range(RANKS)] for z in range(PLANES)]
-AROUND = [[8 * z + r for r in RING] for z in range(PLANES)]
 ACROSS = [[8 * z + 2 * y + c for z in range(PLANES) for c in range(2)] for y in range(NEAR)]
 WITHIN = [[8 * z + 2 * y + c for y in range(NEAR)] for z in range(PLANES) for c in range(2)]
 VIEWS_WITHIN = [[OWNERS * v + d for v in range(VIEWS) for d in group] for group in WITHIN]
@@ -605,7 +603,7 @@
         first_tile, owner, list_local[0], attributes, camera, term_depth[0], image_cot[0]
     )
     rows = exchange(rows.reshape(PLANES, 1, 4608), "dev", ALONG).reshape(PLANES * 36, 128)
-    asked = lax.all_gather(asked, "dev", axis_index_groups=AROUND, tiled=True)
+    asked = lax.all_gather(asked, "dev", axis_index_groups=PLANE, tiled=True)
     sent = serve(first_tile, asked, rows)
     got = exchange(sent.reshape(RANKS, 1, 2304), "dev", PLANE).reshape(18 * RANKS, 128)
     image, grads = composite(got, place, inv, kept, names)

time: 92.8 us -> 86.7 us (0.934)
  blocking collectives: 68.5 us -> 62.3 us
    all_gather x1, blocking collectives: 20.1 us -> 14 us  [per_device(): asked = lax.all_gather(asked, 'dev', axis_index_groups=PLANE, tiled=True)]
where the time goes in v11:
time: 86.7 us; the launch traced here: 86 us
  blocking collectives  62.3 us (72%)
  starting transfers between devices  15.8 us (18%)
  Pallas kernels  7.17 us (8%)
    all_to_all x3, blocking collectives, exchange(): lax.all_to_all(x, axis, split_axis=0, concat_axis=0, tiled=True, axis_ind...  48.3 us
    all_to_all x1, starting transfers between devices, exchange(): lax.all_to_all(x, axis, split_axis=0, concat_axis=0, tiled=True, axis_ind...  15.8 us
    all_gather x1, blocking collectives, per_device(): asked = lax.all_gather(asked, 'dev', axis_index_groups=PLANE, tiled=True)  14 us
    pallas_call x5, Pallas kernels, call(): pl.pallas_call(kernel, out_shape=[jax.ShapeDtypeStruct(s, d) for s, d in...  7.17 us
  transfers between devices with their start and end apart: 1, of which 0 were waited for; matrix products, arithmetic and copies ran while one was open for 0% of the time, Pallas kernels for 0%

profile of v11, /device:TPU:1, one launch (start us, length us, event | category | flops | bytes accessed | tf_op | source)
XLA Modules:
  0.0 86.0 jit_solution(2920737733131424345)
XLA Ops:
  0.6 2.2 %shard_map.77 = (f32[16,128]{1,0:T(8,128)S(1)}, s32[32,128]{1,0:T(8,128)S(1)}, s32[8,1024]{1,0:T(8,128)S(1)}, f32[576,128]{1,0:T(8,128)}, f32[16,256]{1,0:T(8,128)S(1)}, /*index=5*/f32[32,128]{1,0:T(8,128)S(1)}) custom-call(s32[1]{0:T(128)} %bitcast.tile_ref, s32[1,1024]{1,0:T(1,128)} %bitcast.22, s32[4,256]{1,0:T(4,128)} %bitcast.23, f32[59,512]{1,0:T(8,128)} %attr_ref.1, ...), custom_call_target="tpu_custom_call" | custom-call | tf_op jit(solution)/shard_map/pallas_call | solution.py:523
  2.9 15.8 %all-to-all-start = ((f32[16,1,4608]{2,1,0:T(1,128)}), f32[16,1,4608]{2,1,0:T(1,128)S(1)}, u32[]{:S(2)}, u32[]{:S(2)}) async-start(f32[16,1,4608]{2,1,0:T(1,128)} %bitcast.5), calls=%async_computation | async-start | bytes 589824 | tf_op jit(solution)/shard_map/all_to_all | solution.py:589
  18.6 14.0 %all_gather.3.asked_ref = f32[128,128]{1,0:T(8,128)S(1)} all-gather(f32[16,128]{1,0:T(8,128)S(1)} %get-tuple-element.12), channel_id=1, replica_groups={{0,1,2,3,4,5,6,7},{8,9,10,11,12,13,14,15},{16,17,18,19,20,21,22,23},{24..., dimensions={0}, use_global_device_ids=true | all-gather | bytes 73728 | tf_op jit(solution)/shard_map/all_gather | solution.py:606
  32.7 0.0 all-to-all-done
  32.7 0.7 shard_map.78
  33.3 15.4 %all_to_all.20 = f32[8,1,2304]{2,1,0:T(1,128)S(1)} all-to-all(f32[8,1,2304]{2,1,0:T(1,128)S(1)} %bitcast.19), channel_id=1, replica_groups={{0,1,2,3,4,5,6,7},{8,9,10,11,12,13,14,15},{16,17,18,19,20,21,22,23},{24..., dimensions={0} | all-to-all | bytes 147456 | tf_op jit(solution)/shard_map/all_to_all | solution.py:589
  48.7 2.3 %shard_map.79 = (f32[3,4,256]{2,1,0:T(4,128)S(1)}, f32[160,128]{1,0:T(8,128)S(1)}) custom-call(f32[144,128]{1,0:T(8,128)S(1)} %bitcast.18, s32[8,1024]{1,0:T(8,128)S(1)} %get-tuple-element.14.place_ref, s32[32,128]{1,0:T(8,128)S(1)} %get-tuple-element.15.inv_ref, f32[16,256]{1,0:T(8,128)S(1)} %get-tuple-element.16.kept_ref, ...), custom_call_target="tpu_custom_call" | custom-call | tf_op jit(solution)/shard_map/pallas_call | solution.py:523
  51.0 20.6 %all_to_all.21 = f32[32,1,640]{2,1,0:T(1,128)S(1)} all-to-all(f32[32,1,640]{2,1,0:T(1,128)S(1)} %bitcast.20), channel_id=1, replica_groups={{0,1,8,9,16,17,24,25,32,33,40,41,48,49,56,57,64,65,72,73,80,81,88,89,96..., dimensions={0} | all-to-all | bytes 163840 | tf_op jit(solution)/shard_map/all_to_all | solution.py:589
  71.6 0.8 shard_map.80
  72.5 0.0 copy-start
  72.5 12.3 %all_to_all.22 = f32[16,40,128]{2,1,0:T(8,128)S(1)} all-to-all(f32[16,40,128]{2,1,0:T(8,128)S(1)} %bitcast.15), channel_id=1, replica_groups={{0,2,4,6,128,130,132,134,256,258,260,262,384,386,388,390},{1,3,5,7,129,..., dimensions={0} | all-to-all | bytes 655360 | tf_op jit(solution)/shard_map/all_to_all | solution.py:589
  84.8 0.0 copy-done
  84.8 1.1 %shard_map.81 = (f32[59,512]{1,0:T(8,128)}, f32[3,4,256]{2,1,0:T(4,128)}) custom-call(f32[640,128]{1,0:T(8,128)S(1)} %bitcast.14, f32[59,512]{1,0:T(8,128)S(1)} %copy-done, f32[3,4,256]{2,1,0:T(4,128)S(1)} %get-tuple-element.19.image_in_ref), custom_call_target="tpu_custom_call" | custom-call | tf_op jit(solution)/shard_map/pallas_call | solution.py:523
Async XLA Ops:
  2.9 29.8 %all-to-all-start = ((f32[16,1,4608]{2,1,0:T(1,128)}), f32[16,1,4608]{2,1,0:T(1,128)S(1)}, u32[]{:S(2)}, u32[]{:S(2)}) async-start(f32[16,1,4608]{2,1,0:T(1,128)} %bitcast.5), calls=%async_computation | async-start | bytes 589824 | tf_op jit(solution)/shard_map/all_to_all | solution.py:589
  72.5 12.3 %copy-start = (f32[59,512]{1,0:T(8,128)S(1)}, f32[59,512]{1,0:T(8,128)}, u32[]{:S(2)}) copy-start(f32[59,512]{1,0:T(8,128)} %attr_ref.1) | copy-start | bytes 362500

commit v12 on v11

--- a/solution.py
+++ b/solution.py
@@ -155,8 +155,8 @@
 
 def route_kernel(
     tile_ref, owner_hbm, local_hbm, attr_hbm, cam_hbm, depth_hbm, cot_hbm,
-    asked_ref, inv_ref, place_ref, rows_hbm, kept_ref, names_ref,
-    owner_ref, local_ref, attr_ref, cam_ref, depth_ref, cot_ref, wide_ref, tmp_ref, rows_ref, sem,
+    asked_ref, inv_ref, place_ref, rows_hbm, kept_ref, names_ref, wide_ref,
+    owner_ref, local_ref, attr_ref, cam_ref, depth_ref, cot_ref, tmp_ref, rows_ref, sem,
 ):
     pairs = [
         (owner_hbm, owner_ref), (local_hbm, local_ref), (attr_hbm, attr_ref), (cam_hbm, cam_ref),
@@ -476,7 +476,7 @@
             out_ref[40 * (NEAR * v + r) : 40 * (NEAR * v + r + 1), :] = part
 
 
-def pull_kernel(parts_ref, attr_ref, image_in_ref, out_ref, image_ref, wide_ref, res_ref, all_ref):
+def pull_kernel(parts_ref, wide_ref, image_in_ref, out_ref, image_ref, res_ref, all_ref):
     image_ref[...] = image_in_ref[...]
     for v in range(VIEWS):
         start = 40 * NEAR * v
@@ -485,7 +485,6 @@
             total = total + parts_ref[start + 40 * r : start + 40 * r + 36, :]
         all_ref[40 * v : 40 * v + 36, :] = total
         all_ref[40 * v + 36 : 40 * v + 40, :] = parts_ref[start + 36 : start + 40, :]
-    spread_attributes(attr_ref, wide_ref)
     pos, logscale, quat, logit, sh = split_attributes(wide_ref)
     total = None
     opacity_grad = None
@@ -543,16 +542,16 @@
         route_kernel,
         [
             ((2 * RANKS, 128), F32), ((PEERS, 128), I32), ((8, TILES * SLOTS), I32), ((36 * PLANES, 128), F32),
-            ((16, SLOTS), F32), ((PEERS, 128), F32),
+            ((16, SLOTS), F32), ((PEERS, 128), F32), ((ATTR * 8, 128), F32),
         ],
         (first_tile, *[in_hbm(x) for x in (owner, local, attributes, camera, depth, cot)]),
         [
             vmem(1, TILES * SLOTS, dtype=I32), vmem(TILES, SLOTS, dtype=I32), vmem(ATTR, G_DEV), vmem(1, 6),
-            vmem(TILES, SLOTS, dtype=I32), vmem(3, TILES, SLOTS), vmem(ATTR * 8, 128), vmem(36, 128),
+            vmem(TILES, SLOTS, dtype=I32), vmem(3, TILES, SLOTS), vmem(36, 128),
             vmem(36 * PLANES, 128), pltpu.SemaphoreType.DMA((7,)),
         ],
         [SMEM] + [HBM] * 6,
-        [VMEM] * 3 + [HBM] + [VMEM] * 2,
+        [VMEM] * 3 + [HBM] + [VMEM] * 3,
     )
 
 
@@ -576,12 +575,12 @@
     return call(collect_kernel, [((VIEWS * NEAR * 40, 128), F32)], (back, kept))[0]
 
 
-def pull_back(parts, attributes, image):
+def pull_back(parts, wide, image):
     return call(
         pull_kernel,
         [((ATTR, G_DEV), F32), (image.shape, F32)],
-        (parts, attributes, image),
-        [vmem(ATTR * 8, 128), vmem(ATTR * 4, 128), vmem(40 * VIEWS, 128)],
+        (parts, wide, image),
+        [vmem(ATTR * 4, 128), vmem(40 * VIEWS, 128)],
     )
 
 
@@ -599,7 +598,7 @@
 def per_device(attributes, camera, list_owner, list_local, term_depth, image_cot):
     owner = list_owner.reshape(1, -1)
     first_tile = (lax.axis_index("dev") * TILES).astype(I32).reshape(1)
-    asked, inv, place, rows, kept, names = route(
+    asked, inv, place, rows, kept, names, wide = route(
         first_tile, owner, list_local[0], attributes, camera, term_depth[0], image_cot[0]
     )
     rows = exchange(rows.reshape(PLANES, 1, 4608), "dev", ALONG).reshape(PLANES * 36, 128)
@@ -610,7 +609,7 @@
     back = exchange(grads.reshape(PEERS, 1, 640), "dev", ACROSS).reshape(5 * PEERS, 128)
     mine = collect(back, kept)
     parts = exchange(mine.reshape(VIEWS * NEAR, 40, 128), ("view", "dev"), VIEWS_WITHIN)
-    grad, image = pull_back(parts.reshape(VIEWS * NEAR * 40, 128), attributes, image)
+    grad, image = pull_back(parts.reshape(VIEWS * NEAR * 40, 128), wide, image)
     return image[None], grad
 
 

time: 86.7 us -> 86.5 us (level)
  no operation moved by 1% of the time
where the time goes in v12:
time: 86.5 us; the launch traced here: 85.8 us
  blocking collectives  62.2 us (72%)
  starting transfers between devices  15.8 us (18%)
  Pallas kernels  7.18 us (8%)
    all_to_all x3, blocking collectives, exchange(): lax.all_to_all(x, axis, split_axis=0, concat_axis=0, tiled=True, axis_ind...  48.2 us
    all_to_all x1, starting transfers between devices, exchange(): lax.all_to_all(x, axis, split_axis=0, concat_axis=0, tiled=True, axis_ind...  15.8 us
    all_gather x1, blocking collectives, per_device(): asked = lax.all_gather(asked, 'dev', axis_index_groups=PLANE, tiled=True)  14 us
    pallas_call x5, Pallas kernels, call(): pl.pallas_call(kernel, out_shape=[jax.ShapeDtypeStruct(s, d) for s, d in...  7.18 us
  transfers between devices with their start and end apart: 1, of which 0 were waited for; matrix products, arithmetic and copies ran while one was open for 0% of the time, Pallas kernels for 0%

profile of v12, /device:TPU:1, one launch (start us, length us, event | category | flops | bytes accessed | tf_op | source)
XLA Modules:
  0.0 85.8 jit_solution(17176841940581203517)
XLA Ops:
  0.6 2.2 %shard_map.77 = (f32[16,128]{1,0:T(8,128)S(1)}, s32[32,128]{1,0:T(8,128)S(1)}, s32[8,1024]{1,0:T(8,128)S(1)}, f32[576,128]{1,0:T(8,128)}, f32[16,256]{1,0:T(8,12...) custom-call(s32[1]{0:T(128)} %bitcast.tile_ref, s32[1,1024]{1,0:T(1,128)} %bitcast.22, s32[4,256]{1,0:T(4,128)} %bitcast.23, ...), custom_call_target="tpu_custom_call" | custom-call | tf_op jit(solution)/shard_map/pallas_call | solution.py:522
  2.9 15.8 %all-to-all-start = ((f32[16,1,4608]{2,1,0:T(1,128)}), f32[16,1,4608]{2,1,0:T(1,128)S(1)}, u32[]{:S(2)}, u32[]{:S(2)}) async-start(f32[16,1,4608]{2,1,0:T(1,128)} %bitcast.5), calls=%async_computation | async-start | bytes 589824 | tf_op jit(solution)/shard_map/all_to_all | solution.py:588
  18.6 14.0 %all_gather.3.asked_ref = f32[128,128]{1,0:T(8,128)S(1)} all-gather(f32[16,128]{1,0:T(8,128)S(1)} %get-tuple-element.13), channel_id=1, replica_groups={{0,1,2,3,4,5,6,7},{8,9,10,11,12,13,14,15},{16,17,18,19,20,21,22,23},{24..., dimensions={0}, use_global_device_ids=true | all-gather | bytes 73728 | tf_op jit(solution)/shard_map/all_gather | solution.py:605
  32.7 0.0 all-to-all-done
  32.7 0.7 shard_map.78
  33.3 15.4 %all_to_all.20 = f32[8,1,2304]{2,1,0:T(1,128)S(1)} all-to-all(f32[8,1,2304]{2,1,0:T(1,128)S(1)} %bitcast.19), channel_id=1, replica_groups={{0,1,2,3,4,5,6,7},{8,9,10,11,12,13,14,15},{16,17,18,19,20,21,22,23},{24..., dimensions={0} | all-to-all | bytes 147456 | tf_op jit(solution)/shard_map/all_to_all | solution.py:588
  48.7 2.3 %shard_map.79 = (f32[3,4,256]{2,1,0:T(4,128)S(1)}, f32[160,128]{1,0:T(8,128)S(1)}) custom-call(f32[144,128]{1,0:T(8,128)S(1)} %bitcast.18, s32[8,1024]{1,0:T(8,128)S(1)} %get-tuple-element.15.place_ref, s32[32,128]{1,0:T(8,128)S(1)} %get-tuple-element.16.inv_ref, f32[16,256]{1,0:T(8,128)S(1)} %get-tuple-element.17.kept_ref, ...), custom_call_target="tpu_custom_call" | custom-call | tf_op jit(solution)/shard_map/pallas_call | solution.py:522
  51.0 20.6 %all_to_all.21 = f32[32,1,640]{2,1,0:T(1,128)S(1)} all-to-all(f32[32,1,640]{2,1,0:T(1,128)S(1)} %bitcast.20), channel_id=1, replica_groups={{0,1,8,9,16,17,24,25,32,33,40,41,48,49,56,57,64,65,72,73,80,81,88,89,96..., dimensions={0} | all-to-all | bytes 163840 | tf_op jit(solution)/shard_map/all_to_all | solution.py:588
  71.6 0.8 shard_map.80
  72.5 12.2 %all_to_all.22 = f32[16,40,128]{2,1,0:T(8,128)S(1)} all-to-all(f32[16,40,128]{2,1,0:T(8,128)S(1)} %bitcast.15), channel_id=1, replica_groups={{0,2,4,6,128,130,132,134,256,258,260,262,384,386,388,390},{1,3,5,7,129,..., dimensions={0} | all-to-all | bytes 655360 | tf_op jit(solution)/shard_map/all_to_all | solution.py:588
  84.7 1.1 %shard_map.81 = (f32[59,512]{1,0:T(8,128)}, f32[3,4,256]{2,1,0:T(4,128)}) custom-call(f32[640,128]{1,0:T(8,128)S(1)} %bitcast.14, f32[472,128]{1,0:T(8,128)S(1)} %get-tuple-element.20.wide_ref, f32[3,4,256]{2,1,0:T(4,128)S(1)} %get-tuple-element.21.image_in_ref), custom_call_target="tpu_custom_call" | custom-call | tf_op jit(solution)/shard_map/pallas_call | solution.py:522
Async XLA Ops:
  2.9 29.8 %all-to-all-start = ((f32[16,1,4608]{2,1,0:T(1,128)}), f32[16,1,4608]{2,1,0:T(1,128)S(1)}, u32[]{:S(2)}, u32[]{:S(2)}) async-start(f32[16,1,4608]{2,1,0:T(1,128)} %bitcast.5), calls=%async_computation | async-start | bytes 589824 | tf_op jit(solution)/shard_map/all_to_all | solution.py:588
